TPU v7x, 32 devices: a whole 2x2x4 slice. The times are simulated.
32 devices in a mesh: groups: 2 (over x), node: 16 (over z, y, core).
Axes of the slice: x: 2, y: 2, z: 4, core: 2. Of those that a mesh axis runs over, the one named last changes fastest.
Arguments:
- child_query: bfloat16 [3072, 64, 576], P(('groups', 'node')), parts along dimension 0, may hold values from -24 to 24
- parent_cache: bfloat16 [32, 384, 576], P(('groups', 'node')), parts along dimension 0, may hold values from -4 to 4
- child_latent: bfloat16 [3072, 576], P(('groups', 'node')), parts along dimension 0, may hold values from -4 to 4
- parent_place: int32 [32], P('groups'), parts along dimension 0, may hold values from 0 to 15, each once
- child_parent: int32 [3072, 1], P(('groups', 'node')), parts along dimension 0, may hold values from 0 to 15; in each aligned block of 96 rows (0 to 95, 96 to 191, ...) at most 12 rows name the same one
- live_rows: int32 [32], P(('groups', 'node')), parts along dimension 0, may hold values from 72 to 96, as said below
Outputs:
- attended: bfloat16 [3072, 64, 512], P(('groups', 'node')), parts along dimension 0
There are 2 independent parts, one for each index of `groups`. A program takes and returns all parts, laid end to end along the dimension named above; each array names one. Nothing has to cross between parts.
Inputs may be any that keep to these rules, and one draw needn't show every extreme that they name: `child_parent`: within the rows of one device at most 12 rows name the same parent, and some device has exactly 12 rows naming one parent. `live_rows`: some device has all 96 slots live.
All inputs are finite; a program needn't handle non-finite values.
Results may differ from a plain program's by a relative error of at most 0.0047.
Values may be sent and summed in bfloat16 or wider, within the bound.
No kernel may reach another device: no remote copies, remote signals or barrier semaphores. Data moves between devices by JAX's collectives and lax.ppermute only.
A program may use at most 192 MiB of HBM per device.

v0:
```python
import functools
import math

import jax
import jax.numpy as jnp
from jax import lax
from jax.experimental import pallas as pl
from jax.experimental.pallas import tpu as pltpu
from jax.sharding import PartitionSpec as P

LAT = 512
SCALE = 0.07216878364870322
BLOCK = 6
COST = 4
ANY = pl.BlockSpec(memory_space=pl.ANY)
VMEM = pl.BlockSpec(memory_space=pltpu.VMEM)
SMEM = pl.BlockSpec(memory_space=pltpu.SMEM)


def position_of(chip, chips):
    if chips == 8:
        return jnp.where(chip % 2 == 0, chip // 2, 7 - chip // 2)
    return chip


def slot_of(ahead, same, chips):
    far = jnp.minimum(ahead, chips - ahead)
    slot = 4 * far - 2 + jnp.where(2 * ahead > chips, jnp.where(same, 0, 2), jnp.where(same, 3, 1))
    slot = jnp.where(2 * ahead == chips, 4 * far - 2 + jnp.where(same, 0, 1), slot)
    return jnp.where(ahead == 0, jnp.where(same, 0, 1), slot)


def prepare_kernel(
    place_in, parent_in, live_in, query_in, mine_in, _, order, starts, query, mine, __, place, parent, live, slots, names, sem
):
    rows = parent.shape[1]
    parents = place.shape[0]
    dead = starts.shape[0] - 1
    chips = parents // 2
    big = [
        pltpu.make_async_copy(query_in, query, sem.at[0]),
        pltpu.make_async_copy(mine_in, mine, sem.at[1]),
    ]
    small = [
        pltpu.make_async_copy(place_in, place, sem.at[2]),
        pltpu.make_async_copy(parent_in, parent, sem.at[3]),
        pltpu.make_async_copy(live_in, live, sem.at[4]),
    ]
    for copy in small + big:
        copy.start()
    for copy in small:
        copy.wait()
    me = lax.axis_index("node")
    core = me % 2
    here = position_of(me // 2, chips)
    alive = live[0]

    def name(p, _):
        at = place[p]
        there = position_of(at // 2, chips)
        ahead = jnp.where(core == 0, there - here, here - there)
        ahead = jnp.where(ahead < 0, ahead + chips, ahead)
        names[p] = slot_of(ahead, at % 2 == core, chips)
        starts[p] = 0
        return 0

    lax.fori_loop(0, parents, name, 0, unroll=4)
    starts[dead] = 0

    def tally(i, _):
        s = jnp.where(i < alive, names[parent[0, i]], dead)
        slots[i] = s
        starts[s] = starts[s] + 1
        return 0

    lax.fori_loop(0, rows, tally, 0, unroll=8)

    def ends(s, total):
        total = total + starts[s]
        starts[s] = total
        return total

    lax.fori_loop(0, dead + 1, ends, jnp.int32(0))

    def put(i, _):
        i = rows - 1 - i
        s = slots[i]
        j = starts[s] - 1
        starts[s] = j
        order[j] = i
        return 0

    lax.fori_loop(0, rows, put, 0, unroll=8)
    for i in range(rows, order.shape[0]):
        order[i] = 0
    for copy in big:
        copy.wait()


def prepare(place, parent, live, query, mine, other):
    rows, parents = parent.shape[1], place.shape[0]
    return pl.pallas_call(
        prepare_kernel,
        out_shape=(
            jax.ShapeDtypeStruct((rows + 2 * BLOCK,), jnp.int32),
            jax.ShapeDtypeStruct((parents + 1,), jnp.int32),
            pltpu.VMEM(query.shape, query.dtype),
            pltpu.VMEM(mine.shape, mine.dtype),
            pltpu.VMEM(other.shape, other.dtype),
        ),
        in_specs=[ANY] * 5 + [VMEM],
        out_specs=(SMEM, SMEM, VMEM, VMEM, VMEM),
        scratch_shapes=[
            pltpu.SMEM(place.shape, jnp.int32),
            pltpu.SMEM(parent.shape, jnp.int32),
            pltpu.SMEM(live.shape, jnp.int32),
            pltpu.SMEM((rows,), jnp.int32),
            pltpu.SMEM(place.shape, jnp.int32),
            pltpu.SemaphoreType.DMA((5,)),
        ],
        input_output_aliases={5: 4},
        compiler_params=pltpu.CompilerParams(vmem_limit_bytes=46 * 1024 * 1024),
        cost_estimate=pl.CostEstimate(flops=0, bytes_accessed=2 * query.size * 2, transcendentals=0),
    )(place, parent, live, query, mine, other)


def attend_kernel(first, before, last, arrays, order, starts, query, own, *refs):
    slots = refs[:arrays]
    out, ov, kv, even, odd, zeros, blocks, out_sem = refs[-8:]
    done = refs[arrays] if before else None
    rows, heads, depth = query.shape
    prefix = slots[0].shape[-1]
    width = kv.shape[2]
    base = starts[first]
    end = starts[first + arrays]

    if before:
        from_row, to_row = starts[first - before], base
    else:
        zeros[...] = jnp.zeros_like(zeros)
        from_row, to_row = starts[starts.shape[0] - 1], rows

    @pl.loop(from_row, to_row)
    def _(j):
        pltpu.make_async_copy(done.at[j] if before else zeros, out.at[order[j]], out_sem).start()

    number = jnp.int32(0)
    for s in range(arrays):
        kv[s, :, 0:prefix] = slots[s][...]
        kv[s, :, prefix:width] = own[...]
        lo, hi = starts[first + s], starts[first + s + 1]
        more = (hi - lo + BLOCK - 1) // BLOCK

        def note(b, _):
            blocks[0, number + b] = s
            blocks[1, number + b] = lo + b * BLOCK
            blocks[2, number + b] = jnp.minimum(lo + (b + 1) * BLOCK, hi)
            return 0

        lax.fori_loop(0, more, note, 0)
        number = number + more
    for b in range(2):
        blocks[0, number + b] = 0
        blocks[1, number + b] = rows
        blocks[2, number + b] = rows

    column = lax.broadcasted_iota(jnp.int32, (heads, width - prefix), 1)

    def score(b, to):
        begin = blocks[1, b]
        q = jnp.concatenate([query[order[begin + r]] for r in range(BLOCK)])
        to[...] = jnp.dot(q, kv[blocks[0, b]], preferred_element_type=jnp.float32)

    def finish(b, scores):
        begin = blocks[1, b]
        mine = [
            jnp.where(column == order[begin + r], scores[r * heads:(r + 1) * heads, prefix:width], -jnp.inf)
            for r in range(BLOCK)
        ]
        s = jnp.concatenate([scores[:, 0:prefix], jnp.concatenate(mine)], axis=1)
        top = jnp.max(s, axis=1, keepdims=True)
        expo = jnp.exp2((s - top) * (SCALE * math.log2(math.e)))
        total = jnp.sum(expo, axis=1, keepdims=True)
        weights = (expo * (1.0 / total)).astype(jnp.bfloat16)
        mixed = lax.dot_general(
            weights, kv[blocks[0, b], 0:LAT, :], (((1,), (1,)), ((), ())), preferred_element_type=jnp.float32
        )
        ov[pl.ds(begin, BLOCK)] = mixed.astype(jnp.bfloat16).reshape(BLOCK, heads, LAT)

    def send(b):
        @pl.loop(blocks[1, b], blocks[2, b])
        def _(j):
            pltpu.make_async_copy(ov.at[j], out.at[order[j]], out_sem).start()

    @pl.when(number > 0)
    def _():
        @pl.loop(0, (number + 1) // 2)
        def _(pair):
            b = pair * 2
            score(b, even)
            score(b + 1, odd)
            finish(b, even)
            finish(b + 1, odd)
            if last:
                send(b)
                send(b + 1)

    @pl.loop(from_row, to_row)
    def _(j):
        pltpu.make_async_copy(zeros, out.at[0], out_sem).wait()

    if last:

        @pl.loop(base, end)
        def _(j):
            pltpu.make_async_copy(zeros, out.at[0], out_sem).wait()


def attend(order, starts, first, query, own, slots, before=0, done=None, out=None, last=False):
    rows, heads, depth = query.shape
    count = len(slots)
    prefix = slots[0].shape[-1]
    width = prefix + own.shape[1]
    operands = [order, starts, query, own, *slots] + ([done, out] if before else [])
    work = rows * heads * count // (starts.shape[0] - 1)
    result = jax.ShapeDtypeStruct((rows, heads, LAT), jnp.bfloat16)
    made = pltpu.VMEM((rows + BLOCK, heads, LAT), jnp.bfloat16)
    return pl.pallas_call(
        functools.partial(attend_kernel, first, before, last, count),
        out_shape=result if last else (result, made),
        in_specs=[SMEM, SMEM, VMEM, VMEM] + [VMEM] * count + [VMEM, ANY] * (before > 0),
        out_specs=ANY if last else (ANY, VMEM),
        scratch_shapes=[made] * last + [
            pltpu.VMEM((count, depth, width), jnp.bfloat16),
            pltpu.VMEM((BLOCK * heads, width), jnp.float32),
            pltpu.VMEM((BLOCK * heads, width), jnp.float32),
            pltpu.VMEM((heads, LAT), jnp.bfloat16),
            pltpu.SMEM((3, rows // BLOCK + count + 4), jnp.int32),
            pltpu.SemaphoreType.DMA,
        ],
        input_output_aliases={len(operands) - 1: 0} if before else {},
        compiler_params=pltpu.CompilerParams(vmem_limit_bytes=16 * 1024 * 1024),
        cost_estimate=pl.CostEstimate(
            flops=COST * 2 * work * width * (depth + LAT),
            bytes_accessed=COST * (count * depth * width * 2 + work * LAT * 2),
            transcendentals=COST * work * width,
        ),
    )(*operands)


def ring_of(nodes):
    chips = nodes // 2
    if chips == 8:
        return [0, 2, 4, 6, 7, 5, 3, 1]
    return list(range(chips))


def shards(nodes, child_query, parent_cache, child_latent, parent_place, child_parent, live_rows):
    rows = child_query.shape[0]
    ring = ring_of(nodes)
    chips = len(ring)
    along = [(2 * ring[i], 2 * ring[(i + 1) % chips]) for i in range(chips)]
    along += [(2 * ring[(i + 1) % chips] + 1, 2 * ring[i] + 1) for i in range(chips)]
    across = [(i, i ^ 1) for i in range(nodes)]

    mine = jnp.swapaxes(parent_cache[0], 0, 1)
    other = lax.ppermute(mine, "node", across)
    order, starts, query, kept, other = prepare(
        parent_place, jnp.swapaxes(child_parent, 0, 1), live_rows, child_query, mine, other
    )
    padded = -(-rows // 128) * 128
    pick = jnp.arange(rows)[:, None] == jnp.arange(padded)[None, :]
    own = lax.dot_general(
        child_latent, pick.astype(jnp.bfloat16), (((0,), (0,)), ((), ())), preferred_element_type=jnp.float32
    ).astype(jnp.bfloat16)

    phases = [[kept, other]]
    streams = [mine, other]
    for k in range(1, chips // 2 + 1):
        streams = [lax.ppermute(a, "node", along) for a in streams[: 2 if 2 * k < chips else 1]]
        phases += [[a, lax.ppermute(a, "node", across)] for a in streams]
    first, before, result = 0, 0, (None, None)
    for slots in phases:
        last = slots is phases[-1]
        result = attend(order, starts, first, query, own, slots, before, result[1], result[0], last)
        first, before = first + len(slots), len(slots)
    return result


def solution(mesh):
    return jax.shard_map(
        functools.partial(shards, mesh.shape["node"]),
        mesh=mesh,
        in_specs=(
            P(("groups", "node"), None, None),
            P(("groups", "node"), None, None),
            P(("groups", "node"), None),
            P("groups"),
            P(("groups", "node"), None),
            P(("groups", "node")),
        ),
        out_specs=P(("groups", "node"), None, None),
        check_vma=False,
    )
```

profile of v0, /device:TPU:0, one launch (start us, length us, event | category | flops | bytes accessed | tf_op | source)
XLA Modules:
  0.0 54.3 jit_solution(8099954078333911130)
XLA Ops:
  0.0 0.0 copy-start
  0.0 0.5 collective-permute-start
  0.5 2.6 %collective-permute-start.1 = (bf16[576,384]{1,0:T(8,128)(2,1)}, bf16[576,384]{1,0:T(8,128)(2,1)S(1)}, u32[]{:S(2)}, u32[]{:S(2)}) collective-permute-start(bf16[576,384]{1,0:T(8,128)(2,1)} %bitcast.8), channel_id=1, source_target_pairs={{0,4},{4,8},{8,12},{12,14},{14,10},{10,6},{6,2},{2,0},{5,1},{9,5},... | collective-permute-start | bytes 1327112 | tf_op jit(solution)/shard_map/ppermute | solution.py:280
  3.7 0.0 collective-permute-done._
  3.7 3.8 %shard_map.64 = (s32[108]{0:T(128)}, s32[17]{0:T(128)}, bf16[96,64,576]{2,1,0:T(8,128)(2,1)S(1)}, bf16[576,384]{1,0:T(8,128)(2,1)S(1)}, bf16[576,384]{1,0:T(8,128)(2,1)S(1)}) custom-call(s32[16]{0:T(128)} %place_in.1, s32[1,96]{1,0:T(1,128)} %bitcast.10, s32[1]{0:T(128)S(6)} %copy.23.live_in, ...), custom_call_target="tpu_custom_call", output_to_operand_aliasing={{4}: (5, {})} | custom-call | bytes 14155776 | tf_op jit(solution)/shard_map/pallas_call | solution.py:102
  7.6 1.6 %collective-permute-start.6 = (bf16[576,384]{1,0:T(8,128)(2,1)S(1)}, bf16[576,384]{1,0:T(8,128)(2,1)S(1)}, u32[]{:S(2)}, u32[]{:S(2)}) collective-permute-start(bf16[576,384]{1,0:T(8,128)(2,1)S(1)} %get-tuple-element.27.refs_1_), channel_id=1, source_target_pairs={{0,4},{4,8},{8,12},{12,14},{14,10},{10,6},{6,2},{2,0},{5,1},{9,5},... | collective-permute-start | bytes 1327112 | tf_op jit(solution)/shard_map/ppermute | solution.py:280
  9.2 0.3 collective-permute-done.1.refs_0_
  9.5 2.1 %collective-permute-start.2 = (bf16[576,384]{1,0:T(8,128)(2,1)S(1)}, bf16[576,384]{1,0:T(8,128)(2,1)S(1)}, u32[]{:S(2)}, u32[]{:S(2)}) collective-permute-start(bf16[576,384]{1,0:T(8,128)(2,1)S(1)} %collective-permute-done.1.refs_0_), channel_id=1, source_target_pairs={{0,4},{4,8},{8,12},{12,14},{14,10},{10,6},{6,2},{2,0},{5,1},{9,5},... | collective-permute-start | bytes 1327112 | tf_op jit(solution)/shard_map/ppermute | solution.py:280
  11.6 0.0 collective-permute-start.14
  11.6 0.0 copy-done
  11.6 0.2 fusion.own
  11.8 4.1 %collective-permute-done.6.refs_0_ = bf16[576,384]{1,0:T(8,128)(2,1)S(1)} collective-permute-done((bf16[576,384]{1,0:T(8,128)(2,1)S(1)}, bf16[576,384]{1,0:T(8,128)(2,1)S(1)}, u32[]{:S(2)}, u32[]{:S(2)}) %collective-permute-start.6) | collective-permute-done | bytes 442400 | tf_op jit(solution)/shard_map/ppermute | solution.py:280
  15.9 0.0 collective-permute-start.13
  15.9 1.6 %collective-permute-start.7 = (bf16[576,384]{1,0:T(8,128)(2,1)S(1)}, bf16[576,384]{1,0:T(8,128)(2,1)S(1)}, u32[]{:S(2)}, u32[]{:S(2)}) collective-permute-start(bf16[576,384]{1,0:T(8,128)(2,1)S(1)} %collective-permute-done.6.refs_0_), channel_id=1, source_target_pairs={{0,4},{4,8},{8,12},{12,14},{14,10},{10,6},{6,2},{2,0},{5,1},{9,5},... | collective-permute-start | bytes 1327112 | tf_op jit(solution)/shard_map/ppermute | solution.py:280
  17.5 3.2 %collective-permute-done.2.refs_0_ = bf16[576,384]{1,0:T(8,128)(2,1)S(1)} collective-permute-done((bf16[576,384]{1,0:T(8,128)(2,1)S(1)}, bf16[576,384]{1,0:T(8,128)(2,1)S(1)}, u32[]{:S(2)}, u32[]{:S(2)}) %collective-permute-start.2) | collective-permute-done | bytes 442400 | tf_op jit(solution)/shard_map/ppermute | solution.py:280
  20.7 1.6 %collective-permute-start.3 = (bf16[576,384]{1,0:T(8,128)(2,1)S(1)}, bf16[576,384]{1,0:T(8,128)(2,1)S(1)}, u32[]{:S(2)}, u32[]{:S(2)}) collective-permute-start(bf16[576,384]{1,0:T(8,128)(2,1)S(1)} %collective-permute-done.2.refs_0_), channel_id=1, source_target_pairs={{0,4},{4,8},{8,12},{12,14},{14,10},{10,6},{6,2},{2,0},{5,1},{9,5},... | collective-permute-start | bytes 1327112 | tf_op jit(solution)/shard_map/ppermute | solution.py:280
  22.3 0.0 copy-start.2
  22.3 0.7 %copy-done.2 = s32[108]{0:T(128)S(1)} copy-done((s32[108]{0:T(128)S(1)}, s32[108]{0:T(128)}, u32[]{:S(2)}) %copy-start.2) | copy-done | bytes 456
  22.9 0.0 copy-start.3
  22.9 0.6 %copy-done.3 = s32[17]{0:T(128)S(1)} copy-done((s32[17]{0:T(128)S(1)}, s32[17]{0:T(128)}, u32[]{:S(2)}) %copy-start.3) | copy-done | bytes 92
  23.5 2.1 %shard_map.65 = (bf16[96,64,512]{2,1,0:T(8,128)(2,1)}, bf16[102,64,512]{2,1,0:T(8,128)(2,1)S(1)}) custom-call(s32[108]{0:T(128)S(1)} %copy-done.2, s32[17]{0:T(128)S(1)} %copy-done.3, bf16[96,64,576]{2,1,0:T(8,128)(2,1)S(1)} %get-tuple-element.26.query, bf16[576,128]{1,0:T(8,128)(2,1)S(1)} %fusion.own, bf16[576,384]{1,0:T(8,128)(2,1)S(1)} %get-tuple-element.28.refs_0_, ...), custom_call_target="tpu_custom_call" | custom-call | flops 3422552064 | bytes 7864320 | tf_op jit(solution)/shard_map/pallas_call | solution.py:228
  25.6 0.2 collective-permute-start.12
  25.8 0.0 collective-permute-done.14.refs_1_
  25.8 3.3 %shard_map.66 = (bf16[96,64,512]{2,1,0:T(8,128)(2,1)}, bf16[102,64,512]{2,1,0:T(8,128)(2,1)S(1)}) custom-call(s32[108]{0:T(128)S(1)} %copy-done.2, s32[17]{0:T(128)S(1)} %copy-done.3, bf16[96,64,576]{2,1,0:T(8,128)(2,1)S(1)} %get-tuple-element.26.query, bf16[576,128]{1,0:T(8,128)(2,1)S(1)} %fusion.own, ...), custom_call_target="tpu_custom_call", output_to_operand_aliasing={{0}: (7, {})} | custom-call | flops 3422552064 | bytes 7864320 | tf_op jit(solution)/shard_map/pallas_call | solution.py:228
  29.1 0.0 collective-permute-done.7.refs_0_
  29.2 0.5 collective-permute-start.11
  29.6 1.4 %collective-permute-start.8 = (bf16[576,384]{1,0:T(8,128)(2,1)S(1)}, bf16[576,384]{1,0:T(8,128)(2,1)S(1)}, u32[]{:S(2)}, u32[]{:S(2)}) collective-permute-start(bf16[576,384]{1,0:T(8,128)(2,1)S(1)} %collective-permute-done.7.refs_0_), channel_id=1, source_target_pairs={{0,4},{4,8},{8,12},{12,14},{14,10},{10,6},{6,2},{2,0},{5,1},{9,5},... | collective-permute-start | bytes 1327112 | tf_op jit(solution)/shard_map/ppermute | solution.py:280
  31.1 0.0 collective-permute-done.3.refs_0_
  31.1 0.2 collective-permute-start.10
  31.2 0.0 collective-permute-done.13.refs_1_
  31.2 1.5 %collective-permute-start.4 = (bf16[576,384]{1,0:T(8,128)(2,1)S(1)}, bf16[576,384]{1,0:T(8,128)(2,1)S(1)}, u32[]{:S(2)}, u32[]{:S(2)}) collective-permute-start(bf16[576,384]{1,0:T(8,128)(2,1)S(1)} %collective-permute-done.3.refs_0_), channel_id=1, source_target_pairs={{0,4},{4,8},{8,12},{12,14},{14,10},{10,6},{6,2},{2,0},{5,1},{9,5},... | collective-permute-start | bytes 1327112 | tf_op jit(solution)/shard_map/ppermute | solution.py:280
  32.7 3.4 %shard_map.67 = (bf16[96,64,512]{2,1,0:T(8,128)(2,1)}, bf16[102,64,512]{2,1,0:T(8,128)(2,1)S(1)}) custom-call(s32[108]{0:T(128)S(1)} %copy-done.2, s32[17]{0:T(128)S(1)} %copy-done.3, bf16[96,64,576]{2,1,0:T(8,128)(2,1)S(1)} %get-tuple-element.26.query, bf16[576,128]{1,0:T(8,128)(2,1)S(1)} %fusion.own, ...), custom_call_target="tpu_custom_call", output_to_operand_aliasing={{0}: (7, {})} | custom-call | flops 3422552064 | bytes 7864320 | tf_op jit(solution)/shard_map/pallas_call | solution.py:228
  36.1 0.0 collective-permute-done.12.refs_1_
  36.1 3.3 %shard_map.68 = (bf16[96,64,512]{2,1,0:T(8,128)(2,1)}, bf16[102,64,512]{2,1,0:T(8,128)(2,1)S(1)}) custom-call(s32[108]{0:T(128)S(1)} %copy-done.2, s32[17]{0:T(128)S(1)} %copy-done.3, bf16[96,64,576]{2,1,0:T(8,128)(2,1)S(1)} %get-tuple-element.26.query, bf16[576,128]{1,0:T(8,128)(2,1)S(1)} %fusion.own, ...), custom_call_target="tpu_custom_call", output_to_operand_aliasing={{0}: (7, {})} | custom-call | flops 3422552064 | bytes 7864320 | tf_op jit(solution)/shard_map/pallas_call | solution.py:228
  39.4 0.0 collective-permute-done.8.refs_0_
  39.4 0.1 collective-permute-start.9
  39.5 3.2 %collective-permute-done.4.refs_0_ = bf16[576,384]{1,0:T(8,128)(2,1)S(1)} collective-permute-done((bf16[576,384]{1,0:T(8,128)(2,1)S(1)}, bf16[576,384]{1,0:T(8,128)(2,1)S(1)}, u32[]{:S(2)}, u32[]{:S(2)}) %collective-permute-start.4) | collective-permute-done | bytes 442400 | tf_op jit(solution)/shard_map/ppermute | solution.py:280
  42.7 0.0 collective-permute-start.5
  42.7 0.0 collective-permute-done.11.refs_1_
  42.7 3.3 %shard_map.69 = (bf16[96,64,512]{2,1,0:T(8,128)(2,1)}, bf16[102,64,512]{2,1,0:T(8,128)(2,1)S(1)}) custom-call(s32[108]{0:T(128)S(1)} %copy-done.2, s32[17]{0:T(128)S(1)} %copy-done.3, bf16[96,64,576]{2,1,0:T(8,128)(2,1)S(1)} %get-tuple-element.26.query, bf16[576,128]{1,0:T(8,128)(2,1)S(1)} %fusion.own, ...), custom_call_target="tpu_custom_call", output_to_operand_aliasing={{0}: (7, {})} | custom-call | flops 3422552064 | bytes 7864320 | tf_op jit(solution)/shard_map/pallas_call | solution.py:228
  46.0 0.0 collective-permute-done.10.refs_1_
  46.0 3.4 %shard_map.70 = (bf16[96,64,512]{2,1,0:T(8,128)(2,1)}, bf16[102,64,512]{2,1,0:T(8,128)(2,1)S(1)}) custom-call(s32[108]{0:T(128)S(1)} %copy-done.2, s32[17]{0:T(128)S(1)} %copy-done.3, bf16[96,64,576]{2,1,0:T(8,128)(2,1)S(1)} %get-tuple-element.26.query, bf16[576,128]{1,0:T(8,128)(2,1)S(1)} %fusion.own, ...), custom_call_target="tpu_custom_call", output_to_operand_aliasing={{0}: (7, {})} | custom-call | flops 3422552064 | bytes 7864320 | tf_op jit(solution)/shard_map/pallas_call | solution.py:228
  49.4 0.0 collective-permute-done.9.refs_1_
  49.4 2.1 %shard_map.71 = (bf16[96,64,512]{2,1,0:T(8,128)(2,1)}, bf16[102,64,512]{2,1,0:T(8,128)(2,1)S(1)}) custom-call(s32[108]{0:T(128)S(1)} %copy-done.2, s32[17]{0:T(128)S(1)} %copy-done.3, bf16[96,64,576]{2,1,0:T(8,128)(2,1)S(1)} %get-tuple-element.26.query, bf16[576,128]{1,0:T(8,128)(2,1)S(1)} %fusion.own, ...), custom_call_target="tpu_custom_call", output_to_operand_aliasing={{0}: (7, {})} | custom-call | flops 3422552064 | bytes 7864320 | tf_op jit(solution)/shard_map/pallas_call | solution.py:228
  51.6 0.0 collective-permute-done.5.refs_1_
  51.6 0.0 copy-start.1
  51.6 2.8 %shard_map.72 = bf16[96,64,512]{2,1,0:T(8,128)(2,1)} custom-call(s32[108]{0:T(128)S(1)} %copy-done.2, s32[17]{0:T(128)S(1)} %copy-done.3, bf16[96,64,576]{2,1,0:T(8,128)(2,1)S(1)} %get-tuple-element.26.query, bf16[576,128]{1,0:T(8,128)(2,1)S(1)} %fusion.own, bf16[576,384]{1,0:T(8,128)(2,1)S(1)} %collective-permute-done.4.refs_0_, ...), custom_call_target="tpu_custom_call", output_to_operand_aliasing={{}: (7, {})} | custom-call | flops 3422552064 | bytes 7864320 | tf_op jit(solution)/shard_map/pallas_call | solution.py:228
  54.3 0.0 copy-done.1
Async XLA Ops:
  0.0 11.6 %copy-start = (bf16[96,576]{1,0:T(8,128)(2,1)S(1)}, bf16[96,576]{1,0:T(8,128)(2,1)}, u32[]{:S(2)}) copy-start(bf16[96,576]{1,0:T(8,128)(2,1)} %param.8) | copy-start | bytes 331780
  0.0 3.7 %collective-permute-start = (bf16[576,384]{1,0:T(8,128)(2,1)}, bf16[576,384]{1,0:T(8,128)(2,1)S(1)}, u32[]{:S(2)}, u32[]{:S(2)}) collective-permute-start(bf16[576,384]{1,0:T(8,128)(2,1)} %bitcast.7), channel_id=1, source_target_pairs={{0,1},{1,0},{2,3},{3,2},{4,5},{5,4},{6,7},{7,6},{8,9},{9,8},{10,11... | collective-permute-start | bytes 1327112 | tf_op jit(solution)/shard_map/ppermute | solution.py:267
  0.5 9.1 %collective-permute-start.1 = (bf16[576,384]{1,0:T(8,128)(2,1)}, bf16[576,384]{1,0:T(8,128)(2,1)S(1)}, u32[]{:S(2)}, u32[]{:S(2)}) collective-permute-start(bf16[576,384]{1,0:T(8,128)(2,1)} %bitcast.8), channel_id=1, source_target_pairs={{0,4},{4,8},{8,12},{12,14},{14,10},{10,6},{6,2},{2,0},{5,1},{9,5},... | collective-permute-start | bytes 1327112 | tf_op jit(solution)/shard_map/ppermute | solution.py:280
  7.6 8.4 %collective-permute-start.6 = (bf16[576,384]{1,0:T(8,128)(2,1)S(1)}, bf16[576,384]{1,0:T(8,128)(2,1)S(1)}, u32[]{:S(2)}, u32[]{:S(2)}) collective-permute-start(bf16[576,384]{1,0:T(8,128)(2,1)S(1)} %get-tuple-element.27.refs_1_), channel_id=1, source_target_pairs={{0,4},{4,8},{8,12},{12,14},{14,10},{10,6},{6,2},{2,0},{5,1},{9,5},... | collective-permute-start | bytes 1327112 | tf_op jit(solution)/shard_map/ppermute | solution.py:280
  9.5 11.2 %collective-permute-start.2 = (bf16[576,384]{1,0:T(8,128)(2,1)S(1)}, bf16[576,384]{1,0:T(8,128)(2,1)S(1)}, u32[]{:S(2)}, u32[]{:S(2)}) collective-permute-start(bf16[576,384]{1,0:T(8,128)(2,1)S(1)} %collective-permute-done.1.refs_0_), channel_id=1, source_target_pairs={{0,4},{4,8},{8,12},{12,14},{14,10},{10,6},{6,2},{2,0},{5,1},{9,5},... | collective-permute-start | bytes 1327112 | tf_op jit(solution)/shard_map/ppermute | solution.py:280
  11.6 14.2 %collective-permute-start.14 = (bf16[576,384]{1,0:T(8,128)(2,1)S(1)}, bf16[576,384]{1,0:T(8,128)(2,1)S(1)}, u32[]{:S(2)}, u32[]{:S(2)}) collective-permute-start(bf16[576,384]{1,0:T(8,128)(2,1)S(1)} %collective-permute-done.1.refs_0_), channel_id=1, source_target_pairs={{0,1},{1,0},{2,3},{3,2},{4,5},{5,4},{6,7},{7,6},{8,9},{9,8},{10,11... | collective-permute-start | bytes 1327112 | tf_op jit(solution)/shard_map/ppermute | solution.py:281
  15.9 15.3 %collective-permute-start.13 = (bf16[576,384]{1,0:T(8,128)(2,1)S(1)}, bf16[576,384]{1,0:T(8,128)(2,1)S(1)}, u32[]{:S(2)}, u32[]{:S(2)}) collective-permute-start(bf16[576,384]{1,0:T(8,128)(2,1)S(1)} %collective-permute-done.6.refs_0_), channel_id=1, source_target_pairs={{0,1},{1,0},{2,3},{3,2},{4,5},{5,4},{6,7},{7,6},{8,9},{9,8},{10,11... | collective-permute-start | bytes 1327112 | tf_op jit(solution)/shard_map/ppermute | solution.py:281
  15.9 13.2 %collective-permute-start.7 = (bf16[576,384]{1,0:T(8,128)(2,1)S(1)}, bf16[576,384]{1,0:T(8,128)(2,1)S(1)}, u32[]{:S(2)}, u32[]{:S(2)}) collective-permute-start(bf16[576,384]{1,0:T(8,128)(2,1)S(1)} %collective-permute-done.6.refs_0_), channel_id=1, source_target_pairs={{0,4},{4,8},{8,12},{12,14},{14,10},{10,6},{6,2},{2,0},{5,1},{9,5},... | collective-permute-start | bytes 1327112 | tf_op jit(solution)/shard_map/ppermute | solution.py:280
  20.7 10.4 %collective-permute-start.3 = (bf16[576,384]{1,0:T(8,128)(2,1)S(1)}, bf16[576,384]{1,0:T(8,128)(2,1)S(1)}, u32[]{:S(2)}, u32[]{:S(2)}) collective-permute-start(bf16[576,384]{1,0:T(8,128)(2,1)S(1)} %collective-permute-done.2.refs_0_), channel_id=1, source_target_pairs={{0,4},{4,8},{8,12},{12,14},{14,10},{10,6},{6,2},{2,0},{5,1},{9,5},... | collective-permute-start | bytes 1327112 | tf_op jit(solution)/shard_map/ppermute | solution.py:280
  22.3 0.7 %copy-start.2 = (s32[108]{0:T(128)S(1)}, s32[108]{0:T(128)}, u32[]{:S(2)}) copy-start(s32[108]{0:T(128)} %get-tuple-element.24.order) | copy-start | bytes 1300
  22.9 0.6 %copy-start.3 = (s32[17]{0:T(128)S(1)}, s32[17]{0:T(128)}, u32[]{:S(2)}) copy-start(s32[17]{0:T(128)} %get-tuple-element.25.starts) | copy-start | bytes 208
  25.6 10.4 %collective-permute-start.12 = (bf16[576,384]{1,0:T(8,128)(2,1)S(1)}, bf16[576,384]{1,0:T(8,128)(2,1)S(1)}, u32[]{:S(2)}, u32[]{:S(2)}) collective-permute-start(bf16[576,384]{1,0:T(8,128)(2,1)S(1)} %collective-permute-done.2.refs_0_), channel_id=1, source_target_pairs={{0,1},{1,0},{2,3},{3,2},{4,5},{5,4},{6,7},{7,6},{8,9},{9,8},{10,11... | collective-permute-start | bytes 1327112 | tf_op jit(solution)/shard_map/ppermute | solution.py:281
  29.2 13.5 %collective-permute-start.11 = (bf16[576,384]{1,0:T(8,128)(2,1)S(1)}, bf16[576,384]{1,0:T(8,128)(2,1)S(1)}, u32[]{:S(2)}, u32[]{:S(2)}) collective-permute-start(bf16[576,384]{1,0:T(8,128)(2,1)S(1)} %collective-permute-done.7.refs_0_), channel_id=1, source_target_pairs={{0,1},{1,0},{2,3},{3,2},{4,5},{5,4},{6,7},{7,6},{8,9},{9,8},{10,11... | collective-permute-start | bytes 1327112 | tf_op jit(solution)/shard_map/ppermute | solution.py:281
  29.6 9.8 %collective-permute-start.8 = (bf16[576,384]{1,0:T(8,128)(2,1)S(1)}, bf16[576,384]{1,0:T(8,128)(2,1)S(1)}, u32[]{:S(2)}, u32[]{:S(2)}) collective-permute-start(bf16[576,384]{1,0:T(8,128)(2,1)S(1)} %collective-permute-done.7.refs_0_), channel_id=1, source_target_pairs={{0,4},{4,8},{8,12},{12,14},{14,10},{10,6},{6,2},{2,0},{5,1},{9,5},... | collective-permute-start | bytes 1327112 | tf_op jit(solution)/shard_map/ppermute | solution.py:280
  31.1 15.0 %collective-permute-start.10 = (bf16[576,384]{1,0:T(8,128)(2,1)S(1)}, bf16[576,384]{1,0:T(8,128)(2,1)S(1)}, u32[]{:S(2)}, u32[]{:S(2)}) collective-permute-start(bf16[576,384]{1,0:T(8,128)(2,1)S(1)} %collective-permute-done.3.refs_0_), channel_id=1, source_target_pairs={{0,1},{1,0},{2,3},{3,2},{4,5},{5,4},{6,7},{7,6},{8,9},{9,8},{10,11... | collective-permute-start | bytes 1327112 | tf_op jit(solution)/shard_map/ppermute | solution.py:281
  31.2 11.4 %collective-permute-start.4 = (bf16[576,384]{1,0:T(8,128)(2,1)S(1)}, bf16[576,384]{1,0:T(8,128)(2,1)S(1)}, u32[]{:S(2)}, u32[]{:S(2)}) collective-permute-start(bf16[576,384]{1,0:T(8,128)(2,1)S(1)} %collective-permute-done.3.refs_0_), channel_id=1, source_target_pairs={{0,4},{4,8},{8,12},{12,14},{14,10},{10,6},{6,2},{2,0},{5,1},{9,5},... | collective-permute-start | bytes 1327112 | tf_op jit(solution)/shard_map/ppermute | solution.py:280
  39.4 10.0 %collective-permute-start.9 = (bf16[576,384]{1,0:T(8,128)(2,1)S(1)}, bf16[576,384]{1,0:T(8,128)(2,1)S(1)}, u32[]{:S(2)}, u32[]{:S(2)}) collective-permute-start(bf16[576,384]{1,0:T(8,128)(2,1)S(1)} %collective-permute-done.8.refs_0_), channel_id=1, source_target_pairs={{0,1},{1,0},{2,3},{3,2},{4,5},{5,4},{6,7},{7,6},{8,9},{9,8},{10,11... | collective-permute-start | bytes 1327112 | tf_op jit(solution)/shard_map/ppermute | solution.py:281
  42.7 8.9 %collective-permute-start.5 = (bf16[576,384]{1,0:T(8,128)(2,1)S(1)}, bf16[576,384]{1,0:T(8,128)(2,1)S(1)}, u32[]{:S(2)}, u32[]{:S(2)}) collective-permute-start(bf16[576,384]{1,0:T(8,128)(2,1)S(1)} %collective-permute-done.4.refs_0_), channel_id=1, source_target_pairs={{0,1},{1,0},{2,3},{3,2},{4,5},{5,4},{6,7},{7,6},{8,9},{9,8},{10,11... | collective-permute-start | bytes 1327112 | tf_op jit(solution)/shard_map/ppermute | solution.py:281
  51.6 2.8 %copy-start.1 = (bf16[96,576]{1,0:T(8,128)(2,1)S(1)}, bf16[96,576]{1,0:T(8,128)(2,1)}, u32[]{:S(2)}) copy-start(bf16[96,576]{1,0:T(8,128)(2,1)} %param.8) | copy-start | bytes 331780
where the time goes:
time: 55 us; the launch traced here: 54.3 us
  Pallas kernels  27.5 us (50%)
  starting transfers between devices  13.7 us (25%)
  waiting for transfers between devices  10.8 us (20%)
  local copies, waits for them, and re-layouts  1.27 us (2%)
  between operations  0.82 us (1%)
    pallas_call x8, Pallas kernels, attend(): pl.pallas_call(functools.partial(attend_kernel, first, before, last, coun...  23.7 us
    ppermute x7, starting transfers between devices, shards(): lax.ppermute(a, 'node', along)  12.4 us
    ppermute x7, waiting for transfers between devices, shards(): lax.ppermute(a, 'node', along)  10.7 us
    pallas_call x1, Pallas kernels, prepare(): pl.pallas_call(prepare_kernel, out_shape=(jax.ShapeDtypeStruct((rows + 2...  3.83 us
    unnamed x8, local copies, waits for them, and re-layouts  1.27 us
  transfers between devices with their start and end apart: 15, of which 4 were waited for; matrix products, arithmetic and copies ran while one was open for 0% of the time, Pallas kernels for 46%

commit v1 on v0

--- a/solution.py
+++ b/solution.py
@@ -274,16 +274,26 @@
         child_latent, pick.astype(jnp.bfloat16), (((0,), (0,)), ((), ())), preferred_element_type=jnp.float32
     ).astype(jnp.bfloat16)
 
+    first, result = 0, [None, None]
     phases = [[kept, other]]
-    streams = [mine, other]
-    for k in range(1, chips // 2 + 1):
-        streams = [lax.ppermute(a, "node", along) for a in streams[: 2 if 2 * k < chips else 1]]
-        phases += [[a, lax.ppermute(a, "node", across)] for a in streams]
-    first, before, result = 0, 0, (None, None)
-    for slots in phases:
-        last = slots is phases[-1]
-        result = attend(order, starts, first, query, own, slots, before, result[1], result[0], last)
-        first, before = first + len(slots), len(slots)
+    sent = [mine, other]
+
+    def work(phase, last=False):
+        nonlocal first, result
+        before = 2 if first else 0
+        result = attend(order, starts, first, query, own, phases[phase], before, result[1], result[0], last)
+        first += 2
+
+    for i in range(1, chips):
+        a = forward = lax.ppermute(sent[i - 1], "node", along)
+        if i >= 2:
+            work(i - 2)
+            forward, kept = lax.optimization_barrier((a, result[1]))
+            result = result[0], kept
+        sent.append(forward)
+        phases.append([a, lax.ppermute(a if i + 2 < chips else forward, "node", across)])
+    work(chips - 2)
+    work(chips - 1, True)
     return result
 
 

time: 55 us -> 48.6 us (0.88)
  waiting for transfers between devices: 10.8 us -> 5.27 us
  starting transfers between devices: 13.7 us -> 11.9 us
  Pallas kernels: 27.5 us -> 28.7 us
    ppermute x14, waiting for transfers between devices: 10.8 us -> 5.27 us  [the longest x7 5.25 us: shards(): a = forward = lax.ppermute(sent[i - 1], 'node', along)]
    ppermute x14, starting transfers between devices: 13.3 us -> 11.4 us  [the longest x7 10.7 us: shards(): a = forward = lax.ppermute(sent[i - 1], 'node', along)]
    pallas_call x8, Pallas kernels: 23.7 us -> 24.9 us  [attend(): pl.pallas_call(functools.partial(attend_kernel, first, before, last, coun...]
    unnamed x8 -> x10, local copies, waits for them, and re-layouts: 1.27 us -> 1.33 us
  transfers between devices with their start and end apart: 15 -> 15, of which waited for: 4 -> 4; matrix products, arithmetic and copies ran while one was open for 0% -> 0% of each run, Pallas kernels for 46% -> 51%
where the time goes in v1:
time: 48.6 us; the launch traced here: 48.2 us
  Pallas kernels  28.7 us (59%)
  starting transfers between devices  11.9 us (24%)
  waiting for transfers between devices  5.27 us (11%)
  local copies, waits for them, and re-layouts  1.33 us (3%)
  between operations  0.8 us (2%)
    pallas_call x8, Pallas kernels, attend(): pl.pallas_call(functools.partial(attend_kernel, first, before, last, coun...  24.9 us
    ppermute x7, starting transfers between devices, shards(): a = forward = lax.ppermute(sent[i - 1], 'node', along)  10.7 us
    ppermute x7, waiting for transfers between devices, shards(): a = forward = lax.ppermute(sent[i - 1], 'node', along)  5.25 us
    pallas_call x1, Pallas kernels, prepare(): pl.pallas_call(prepare_kernel, out_shape=(jax.ShapeDtypeStruct((rows + 2...  3.83 us
    unnamed x10, local copies, waits for them, and re-layouts  1.33 us
  transfers between devices with their start and end apart: 15, of which 4 were waited for; matrix products, arithmetic and copies ran while one was open for 0% of the time, Pallas kernels for 51%

profile of v1, /device:TPU:0, one launch (start us, length us, event | category | flops | bytes accessed | tf_op | source)
XLA Modules:
  0.0 48.2 jit_solution(16900566007221886630)
XLA Ops:
  0.0 0.0 copy-start
  0.0 0.5 collective-permute-start
  0.5 2.6 %collective-permute-start.1 = (bf16[576,384]{1,0:T(8,128)(2,1)}, bf16[576,384]{1,0:T(8,128)(2,1)S(1)}, u32[]{:S(2)}, u32[]{:S(2)}) collective-permute-start(bf16[576,384]{1,0:T(8,128)(2,1)} %bitcast.8), channel_id=1, source_target_pairs={{0,4},{4,8},{8,12},{12,14},{14,10},{10,6},{6,2},{2,0},{5,1},{9,5},... | collective-permute-start | bytes 1327112 | tf_op jit(solution)/shard_map/ppermute | solution.py:288
  3.7 0.0 collective-permute-done._
  3.7 3.8 %shard_map.64 = (s32[108]{0:T(128)}, s32[17]{0:T(128)}, bf16[96,64,576]{2,1,0:T(8,128)(2,1)S(1)}, bf16[576,384]{1,0:T(8,128)(2,1)S(1)}, bf16[576,384]{1,0:T(8,128)(2,1)S(1)}) custom-call(s32[16]{0:T(128)} %place_in.1, s32[1,96]{1,0:T(1,128)} %bitcast.10, s32[1]{0:T(128)S(6)} %copy.23.live_in, ...), custom_call_target="tpu_custom_call", output_to_operand_aliasing={{4}: (5, {})} | custom-call | bytes 14155776 | tf_op jit(solution)/shard_map/pallas_call | solution.py:102
  7.6 1.6 %collective-permute-start.4 = (bf16[576,384]{1,0:T(8,128)(2,1)S(1)}, bf16[576,384]{1,0:T(8,128)(2,1)S(1)}, u32[]{:S(2)}, u32[]{:S(2)}) collective-permute-start(bf16[576,384]{1,0:T(8,128)(2,1)S(1)} %get-tuple-element.39.refs_1_), channel_id=1, source_target_pairs={{0,4},{4,8},{8,12},{12,14},{14,10},{10,6},{6,2},{2,0},{5,1},{9,5},... | collective-permute-start | bytes 1327112 | tf_op jit(solution)/shard_map/ppermute | solution.py:288
  9.2 0.3 collective-permute-done.1.refs_0_
  9.5 0.0 collective-permute-start.3
  9.5 0.0 copy-done
  9.5 0.2 fusion.own
  9.8 2.1 %collective-permute-start.2 = (bf16[576,384]{1,0:T(8,128)(2,1)S(1)}, bf16[576,384]{1,0:T(8,128)(2,1)S(1)}, u32[]{:S(2)}, u32[]{:S(2)}) collective-permute-start(bf16[576,384]{1,0:T(8,128)(2,1)S(1)} %collective-permute-done.1.refs_0_), channel_id=1, source_target_pairs={{0,4},{4,8},{8,12},{12,14},{14,10},{10,6},{6,2},{2,0},{5,1},{9,5},... | collective-permute-start | bytes 1327112 | tf_op jit(solution)/shard_map/ppermute | solution.py:288
  11.9 0.0 copy-start.2
  11.9 0.7 %copy-done.2 = s32[108]{0:T(128)S(1)} copy-done((s32[108]{0:T(128)S(1)}, s32[108]{0:T(128)}, u32[]{:S(2)}) %copy-start.2) | copy-done | bytes 456
  12.6 0.0 copy-start.3
  12.6 0.7 %copy-done.3 = s32[17]{0:T(128)S(1)} copy-done((s32[17]{0:T(128)S(1)}, s32[17]{0:T(128)}, u32[]{:S(2)}) %copy-start.3) | copy-done | bytes 92
  13.2 2.0 %shard_map.65 = (bf16[96,64,512]{2,1,0:T(8,128)(2,1)}, bf16[102,64,512]{2,1,0:T(8,128)(2,1)S(1)}) custom-call(s32[108]{0:T(128)S(1)} %copy-done.2, s32[17]{0:T(128)S(1)} %copy-done.3, bf16[96,64,576]{2,1,0:T(8,128)(2,1)S(1)} %get-tuple-element.38.query, bf16[576,128]{1,0:T(8,128)(2,1)S(1)} %fusion.own, bf16[576,384]{1,0:T(8,128)(2,1)S(1)} %get-tuple-element.40.refs_0_, ...), custom_call_target="tpu_custom_call" | custom-call | flops 3422552064 | bytes 7864320 | tf_op jit(solution)/shard_map/pallas_call | solution.py:228
  15.2 0.7 %collective-permute-done.4.refs_0_ = bf16[576,384]{1,0:T(8,128)(2,1)S(1)} collective-permute-done((bf16[576,384]{1,0:T(8,128)(2,1)S(1)}, bf16[576,384]{1,0:T(8,128)(2,1)S(1)}, u32[]{:S(2)}, u32[]{:S(2)}) %collective-permute-start.4) | collective-permute-done | bytes 442400 | tf_op jit(solution)/shard_map/ppermute | solution.py:288
  15.9 1.6 %collective-permute-start.7 = (bf16[576,384]{1,0:T(8,128)(2,1)S(1)}, bf16[576,384]{1,0:T(8,128)(2,1)S(1)}, u32[]{:S(2)}, u32[]{:S(2)}) collective-permute-start(bf16[576,384]{1,0:T(8,128)(2,1)S(1)} %collective-permute-done.4.refs_0_), channel_id=1, source_target_pairs={{0,4},{4,8},{8,12},{12,14},{14,10},{10,6},{6,2},{2,0},{5,1},{9,5},... | collective-permute-start | bytes 1327112 | tf_op jit(solution)/shard_map/ppermute | solution.py:288
  17.5 0.5 %collective-permute-start.8 = (bf16[576,384]{1,0:T(8,128)(2,1)S(1)}, bf16[576,384]{1,0:T(8,128)(2,1)S(1)}, u32[]{:S(2)}, u32[]{:S(2)}) collective-permute-start(bf16[576,384]{1,0:T(8,128)(2,1)S(1)} %collective-permute-done.4.refs_0_), channel_id=1, source_target_pairs={{0,1},{1,0},{2,3},{3,2},{4,5},{5,4},{6,7},{7,6},{8,9},{9,8},{10,11... | collective-permute-start | bytes 1327112 | tf_op jit(solution)/shard_map/ppermute | solution.py:294
  18.0 0.0 collective-permute-done.3.refs_1_
  18.0 0.0 copy-start.4
  18.0 3.3 %shard_map.66 = (bf16[96,64,512]{2,1,0:T(8,128)(2,1)}, bf16[102,64,512]{2,1,0:T(8,128)(2,1)S(1)}) custom-call(s32[108]{0:T(128)S(1)} %copy-done.2, s32[17]{0:T(128)S(1)} %copy-done.3, bf16[96,64,576]{2,1,0:T(8,128)(2,1)S(1)} %get-tuple-element.38.query, bf16[576,128]{1,0:T(8,128)(2,1)S(1)} %fusion.own, ...), custom_call_target="tpu_custom_call", output_to_operand_aliasing={{0}: (7, {})} | custom-call | flops 3422552064 | bytes 7864320 | tf_op jit(solution)/shard_map/pallas_call | solution.py:228
  21.3 0.0 collective-permute-done.2.refs_0_
  21.3 0.9 %collective-permute-start.5 = (bf16[576,384]{1,0:T(8,128)(2,1)S(1)}, bf16[576,384]{1,0:T(8,128)(2,1)S(1)}, u32[]{:S(2)}, u32[]{:S(2)}) collective-permute-start(bf16[576,384]{1,0:T(8,128)(2,1)S(1)} %collective-permute-done.2.refs_0_), channel_id=1, source_target_pairs={{0,4},{4,8},{8,12},{12,14},{14,10},{10,6},{6,2},{2,0},{5,1},{9,5},... | collective-permute-start | bytes 1327112 | tf_op jit(solution)/shard_map/ppermute | solution.py:288
  22.3 0.0 collective-permute-start.6
  22.3 3.2 %collective-permute-done.7.refs_0_ = bf16[576,384]{1,0:T(8,128)(2,1)S(1)} collective-permute-done((bf16[576,384]{1,0:T(8,128)(2,1)S(1)}, bf16[576,384]{1,0:T(8,128)(2,1)S(1)}, u32[]{:S(2)}, u32[]{:S(2)}) %collective-permute-start.7) | collective-permute-done | bytes 442400 | tf_op jit(solution)/shard_map/ppermute | solution.py:288
  25.4 0.0 collective-permute-start.12
  25.4 0.0 collective-permute-done.8.refs_1_
  25.4 0.0 copy-done.4
  25.4 3.4 %shard_map.67 = (bf16[96,64,512]{2,1,0:T(8,128)(2,1)}, bf16[102,64,512]{2,1,0:T(8,128)(2,1)S(1)}) custom-call(s32[108]{0:T(128)S(1)} %copy-done.2, s32[17]{0:T(128)S(1)} %copy-done.4, bf16[96,64,576]{2,1,0:T(8,128)(2,1)S(1)} %get-tuple-element.38.query, bf16[576,128]{1,0:T(8,128)(2,1)S(1)} %fusion.own, ...), custom_call_target="tpu_custom_call", output_to_operand_aliasing={{0}: (7, {})} | custom-call | flops 3422552064 | bytes 7864320 | tf_op jit(solution)/shard_map/pallas_call | solution.py:228
  28.8 0.3 collective-permute-start.11
  29.1 1.0 %collective-permute-done.5.refs_0_ = bf16[576,384]{1,0:T(8,128)(2,1)S(1)} collective-permute-done((bf16[576,384]{1,0:T(8,128)(2,1)S(1)}, bf16[576,384]{1,0:T(8,128)(2,1)S(1)}, u32[]{:S(2)}, u32[]{:S(2)}) %collective-permute-start.5) | collective-permute-done | bytes 442400 | tf_op jit(solution)/shard_map/ppermute | solution.py:288
  30.2 0.1 collective-permute-start.10
  30.2 0.0 collective-permute-done.6.refs_1_
  30.2 3.4 %shard_map.68 = (bf16[96,64,512]{2,1,0:T(8,128)(2,1)}, bf16[102,64,512]{2,1,0:T(8,128)(2,1)S(1)}) custom-call(s32[108]{0:T(128)S(1)} %copy-done.2, s32[17]{0:T(128)S(1)} %copy-done.4, bf16[96,64,576]{2,1,0:T(8,128)(2,1)S(1)} %get-tuple-element.38.query, bf16[576,128]{1,0:T(8,128)(2,1)S(1)} %fusion.own, ...), custom_call_target="tpu_custom_call", output_to_operand_aliasing={{0}: (7, {})} | custom-call | flops 3422552064 | bytes 7864320 | tf_op jit(solution)/shard_map/pallas_call | solution.py:228
  33.6 1.5 %collective-permute-start.9 = (bf16[576,384]{1,0:T(8,128)(2,1)S(1)}, bf16[576,384]{1,0:T(8,128)(2,1)S(1)}, u32[]{:S(2)}, u32[]{:S(2)}) collective-permute-start(bf16[576,384]{1,0:T(8,128)(2,1)S(1)} %collective-permute-done.5.refs_0_), channel_id=1, source_target_pairs={{0,4},{4,8},{8,12},{12,14},{14,10},{10,6},{6,2},{2,0},{5,1},{9,5},... | collective-permute-start | bytes 1327112 | tf_op jit(solution)/shard_map/ppermute | solution.py:288
  35.1 0.0 collective-permute-done.12.refs_1_
  35.1 3.3 %shard_map.69 = (bf16[96,64,512]{2,1,0:T(8,128)(2,1)}, bf16[102,64,512]{2,1,0:T(8,128)(2,1)S(1)}) custom-call(s32[108]{0:T(128)S(1)} %copy-done.2, s32[17]{0:T(128)S(1)} %copy-done.4, bf16[96,64,576]{2,1,0:T(8,128)(2,1)S(1)} %get-tuple-element.38.query, bf16[576,128]{1,0:T(8,128)(2,1)S(1)} %fusion.own, ...), custom_call_target="tpu_custom_call", output_to_operand_aliasing={{0}: (7, {})} | custom-call | flops 3422552064 | bytes 7864320 | tf_op jit(solution)/shard_map/pallas_call | solution.py:228
  38.4 0.0 collective-permute-done.11.refs_0_
  38.4 0.1 collective-permute-start.14
  38.5 0.0 collective-permute-done.10.refs_1_
  38.5 3.4 %shard_map.70 = (bf16[96,64,512]{2,1,0:T(8,128)(2,1)}, bf16[102,64,512]{2,1,0:T(8,128)(2,1)S(1)}) custom-call(s32[108]{0:T(128)S(1)} %copy-done.2, s32[17]{0:T(128)S(1)} %copy-done.4, bf16[96,64,576]{2,1,0:T(8,128)(2,1)S(1)} %get-tuple-element.38.query, bf16[576,128]{1,0:T(8,128)(2,1)S(1)} %fusion.own, ...), custom_call_target="tpu_custom_call", output_to_operand_aliasing={{0}: (7, {})} | custom-call | flops 3422552064 | bytes 7864320 | tf_op jit(solution)/shard_map/pallas_call | solution.py:228
  41.9 0.0 collective-permute-done.9.refs_0_
  42.0 0.1 collective-permute-start.13
  42.0 0.0 collective-permute-done.14.refs_1_
  42.0 2.1 %shard_map.71 = (bf16[96,64,512]{2,1,0:T(8,128)(2,1)}, bf16[102,64,512]{2,1,0:T(8,128)(2,1)S(1)}) custom-call(s32[108]{0:T(128)S(1)} %copy-done.2, s32[17]{0:T(128)S(1)} %copy-done.4, bf16[96,64,576]{2,1,0:T(8,128)(2,1)S(1)} %get-tuple-element.38.query, bf16[576,128]{1,0:T(8,128)(2,1)S(1)} %fusion.own, ...), custom_call_target="tpu_custom_call", output_to_operand_aliasing={{0}: (7, {})} | custom-call | flops 3422552064 | bytes 7864320 | tf_op jit(solution)/shard_map/pallas_call | solution.py:228
  44.1 0.0 collective-permute-done.13.refs_1_
  44.1 0.0 copy-start.1
  44.2 4.0 %shard_map.72 = bf16[96,64,512]{2,1,0:T(8,128)(2,1)} custom-call(s32[108]{0:T(128)S(1)} %copy-done.2, s32[17]{0:T(128)S(1)} %copy-done.4, bf16[96,64,576]{2,1,0:T(8,128)(2,1)S(1)} %get-tuple-element.38.query, bf16[576,128]{1,0:T(8,128)(2,1)S(1)} %fusion.own, bf16[576,384]{1,0:T(8,128)(2,1)S(1)} %collective-permute-done.9.refs_0_, ...), custom_call_target="tpu_custom_call", output_to_operand_aliasing={{}: (7, {})} | custom-call | flops 3422552064 | bytes 7864320 | tf_op jit(solution)/shard_map/pallas_call | solution.py:228
  48.2 0.0 copy-done.1
Async XLA Ops:
  0.0 9.5 %copy-start = (bf16[96,576]{1,0:T(8,128)(2,1)S(1)}, bf16[96,576]{1,0:T(8,128)(2,1)}, u32[]{:S(2)}) copy-start(bf16[96,576]{1,0:T(8,128)(2,1)} %param.8) | copy-start | bytes 331780
  0.0 3.7 %collective-permute-start = (bf16[576,384]{1,0:T(8,128)(2,1)}, bf16[576,384]{1,0:T(8,128)(2,1)S(1)}, u32[]{:S(2)}, u32[]{:S(2)}) collective-permute-start(bf16[576,384]{1,0:T(8,128)(2,1)} %bitcast.7), channel_id=1, source_target_pairs={{0,1},{1,0},{2,3},{3,2},{4,5},{5,4},{6,7},{7,6},{8,9},{9,8},{10,11... | collective-permute-start | bytes 1327112 | tf_op jit(solution)/shard_map/ppermute | solution.py:267
  0.5 9.1 %collective-permute-start.1 = (bf16[576,384]{1,0:T(8,128)(2,1)}, bf16[576,384]{1,0:T(8,128)(2,1)S(1)}, u32[]{:S(2)}, u32[]{:S(2)}) collective-permute-start(bf16[576,384]{1,0:T(8,128)(2,1)} %bitcast.8), channel_id=1, source_target_pairs={{0,4},{4,8},{8,12},{12,14},{14,10},{10,6},{6,2},{2,0},{5,1},{9,5},... | collective-permute-start | bytes 1327112 | tf_op jit(solution)/shard_map/ppermute | solution.py:288
  7.6 8.4 %collective-permute-start.4 = (bf16[576,384]{1,0:T(8,128)(2,1)S(1)}, bf16[576,384]{1,0:T(8,128)(2,1)S(1)}, u32[]{:S(2)}, u32[]{:S(2)}) collective-permute-start(bf16[576,384]{1,0:T(8,128)(2,1)S(1)} %get-tuple-element.39.refs_1_), channel_id=1, source_target_pairs={{0,4},{4,8},{8,12},{12,14},{14,10},{10,6},{6,2},{2,0},{5,1},{9,5},... | collective-permute-start | bytes 1327112 | tf_op jit(solution)/shard_map/ppermute | solution.py:288
  9.5 8.5 %collective-permute-start.3 = (bf16[576,384]{1,0:T(8,128)(2,1)S(1)}, bf16[576,384]{1,0:T(8,128)(2,1)S(1)}, u32[]{:S(2)}, u32[]{:S(2)}) collective-permute-start(bf16[576,384]{1,0:T(8,128)(2,1)S(1)} %collective-permute-done.1.refs_0_), channel_id=1, source_target_pairs={{0,1},{1,0},{2,3},{3,2},{4,5},{5,4},{6,7},{7,6},{8,9},{9,8},{10,11... | collective-permute-start | bytes 1327112 | tf_op jit(solution)/shard_map/ppermute | solution.py:294
  9.8 11.6 %collective-permute-start.2 = (bf16[576,384]{1,0:T(8,128)(2,1)S(1)}, bf16[576,384]{1,0:T(8,128)(2,1)S(1)}, u32[]{:S(2)}, u32[]{:S(2)}) collective-permute-start(bf16[576,384]{1,0:T(8,128)(2,1)S(1)} %collective-permute-done.1.refs_0_), channel_id=1, source_target_pairs={{0,4},{4,8},{8,12},{12,14},{14,10},{10,6},{6,2},{2,0},{5,1},{9,5},... | collective-permute-start | bytes 1327112 | tf_op jit(solution)/shard_map/ppermute | solution.py:288
  11.9 0.7 %copy-start.2 = (s32[108]{0:T(128)S(1)}, s32[108]{0:T(128)}, u32[]{:S(2)}) copy-start(s32[108]{0:T(128)} %get-tuple-element.36.order) | copy-start | bytes 1300
  12.6 0.7 %copy-start.3 = (s32[17]{0:T(128)S(1)}, s32[17]{0:T(128)}, u32[]{:S(2)}) copy-start(s32[17]{0:T(128)} %get-tuple-element.37.starts) | copy-start | bytes 208
  15.9 9.5 %collective-permute-start.7 = (bf16[576,384]{1,0:T(8,128)(2,1)S(1)}, bf16[576,384]{1,0:T(8,128)(2,1)S(1)}, u32[]{:S(2)}, u32[]{:S(2)}) collective-permute-start(bf16[576,384]{1,0:T(8,128)(2,1)S(1)} %collective-permute-done.4.refs_0_), channel_id=1, source_target_pairs={{0,4},{4,8},{8,12},{12,14},{14,10},{10,6},{6,2},{2,0},{5,1},{9,5},... | collective-permute-start | bytes 1327112 | tf_op jit(solution)/shard_map/ppermute | solution.py:288
  17.5 7.9 %collective-permute-start.8 = (bf16[576,384]{1,0:T(8,128)(2,1)S(1)}, bf16[576,384]{1,0:T(8,128)(2,1)S(1)}, u32[]{:S(2)}, u32[]{:S(2)}) collective-permute-start(bf16[576,384]{1,0:T(8,128)(2,1)S(1)} %collective-permute-done.4.refs_0_), channel_id=1, source_target_pairs={{0,1},{1,0},{2,3},{3,2},{4,5},{5,4},{6,7},{7,6},{8,9},{9,8},{10,11... | collective-permute-start | bytes 1327112 | tf_op jit(solution)/shard_map/ppermute | solution.py:294
  18.0 7.4 %copy-start.4 = (s32[17]{0:T(128)S(1)}, s32[17]{0:T(128)}, u32[]{:S(2)}) copy-start(s32[17]{0:T(128)} %get-tuple-element.37.starts) | copy-start | bytes 208
  21.3 8.8 %collective-permute-start.5 = (bf16[576,384]{1,0:T(8,128)(2,1)S(1)}, bf16[576,384]{1,0:T(8,128)(2,1)S(1)}, u32[]{:S(2)}, u32[]{:S(2)}) collective-permute-start(bf16[576,384]{1,0:T(8,128)(2,1)S(1)} %collective-permute-done.2.refs_0_), channel_id=1, source_target_pairs={{0,4},{4,8},{8,12},{12,14},{14,10},{10,6},{6,2},{2,0},{5,1},{9,5},... | collective-permute-start | bytes 1327112 | tf_op jit(solution)/shard_map/ppermute | solution.py:288
  22.3 8.0 %collective-permute-start.6 = (bf16[576,384]{1,0:T(8,128)(2,1)S(1)}, bf16[576,384]{1,0:T(8,128)(2,1)S(1)}, u32[]{:S(2)}, u32[]{:S(2)}) collective-permute-start(bf16[576,384]{1,0:T(8,128)(2,1)S(1)} %collective-permute-done.2.refs_0_), channel_id=1, source_target_pairs={{0,1},{1,0},{2,3},{3,2},{4,5},{5,4},{6,7},{7,6},{8,9},{9,8},{10,11... | collective-permute-start | bytes 1327112 | tf_op jit(solution)/shard_map/ppermute | solution.py:294
  25.4 9.7 %collective-permute-start.12 = (bf16[576,384]{1,0:T(8,128)(2,1)S(1)}, bf16[576,384]{1,0:T(8,128)(2,1)S(1)}, u32[]{:S(2)}, u32[]{:S(2)}) collective-permute-start(bf16[576,384]{1,0:T(8,128)(2,1)S(1)} %collective-permute-done.7.refs_0_), channel_id=1, source_target_pairs={{0,1},{1,0},{2,3},{3,2},{4,5},{5,4},{6,7},{7,6},{8,9},{9,8},{10,11... | collective-permute-start | bytes 1327112 | tf_op jit(solution)/shard_map/ppermute | solution.py:294
  28.8 9.6 %collective-permute-start.11 = (bf16[576,384]{1,0:T(8,128)(2,1)S(1)}, bf16[576,384]{1,0:T(8,128)(2,1)S(1)}, u32[]{:S(2)}, u32[]{:S(2)}) collective-permute-start(bf16[576,384]{1,0:T(8,128)(2,1)S(1)} %collective-permute-done.7.refs_0_), channel_id=1, source_target_pairs={{0,4},{4,8},{8,12},{12,14},{14,10},{10,6},{6,2},{2,0},{5,1},{9,5},... | collective-permute-start | bytes 1327112 | tf_op jit(solution)/shard_map/ppermute | solution.py:288
  30.2 8.4 %collective-permute-start.10 = (bf16[576,384]{1,0:T(8,128)(2,1)S(1)}, bf16[576,384]{1,0:T(8,128)(2,1)S(1)}, u32[]{:S(2)}, u32[]{:S(2)}) collective-permute-start(bf16[576,384]{1,0:T(8,128)(2,1)S(1)} %collective-permute-done.5.refs_0_), channel_id=1, source_target_pairs={{0,1},{1,0},{2,3},{3,2},{4,5},{5,4},{6,7},{7,6},{8,9},{9,8},{10,11... | collective-permute-start | bytes 1327112 | tf_op jit(solution)/shard_map/ppermute | solution.py:294
  33.6 8.4 %collective-permute-start.9 = (bf16[576,384]{1,0:T(8,128)(2,1)S(1)}, bf16[576,384]{1,0:T(8,128)(2,1)S(1)}, u32[]{:S(2)}, u32[]{:S(2)}) collective-permute-start(bf16[576,384]{1,0:T(8,128)(2,1)S(1)} %collective-permute-done.5.refs_0_), channel_id=1, source_target_pairs={{0,4},{4,8},{8,12},{12,14},{14,10},{10,6},{6,2},{2,0},{5,1},{9,5},... | collective-permute-start | bytes 1327112 | tf_op jit(solution)/shard_map/ppermute | solution.py:288
  38.4 3.6 %collective-permute-start.14 = (bf16[576,384]{1,0:T(8,128)(2,1)S(1)}, bf16[576,384]{1,0:T(8,128)(2,1)S(1)}, u32[]{:S(2)}, u32[]{:S(2)}) collective-permute-start(bf16[576,384]{1,0:T(8,128)(2,1)S(1)} %collective-permute-done.11.refs_0_), channel_id=1, source_target_pairs={{0,1},{1,0},{2,3},{3,2},{4,5},{5,4},{6,7},{7,6},{8,9},{9,8},{10,11... | collective-permute-start | bytes 1327112 | tf_op jit(solution)/shard_map/ppermute | solution.py:294
  42.0 2.2 %collective-permute-start.13 = (bf16[576,384]{1,0:T(8,128)(2,1)S(1)}, bf16[576,384]{1,0:T(8,128)(2,1)S(1)}, u32[]{:S(2)}, u32[]{:S(2)}) collective-permute-start(bf16[576,384]{1,0:T(8,128)(2,1)S(1)} %collective-permute-done.9.refs_0_), channel_id=1, source_target_pairs={{0,1},{1,0},{2,3},{3,2},{4,5},{5,4},{6,7},{7,6},{8,9},{9,8},{10,11... | collective-permute-start | bytes 1327112 | tf_op jit(solution)/shard_map/ppermute | solution.py:294
  44.1 4.1 %copy-start.1 = (bf16[96,576]{1,0:T(8,128)(2,1)S(1)}, bf16[96,576]{1,0:T(8,128)(2,1)}, u32[]{:S(2)}) copy-start(bf16[96,576]{1,0:T(8,128)(2,1)} %param.8) | copy-start | bytes 331780

commit v2 on v1

--- a/solution.py
+++ b/solution.py
@@ -31,7 +31,7 @@
 
 
 def prepare_kernel(
-    place_in, parent_in, live_in, query_in, mine_in, _, order, starts, query, mine, __, place, parent, live, slots, names, sem
+    place_in, parent_in, live_in, query_in, mine_in, _, plan, query, mine, __, place, parent, live, slots, names, starts, sem
 ):
     rows = parent.shape[1]
     parents = place.shape[0]
@@ -87,12 +87,18 @@
         s = slots[i]
         j = starts[s] - 1
         starts[s] = j
-        order[j] = i
+        plan[dead + 1 + j] = i
         return 0
 
     lax.fori_loop(0, rows, put, 0, unroll=8)
-    for i in range(rows, order.shape[0]):
-        order[i] = 0
+    for i in range(dead + 1 + rows, plan.shape[0]):
+        plan[i] = 0
+
+    def tell(s, _):
+        plan[s] = starts[s]
+        return 0
+
+    lax.fori_loop(0, dead + 1, tell, 0)
     for copy in big:
         copy.wait()
 
@@ -102,35 +108,38 @@
     return pl.pallas_call(
         prepare_kernel,
         out_shape=(
-            jax.ShapeDtypeStruct((rows + 2 * BLOCK,), jnp.int32),
-            jax.ShapeDtypeStruct((parents + 1,), jnp.int32),
+            jax.ShapeDtypeStruct((parents + 1 + rows + BLOCK,), jnp.int32),
             pltpu.VMEM(query.shape, query.dtype),
             pltpu.VMEM(mine.shape, mine.dtype),
             pltpu.VMEM(other.shape, other.dtype),
         ),
         in_specs=[ANY] * 5 + [VMEM],
-        out_specs=(SMEM, SMEM, VMEM, VMEM, VMEM),
+        out_specs=(SMEM, VMEM, VMEM, VMEM),
         scratch_shapes=[
             pltpu.SMEM(place.shape, jnp.int32),
             pltpu.SMEM(parent.shape, jnp.int32),
             pltpu.SMEM(live.shape, jnp.int32),
             pltpu.SMEM((rows,), jnp.int32),
             pltpu.SMEM(place.shape, jnp.int32),
+            pltpu.SMEM((parents + 1,), jnp.int32),
             pltpu.SemaphoreType.DMA((5,)),
         ],
-        input_output_aliases={5: 4},
+        input_output_aliases={5: 3},
         compiler_params=pltpu.CompilerParams(vmem_limit_bytes=46 * 1024 * 1024),
         cost_estimate=pl.CostEstimate(flops=0, bytes_accessed=2 * query.size * 2, transcendentals=0),
     )(place, parent, live, query, mine, other)
 
 
-def attend_kernel(first, before, last, arrays, order, starts, query, own, *refs):
+def attend_kernel(first, before, last, arrays, plan, query, own, *refs):
     slots = refs[:arrays]
     out, ov, kv, even, odd, zeros, blocks, out_sem = refs[-8:]
     done = refs[arrays] if before else None
     rows, heads, depth = query.shape
     prefix = slots[0].shape[-1]
     width = kv.shape[2]
+    dead = plan.shape[0] - BLOCK - rows - 1
+    order = plan.at[pl.ds(dead + 1, rows + BLOCK)]
+    starts = plan.at[pl.ds(0, dead + 1)]
     base = starts[first]
     end = starts[first + arrays]
 
@@ -138,7 +147,7 @@
         from_row, to_row = starts[first - before], base
     else:
         zeros[...] = jnp.zeros_like(zeros)
-        from_row, to_row = starts[starts.shape[0] - 1], rows
+        from_row, to_row = starts[dead], rows
 
     @pl.loop(from_row, to_row)
     def _(j):
@@ -159,11 +168,6 @@
 
         lax.fori_loop(0, more, note, 0)
         number = number + more
-    for b in range(2):
-        blocks[0, number + b] = 0
-        blocks[1, number + b] = rows
-        blocks[2, number + b] = rows
-
     column = lax.broadcasted_iota(jnp.int32, (heads, width - prefix), 1)
 
     def score(b, to):
@@ -192,18 +196,23 @@
         def _(j):
             pltpu.make_async_copy(ov.at[j], out.at[order[j]], out_sem).start()
 
-    @pl.when(number > 0)
+    @pl.loop(0, number // 2)
+    def _(pair):
+        b = pair * 2
+        score(b, even)
+        score(b + 1, odd)
+        finish(b, even)
+        finish(b + 1, odd)
+        if last:
+            send(b)
+            send(b + 1)
+
+    @pl.when(number % 2 == 1)
     def _():
-        @pl.loop(0, (number + 1) // 2)
-        def _(pair):
-            b = pair * 2
-            score(b, even)
-            score(b + 1, odd)
-            finish(b, even)
-            finish(b + 1, odd)
-            if last:
-                send(b)
-                send(b + 1)
+        score(number - 1, even)
+        finish(number - 1, even)
+        if last:
+            send(number - 1)
 
     @pl.loop(from_row, to_row)
     def _(j):
@@ -216,19 +225,19 @@
             pltpu.make_async_copy(zeros, out.at[0], out_sem).wait()
 
 
-def attend(order, starts, first, query, own, slots, before=0, done=None, out=None, last=False):
+def attend(plan, first, query, own, slots, before=0, done=None, out=None, last=False):
     rows, heads, depth = query.shape
     count = len(slots)
     prefix = slots[0].shape[-1]
     width = prefix + own.shape[1]
-    operands = [order, starts, query, own, *slots] + ([done, out] if before else [])
-    work = rows * heads * count // (starts.shape[0] - 1)
+    operands = [plan, query, own, *slots] + ([done, out] if before else [])
+    work = rows * heads * count // (plan.shape[0] - BLOCK - rows - 1)
     result = jax.ShapeDtypeStruct((rows, heads, LAT), jnp.bfloat16)
     made = pltpu.VMEM((rows + BLOCK, heads, LAT), jnp.bfloat16)
     return pl.pallas_call(
         functools.partial(attend_kernel, first, before, last, count),
         out_shape=result if last else (result, made),
-        in_specs=[SMEM, SMEM, VMEM, VMEM] + [VMEM] * count + [VMEM, ANY] * (before > 0),
+        in_specs=[SMEM, VMEM, VMEM] + [VMEM] * count + [VMEM, ANY] * (before > 0),
         out_specs=ANY if last else (ANY, VMEM),
         scratch_shapes=[made] * last + [
             pltpu.VMEM((count, depth, width), jnp.bfloat16),
@@ -265,7 +274,7 @@
 
     mine = jnp.swapaxes(parent_cache[0], 0, 1)
     other = lax.ppermute(mine, "node", across)
-    order, starts, query, kept, other = prepare(
+    plan, query, kept, other = prepare(
         parent_place, jnp.swapaxes(child_parent, 0, 1), live_rows, child_query, mine, other
     )
     padded = -(-rows // 128) * 128
@@ -274,24 +283,24 @@
         child_latent, pick.astype(jnp.bfloat16), (((0,), (0,)), ((), ())), preferred_element_type=jnp.float32
     ).astype(jnp.bfloat16)
 
-    first, result = 0, [None, None]
+    first, result = 0, (None, None)
     phases = [[kept, other]]
     sent = [mine, other]
 
     def work(phase, last=False):
         nonlocal first, result
         before = 2 if first else 0
-        result = attend(order, starts, first, query, own, phases[phase], before, result[1], result[0], last)
+        result = attend(plan, first, query, own, phases[phase], before, result[1], result[0], last)
         first += 2
 
     for i in range(1, chips):
         a = forward = lax.ppermute(sent[i - 1], "node", along)
         if i >= 2:
             work(i - 2)
-            forward, kept = lax.optimization_barrier((a, result[1]))
-            result = result[0], kept
+            forward, done = lax.optimization_barrier((a, result[1]))
+            result = result[0], done
         sent.append(forward)
-        phases.append([a, lax.ppermute(a if i + 2 < chips else forward, "node", across)])
+        phases.append([a, lax.ppermute(forward, "node", across)])
     work(chips - 2)
     work(chips - 1, True)
     return result

time: 48.6 us -> 46.5 us (0.957)
  Pallas kernels: 28.7 us -> 24.2 us
  starting transfers between devices: 11.9 us -> 13.5 us
  waiting for transfers between devices: 5.27 us -> 6.38 us
  local copies, waits for them, and re-layouts: 1.33 us -> 0.62 us
    pallas_call x8, Pallas kernels: 24.9 us -> 20.4 us  [attend(): pl.pallas_call(functools.partial(attend_kernel, first, before, last, coun...]
    ppermute x7, starting transfers between devices: 10.7 us -> 12.9 us  [shards(): a = forward = lax.ppermute(sent[i - 1], 'node', along)]
    ppermute x7, waiting for transfers between devices: 5.25 us -> 6.36 us  [shards(): a = forward = lax.ppermute(sent[i - 1], 'node', along)]
    unnamed x10 -> x8, local copies, waits for them, and re-layouts: 1.33 us -> 0.62 us
    ppermute x7, starting transfers between devices: 0.76 us -> 0.13 us  [shards(): phases.append([a, lax.ppermute(forward, 'node', across)])]
  transfers between devices with their start and end apart: 15 -> 15, of which waited for: 4 -> 7; matrix products, arithmetic and copies ran while one was open for 0% -> 1% of each run, Pallas kernels for 51% -> 47%
where the time goes in v2:
time: 46.5 us; the launch traced here: 45.9 us
  Pallas kernels  24.2 us (52%)
  starting transfers between devices  13.5 us (29%)
  waiting for transfers between devices  6.38 us (14%)
  between operations  0.94 us (2%)
  local copies, waits for them, and re-layouts  0.62 us (1%)
    pallas_call x8, Pallas kernels, attend(): pl.pallas_call(functools.partial(attend_kernel, first, before, last, coun...  20.4 us
    ppermute x7, starting transfers between devices, shards(): a = forward = lax.ppermute(sent[i - 1], 'node', along)  12.9 us
    ppermute x7, waiting for transfers between devices, shards(): a = forward = lax.ppermute(sent[i - 1], 'node', along)  6.36 us
    pallas_call x1, Pallas kernels, prepare(): pl.pallas_call(prepare_kernel, out_shape=(jax.ShapeDtypeStruct((parents +...  3.82 us
  transfers between devices with their start and end apart: 15, of which 7 were waited for; matrix products, arithmetic and copies ran while one was open for 1% of the time, Pallas kernels for 47%

profile of v2, /device:TPU:0, one launch (start us, length us, event | category | flops | bytes accessed | tf_op | source)
XLA Modules:
  0.0 45.9 jit_solution(18165791582170647401)
XLA Ops:
  0.0 0.0 copy-start
  0.0 0.5 collective-permute-start
  0.5 2.6 %collective-permute-start.1 = (bf16[576,384]{1,0:T(8,128)(2,1)}, bf16[576,384]{1,0:T(8,128)(2,1)S(1)}, u32[]{:S(2)}, u32[]{:S(2)}) collective-permute-start(bf16[576,384]{1,0:T(8,128)(2,1)} %bitcast.8), channel_id=1, source_target_pairs={{0,4},{4,8},{8,12},{12,14},{14,10},{10,6},{6,2},{2,0},{5,1},{9,5},... | collective-permute-start | bytes 1327112 | tf_op jit(solution)/shard_map/ppermute | solution.py:297
  3.7 0.0 collective-permute-done._
  3.7 3.8 %shard_map.64 = (s32[119]{0:T(128)}, bf16[96,64,576]{2,1,0:T(8,128)(2,1)S(1)}, bf16[576,384]{1,0:T(8,128)(2,1)S(1)}, bf16[576,384]{1,0:T(8,128)(2,1)S(1)}) custom-call(s32[16]{0:T(128)} %place_in.1, s32[1,96]{1,0:T(1,128)} %bitcast.10, s32[1]{0:T(128)S(6)} %copy.23.live_in, bf16[96,64,576]{2,1,0:T(8,128)(2,1)} %query_in.1, ...), custom_call_target="tpu_custom_call", output_to_operand_aliasing={{3}: (5, {})} | custom-call | bytes 14155776 | tf_op jit(solution)/shard_map/pallas_call | solution.py:108
  7.6 0.0 copy-start.3
  7.6 1.6 %collective-permute-start.4 = (bf16[576,384]{1,0:T(8,128)(2,1)S(1)}, bf16[576,384]{1,0:T(8,128)(2,1)S(1)}, u32[]{:S(2)}, u32[]{:S(2)}) collective-permute-start(bf16[576,384]{1,0:T(8,128)(2,1)S(1)} %get-tuple-element.37.refs_1_), channel_id=1, source_target_pairs={{0,4},{4,8},{8,12},{12,14},{14,10},{10,6},{6,2},{2,0},{5,1},{9,5},... | collective-permute-start | bytes 1327112 | tf_op jit(solution)/shard_map/ppermute | solution.py:297
  9.2 0.3 collective-permute-done.1.refs_0_
  9.5 0.0 collective-permute-start.3
  9.5 0.0 copy-done
  9.5 0.2 fusion.own
  9.8 2.1 %collective-permute-start.2 = (bf16[576,384]{1,0:T(8,128)(2,1)S(1)}, bf16[576,384]{1,0:T(8,128)(2,1)S(1)}, u32[]{:S(2)}, u32[]{:S(2)}) collective-permute-start(bf16[576,384]{1,0:T(8,128)(2,1)S(1)} %collective-permute-done.1.refs_0_), channel_id=1, source_target_pairs={{0,4},{4,8},{8,12},{12,14},{14,10},{10,6},{6,2},{2,0},{5,1},{9,5},... | collective-permute-start | bytes 1327112 | tf_op jit(solution)/shard_map/ppermute | solution.py:297
  11.9 0.0 copy-start.2
  11.9 0.6 %copy-done.2 = s32[119]{0:T(128)S(1)} copy-done((s32[119]{0:T(128)S(1)}, s32[119]{0:T(128)}, u32[]{:S(2)}) %copy-start.2) | copy-done | bytes 500
  12.5 2.1 %shard_map.65 = (bf16[96,64,512]{2,1,0:T(8,128)(2,1)}, bf16[102,64,512]{2,1,0:T(8,128)(2,1)S(1)}) custom-call(s32[119]{0:T(128)S(1)} %copy-done.2, bf16[96,64,576]{2,1,0:T(8,128)(2,1)S(1)} %get-tuple-element.36.query, bf16[576,128]{1,0:T(8,128)(2,1)S(1)} %fusion.own, bf16[576,384]{1,0:T(8,128)(2,1)S(1)} %get-tuple-element.38.refs_0_, ...), custom_call_target="tpu_custom_call" | custom-call | flops 3422552064 | bytes 7864320 | tf_op jit(solution)/shard_map/pallas_call | solution.py:237
  14.6 1.3 %collective-permute-done.4.refs_0_ = bf16[576,384]{1,0:T(8,128)(2,1)S(1)} collective-permute-done((bf16[576,384]{1,0:T(8,128)(2,1)S(1)}, bf16[576,384]{1,0:T(8,128)(2,1)S(1)}, u32[]{:S(2)}, u32[]{:S(2)}) %collective-permute-start.4) | collective-permute-done | bytes 442400 | tf_op jit(solution)/shard_map/ppermute | solution.py:297
  15.9 0.0 collective-permute-start.8
  15.9 1.6 %collective-permute-start.7 = (bf16[576,384]{1,0:T(8,128)(2,1)S(1)}, bf16[576,384]{1,0:T(8,128)(2,1)S(1)}, u32[]{:S(2)}, u32[]{:S(2)}) collective-permute-start(bf16[576,384]{1,0:T(8,128)(2,1)S(1)} %collective-permute-done.4.refs_0_), channel_id=1, source_target_pairs={{0,4},{4,8},{8,12},{12,14},{14,10},{10,6},{6,2},{2,0},{5,1},{9,5},... | collective-permute-start | bytes 1327112 | tf_op jit(solution)/shard_map/ppermute | solution.py:297
  17.5 0.0 collective-permute-done.3.refs_1_
  17.5 0.0 copy-done.3
  17.5 2.1 %shard_map.66 = (bf16[96,64,512]{2,1,0:T(8,128)(2,1)}, bf16[102,64,512]{2,1,0:T(8,128)(2,1)S(1)}) custom-call(s32[119]{0:T(128)S(1)} %copy-done.3, bf16[96,64,576]{2,1,0:T(8,128)(2,1)S(1)} %get-tuple-element.36.query, bf16[576,128]{1,0:T(8,128)(2,1)S(1)} %fusion.own, ...), custom_call_target="tpu_custom_call", output_to_operand_aliasing={{0}: (6, {})} | custom-call | flops 3422552064 | bytes 7864320 | tf_op jit(solution)/shard_map/pallas_call | solution.py:237
  19.6 1.1 %collective-permute-done.2.refs_0_ = bf16[576,384]{1,0:T(8,128)(2,1)S(1)} collective-permute-done((bf16[576,384]{1,0:T(8,128)(2,1)S(1)}, bf16[576,384]{1,0:T(8,128)(2,1)S(1)}, u32[]{:S(2)}, u32[]{:S(2)}) %collective-permute-start.2) | collective-permute-done | bytes 442400 | tf_op jit(solution)/shard_map/ppermute | solution.py:297
  20.7 0.0 collective-permute-start.6
  20.7 1.6 %collective-permute-start.5 = (bf16[576,384]{1,0:T(8,128)(2,1)S(1)}, bf16[576,384]{1,0:T(8,128)(2,1)S(1)}, u32[]{:S(2)}, u32[]{:S(2)}) collective-permute-start(bf16[576,384]{1,0:T(8,128)(2,1)S(1)} %collective-permute-done.2.refs_0_), channel_id=1, source_target_pairs={{0,4},{4,8},{8,12},{12,14},{14,10},{10,6},{6,2},{2,0},{5,1},{9,5},... | collective-permute-start | bytes 1327112 | tf_op jit(solution)/shard_map/ppermute | solution.py:297
  22.3 0.0 collective-permute-done.8.refs_1_
  22.3 3.0 %shard_map.67 = (bf16[96,64,512]{2,1,0:T(8,128)(2,1)}, bf16[102,64,512]{2,1,0:T(8,128)(2,1)S(1)}) custom-call(s32[119]{0:T(128)S(1)} %copy-done.3, bf16[96,64,576]{2,1,0:T(8,128)(2,1)S(1)} %get-tuple-element.36.query, bf16[576,128]{1,0:T(8,128)(2,1)S(1)} %fusion.own, ...), custom_call_target="tpu_custom_call", output_to_operand_aliasing={{0}: (6, {})} | custom-call | flops 3422552064 | bytes 7864320 | tf_op jit(solution)/shard_map/pallas_call | solution.py:237
  25.3 0.1 collective-permute-done.7.refs_0_
  25.4 0.1 collective-permute-start.12
  25.5 1.7 %collective-permute-start.11 = (bf16[576,384]{1,0:T(8,128)(2,1)S(1)}, bf16[576,384]{1,0:T(8,128)(2,1)S(1)}, u32[]{:S(2)}, u32[]{:S(2)}) collective-permute-start(bf16[576,384]{1,0:T(8,128)(2,1)S(1)} %collective-permute-done.7.refs_0_), channel_id=1, source_target_pairs={{0,4},{4,8},{8,12},{12,14},{14,10},{10,6},{6,2},{2,0},{5,1},{9,5},... | collective-permute-start | bytes 1327112 | tf_op jit(solution)/shard_map/ppermute | solution.py:297
  27.2 0.0 collective-permute-done.6.refs_1_
  27.3 2.1 %shard_map.68 = (bf16[96,64,512]{2,1,0:T(8,128)(2,1)}, bf16[102,64,512]{2,1,0:T(8,128)(2,1)S(1)}) custom-call(s32[119]{0:T(128)S(1)} %copy-done.3, bf16[96,64,576]{2,1,0:T(8,128)(2,1)S(1)} %get-tuple-element.36.query, bf16[576,128]{1,0:T(8,128)(2,1)S(1)} %fusion.own, ...), custom_call_target="tpu_custom_call", output_to_operand_aliasing={{0}: (6, {})} | custom-call | flops 3422552064 | bytes 7864320 | tf_op jit(solution)/shard_map/pallas_call | solution.py:237
  29.4 0.8 %collective-permute-done.5.refs_0_ = bf16[576,384]{1,0:T(8,128)(2,1)S(1)} collective-permute-done((bf16[576,384]{1,0:T(8,128)(2,1)S(1)}, bf16[576,384]{1,0:T(8,128)(2,1)S(1)}, u32[]{:S(2)}, u32[]{:S(2)}) %collective-permute-start.5) | collective-permute-done | bytes 442400 | tf_op jit(solution)/shard_map/ppermute | solution.py:297
  30.2 0.0 collective-permute-start.10
  30.2 1.6 %collective-permute-start.9 = (bf16[576,384]{1,0:T(8,128)(2,1)S(1)}, bf16[576,384]{1,0:T(8,128)(2,1)S(1)}, u32[]{:S(2)}, u32[]{:S(2)}) collective-permute-start(bf16[576,384]{1,0:T(8,128)(2,1)S(1)} %collective-permute-done.5.refs_0_), channel_id=1, source_target_pairs={{0,4},{4,8},{8,12},{12,14},{14,10},{10,6},{6,2},{2,0},{5,1},{9,5},... | collective-permute-start | bytes 1327112 | tf_op jit(solution)/shard_map/ppermute | solution.py:297
  31.8 0.0 collective-permute-done.12.refs_1_
  31.8 2.0 %shard_map.69 = (bf16[96,64,512]{2,1,0:T(8,128)(2,1)}, bf16[102,64,512]{2,1,0:T(8,128)(2,1)S(1)}) custom-call(s32[119]{0:T(128)S(1)} %copy-done.3, bf16[96,64,576]{2,1,0:T(8,128)(2,1)S(1)} %get-tuple-element.36.query, bf16[576,128]{1,0:T(8,128)(2,1)S(1)} %fusion.own, ...), custom_call_target="tpu_custom_call", output_to_operand_aliasing={{0}: (6, {})} | custom-call | flops 3422552064 | bytes 7864320 | tf_op jit(solution)/shard_map/pallas_call | solution.py:237
  33.8 1.1 %collective-permute-done.11.refs_0_ = bf16[576,384]{1,0:T(8,128)(2,1)S(1)} collective-permute-done((bf16[576,384]{1,0:T(8,128)(2,1)S(1)}, bf16[576,384]{1,0:T(8,128)(2,1)S(1)}, u32[]{:S(2)}, u32[]{:S(2)}) %collective-permute-start.11) | collective-permute-done | bytes 442400 | tf_op jit(solution)/shard_map/ppermute | solution.py:297
  34.9 0.0 collective-permute-start.14
  34.9 0.0 collective-permute-done.10.refs_1_
  34.9 3.0 %shard_map.70 = (bf16[96,64,512]{2,1,0:T(8,128)(2,1)}, bf16[102,64,512]{2,1,0:T(8,128)(2,1)S(1)}) custom-call(s32[119]{0:T(128)S(1)} %copy-done.3, bf16[96,64,576]{2,1,0:T(8,128)(2,1)S(1)} %get-tuple-element.36.query, bf16[576,128]{1,0:T(8,128)(2,1)S(1)} %fusion.own, ...), custom_call_target="tpu_custom_call", output_to_operand_aliasing={{0}: (6, {})} | custom-call | flops 3422552064 | bytes 7864320 | tf_op jit(solution)/shard_map/pallas_call | solution.py:237
  37.9 1.7 %collective-permute-done.9.refs_0_ = bf16[576,384]{1,0:T(8,128)(2,1)S(1)} collective-permute-done((bf16[576,384]{1,0:T(8,128)(2,1)S(1)}, bf16[576,384]{1,0:T(8,128)(2,1)S(1)}, u32[]{:S(2)}, u32[]{:S(2)}) %collective-permute-start.9) | collective-permute-done | bytes 442400 | tf_op jit(solution)/shard_map/ppermute | solution.py:297
  39.6 0.0 collective-permute-start.13
  39.6 0.0 collective-permute-done.14.refs_1_
  39.6 3.2 %shard_map.71 = (bf16[96,64,512]{2,1,0:T(8,128)(2,1)}, bf16[102,64,512]{2,1,0:T(8,128)(2,1)S(1)}) custom-call(s32[119]{0:T(128)S(1)} %copy-done.3, bf16[96,64,576]{2,1,0:T(8,128)(2,1)S(1)} %get-tuple-element.36.query, bf16[576,128]{1,0:T(8,128)(2,1)S(1)} %fusion.own, ...), custom_call_target="tpu_custom_call", output_to_operand_aliasing={{0}: (6, {})} | custom-call | flops 3422552064 | bytes 7864320 | tf_op jit(solution)/shard_map/pallas_call | solution.py:237
  42.9 0.0 collective-permute-done.13.refs_1_
  42.9 0.0 copy-start.1
  42.9 2.8 %shard_map.72 = bf16[96,64,512]{2,1,0:T(8,128)(2,1)} custom-call(s32[119]{0:T(128)S(1)} %copy-done.3, bf16[96,64,576]{2,1,0:T(8,128)(2,1)S(1)} %get-tuple-element.36.query, bf16[576,128]{1,0:T(8,128)(2,1)S(1)} %fusion.own, bf16[576,384]{1,0:T(8,128)(2,1)S(1)} %collective-permute-done.9.refs_0_, ...), custom_call_target="tpu_custom_call", output_to_operand_aliasing={{}: (6, {})} | custom-call | flops 3422552064 | bytes 7864320 | tf_op jit(solution)/shard_map/pallas_call | solution.py:237
  45.7 0.0 copy-done.1
Async XLA Ops:
  0.0 9.5 %copy-start = (bf16[96,576]{1,0:T(8,128)(2,1)S(1)}, bf16[96,576]{1,0:T(8,128)(2,1)}, u32[]{:S(2)}) copy-start(bf16[96,576]{1,0:T(8,128)(2,1)} %param.8) | copy-start | bytes 331780
  0.0 3.7 %collective-permute-start = (bf16[576,384]{1,0:T(8,128)(2,1)}, bf16[576,384]{1,0:T(8,128)(2,1)S(1)}, u32[]{:S(2)}, u32[]{:S(2)}) collective-permute-start(bf16[576,384]{1,0:T(8,128)(2,1)} %bitcast.7), channel_id=1, source_target_pairs={{0,1},{1,0},{2,3},{3,2},{4,5},{5,4},{6,7},{7,6},{8,9},{9,8},{10,11... | collective-permute-start | bytes 1327112 | tf_op jit(solution)/shard_map/ppermute | solution.py:276
  0.5 9.1 %collective-permute-start.1 = (bf16[576,384]{1,0:T(8,128)(2,1)}, bf16[576,384]{1,0:T(8,128)(2,1)S(1)}, u32[]{:S(2)}, u32[]{:S(2)}) collective-permute-start(bf16[576,384]{1,0:T(8,128)(2,1)} %bitcast.8), channel_id=1, source_target_pairs={{0,4},{4,8},{8,12},{12,14},{14,10},{10,6},{6,2},{2,0},{5,1},{9,5},... | collective-permute-start | bytes 1327112 | tf_op jit(solution)/shard_map/ppermute | solution.py:297
  7.6 10.0 %copy-start.3 = (s32[119]{0:T(128)S(1)}, s32[119]{0:T(128)}, u32[]{:S(2)}) copy-start(s32[119]{0:T(128)} %get-tuple-element.35.plan) | copy-start | bytes 1432
  7.6 8.4 %collective-permute-start.4 = (bf16[576,384]{1,0:T(8,128)(2,1)S(1)}, bf16[576,384]{1,0:T(8,128)(2,1)S(1)}, u32[]{:S(2)}, u32[]{:S(2)}) collective-permute-start(bf16[576,384]{1,0:T(8,128)(2,1)S(1)} %get-tuple-element.37.refs_1_), channel_id=1, source_target_pairs={{0,4},{4,8},{8,12},{12,14},{14,10},{10,6},{6,2},{2,0},{5,1},{9,5},... | collective-permute-start | bytes 1327112 | tf_op jit(solution)/shard_map/ppermute | solution.py:297
  9.5 8.0 %collective-permute-start.3 = (bf16[576,384]{1,0:T(8,128)(2,1)S(1)}, bf16[576,384]{1,0:T(8,128)(2,1)S(1)}, u32[]{:S(2)}, u32[]{:S(2)}) collective-permute-start(bf16[576,384]{1,0:T(8,128)(2,1)S(1)} %collective-permute-done.1.refs_0_), channel_id=1, source_target_pairs={{0,1},{1,0},{2,3},{3,2},{4,5},{5,4},{6,7},{7,6},{8,9},{9,8},{10,11... | collective-permute-start | bytes 1327112 | tf_op jit(solution)/shard_map/ppermute | solution.py:303
  9.8 10.9 %collective-permute-start.2 = (bf16[576,384]{1,0:T(8,128)(2,1)S(1)}, bf16[576,384]{1,0:T(8,128)(2,1)S(1)}, u32[]{:S(2)}, u32[]{:S(2)}) collective-permute-start(bf16[576,384]{1,0:T(8,128)(2,1)S(1)} %collective-permute-done.1.refs_0_), channel_id=1, source_target_pairs={{0,4},{4,8},{8,12},{12,14},{14,10},{10,6},{6,2},{2,0},{5,1},{9,5},... | collective-permute-start | bytes 1327112 | tf_op jit(solution)/shard_map/ppermute | solution.py:297
  11.9 0.6 %copy-start.2 = (s32[119]{0:T(128)S(1)}, s32[119]{0:T(128)}, u32[]{:S(2)}) copy-start(s32[119]{0:T(128)} %get-tuple-element.35.plan) | copy-start | bytes 1432
  15.9 6.3 %collective-permute-start.8 = (bf16[576,384]{1,0:T(8,128)(2,1)S(1)}, bf16[576,384]{1,0:T(8,128)(2,1)S(1)}, u32[]{:S(2)}, u32[]{:S(2)}) collective-permute-start(bf16[576,384]{1,0:T(8,128)(2,1)S(1)} %collective-permute-done.4.refs_0_), channel_id=1, source_target_pairs={{0,1},{1,0},{2,3},{3,2},{4,5},{5,4},{6,7},{7,6},{8,9},{9,8},{10,11... | collective-permute-start | bytes 1327112 | tf_op jit(solution)/shard_map/ppermute | solution.py:303
  15.9 9.5 %collective-permute-start.7 = (bf16[576,384]{1,0:T(8,128)(2,1)S(1)}, bf16[576,384]{1,0:T(8,128)(2,1)S(1)}, u32[]{:S(2)}, u32[]{:S(2)}) collective-permute-start(bf16[576,384]{1,0:T(8,128)(2,1)S(1)} %collective-permute-done.4.refs_0_), channel_id=1, source_target_pairs={{0,4},{4,8},{8,12},{12,14},{14,10},{10,6},{6,2},{2,0},{5,1},{9,5},... | collective-permute-start | bytes 1327112 | tf_op jit(solution)/shard_map/ppermute | solution.py:297
  20.7 6.6 %collective-permute-start.6 = (bf16[576,384]{1,0:T(8,128)(2,1)S(1)}, bf16[576,384]{1,0:T(8,128)(2,1)S(1)}, u32[]{:S(2)}, u32[]{:S(2)}) collective-permute-start(bf16[576,384]{1,0:T(8,128)(2,1)S(1)} %collective-permute-done.2.refs_0_), channel_id=1, source_target_pairs={{0,1},{1,0},{2,3},{3,2},{4,5},{5,4},{6,7},{7,6},{8,9},{9,8},{10,11... | collective-permute-start | bytes 1327112 | tf_op jit(solution)/shard_map/ppermute | solution.py:303
  20.7 9.5 %collective-permute-start.5 = (bf16[576,384]{1,0:T(8,128)(2,1)S(1)}, bf16[576,384]{1,0:T(8,128)(2,1)S(1)}, u32[]{:S(2)}, u32[]{:S(2)}) collective-permute-start(bf16[576,384]{1,0:T(8,128)(2,1)S(1)} %collective-permute-done.2.refs_0_), channel_id=1, source_target_pairs={{0,4},{4,8},{8,12},{12,14},{14,10},{10,6},{6,2},{2,0},{5,1},{9,5},... | collective-permute-start | bytes 1327112 | tf_op jit(solution)/shard_map/ppermute | solution.py:297
  25.4 6.4 %collective-permute-start.12 = (bf16[576,384]{1,0:T(8,128)(2,1)S(1)}, bf16[576,384]{1,0:T(8,128)(2,1)S(1)}, u32[]{:S(2)}, u32[]{:S(2)}) collective-permute-start(bf16[576,384]{1,0:T(8,128)(2,1)S(1)} %collective-permute-done.7.refs_0_), channel_id=1, source_target_pairs={{0,1},{1,0},{2,3},{3,2},{4,5},{5,4},{6,7},{7,6},{8,9},{9,8},{10,11... | collective-permute-start | bytes 1327112 | tf_op jit(solution)/shard_map/ppermute | solution.py:303
  25.5 9.4 %collective-permute-start.11 = (bf16[576,384]{1,0:T(8,128)(2,1)S(1)}, bf16[576,384]{1,0:T(8,128)(2,1)S(1)}, u32[]{:S(2)}, u32[]{:S(2)}) collective-permute-start(bf16[576,384]{1,0:T(8,128)(2,1)S(1)} %collective-permute-done.7.refs_0_), channel_id=1, source_target_pairs={{0,4},{4,8},{8,12},{12,14},{14,10},{10,6},{6,2},{2,0},{5,1},{9,5},... | collective-permute-start | bytes 1327112 | tf_op jit(solution)/shard_map/ppermute | solution.py:297
  30.2 4.7 %collective-permute-start.10 = (bf16[576,384]{1,0:T(8,128)(2,1)S(1)}, bf16[576,384]{1,0:T(8,128)(2,1)S(1)}, u32[]{:S(2)}, u32[]{:S(2)}) collective-permute-start(bf16[576,384]{1,0:T(8,128)(2,1)S(1)} %collective-permute-done.5.refs_0_), channel_id=1, source_target_pairs={{0,1},{1,0},{2,3},{3,2},{4,5},{5,4},{6,7},{7,6},{8,9},{9,8},{10,11... | collective-permute-start | bytes 1327112 | tf_op jit(solution)/shard_map/ppermute | solution.py:303
  30.2 9.5 %collective-permute-start.9 = (bf16[576,384]{1,0:T(8,128)(2,1)S(1)}, bf16[576,384]{1,0:T(8,128)(2,1)S(1)}, u32[]{:S(2)}, u32[]{:S(2)}) collective-permute-start(bf16[576,384]{1,0:T(8,128)(2,1)S(1)} %collective-permute-done.5.refs_0_), channel_id=1, source_target_pairs={{0,4},{4,8},{8,12},{12,14},{14,10},{10,6},{6,2},{2,0},{5,1},{9,5},... | collective-permute-start | bytes 1327112 | tf_op jit(solution)/shard_map/ppermute | solution.py:297
  34.9 4.7 %collective-permute-start.14 = (bf16[576,384]{1,0:T(8,128)(2,1)S(1)}, bf16[576,384]{1,0:T(8,128)(2,1)S(1)}, u32[]{:S(2)}, u32[]{:S(2)}) collective-permute-start(bf16[576,384]{1,0:T(8,128)(2,1)S(1)} %collective-permute-done.11.refs_0_), channel_id=1, source_target_pairs={{0,1},{1,0},{2,3},{3,2},{4,5},{5,4},{6,7},{7,6},{8,9},{9,8},{10,11... | collective-permute-start | bytes 1327112 | tf_op jit(solution)/shard_map/ppermute | solution.py:303
  39.6 3.2 %collective-permute-start.13 = (bf16[576,384]{1,0:T(8,128)(2,1)S(1)}, bf16[576,384]{1,0:T(8,128)(2,1)S(1)}, u32[]{:S(2)}, u32[]{:S(2)}) collective-permute-start(bf16[576,384]{1,0:T(8,128)(2,1)S(1)} %collective-permute-done.9.refs_0_), channel_id=1, source_target_pairs={{0,1},{1,0},{2,3},{3,2},{4,5},{5,4},{6,7},{7,6},{8,9},{9,8},{10,11... | collective-permute-start | bytes 1327112 | tf_op jit(solution)/shard_map/ppermute | solution.py:303
  42.9 2.8 %copy-start.1 = (bf16[96,576]{1,0:T(8,128)(2,1)S(1)}, bf16[96,576]{1,0:T(8,128)(2,1)}, u32[]{:S(2)}) copy-start(bf16[96,576]{1,0:T(8,128)(2,1)} %param.8) | copy-start | bytes 331780

commit v3 on v2

--- a/solution.py
+++ b/solution.py
@@ -12,6 +12,7 @@
 SCALE = 0.07216878364870322
 BLOCK = 6
 COST = 4
+FIRST = 1
 ANY = pl.BlockSpec(memory_space=pl.ANY)
 VMEM = pl.BlockSpec(memory_space=pltpu.VMEM)
 SMEM = pl.BlockSpec(memory_space=pltpu.SMEM)
@@ -31,7 +32,7 @@
 
 
 def prepare_kernel(
-    place_in, parent_in, live_in, query_in, mine_in, _, plan, query, mine, __, place, parent, live, slots, names, starts, sem
+    place_in, parent_in, live_in, query_in, mine_in, plan, query, mine, place, parent, live, slots, names, starts, sem
 ):
     rows = parent.shape[1]
     parents = place.shape[0]
@@ -103,7 +104,7 @@
         copy.wait()
 
 
-def prepare(place, parent, live, query, mine, other):
+def prepare(place, parent, live, query, mine):
     rows, parents = parent.shape[1], place.shape[0]
     return pl.pallas_call(
         prepare_kernel,
@@ -111,10 +112,9 @@
             jax.ShapeDtypeStruct((parents + 1 + rows + BLOCK,), jnp.int32),
             pltpu.VMEM(query.shape, query.dtype),
             pltpu.VMEM(mine.shape, mine.dtype),
-            pltpu.VMEM(other.shape, other.dtype),
         ),
-        in_specs=[ANY] * 5 + [VMEM],
-        out_specs=(SMEM, VMEM, VMEM, VMEM),
+        in_specs=[ANY] * 5,
+        out_specs=(SMEM, VMEM, VMEM),
         scratch_shapes=[
             pltpu.SMEM(place.shape, jnp.int32),
             pltpu.SMEM(parent.shape, jnp.int32),
@@ -124,10 +124,9 @@
             pltpu.SMEM((parents + 1,), jnp.int32),
             pltpu.SemaphoreType.DMA((5,)),
         ],
-        input_output_aliases={5: 3},
-        compiler_params=pltpu.CompilerParams(vmem_limit_bytes=46 * 1024 * 1024),
+        compiler_params=pltpu.CompilerParams(vmem_limit_bytes=48 * 1024 * 1024),
         cost_estimate=pl.CostEstimate(flops=0, bytes_accessed=2 * query.size * 2, transcendentals=0),
-    )(place, parent, live, query, mine, other)
+    )(place, parent, live, query, mine)
 
 
 def attend_kernel(first, before, last, arrays, plan, query, own, *refs):
@@ -225,7 +224,7 @@
             pltpu.make_async_copy(zeros, out.at[0], out_sem).wait()
 
 
-def attend(plan, first, query, own, slots, before=0, done=None, out=None, last=False):
+def attend(plan, first, query, own, slots, before=0, done=None, out=None, last=False, cost=COST):
     rows, heads, depth = query.shape
     count = len(slots)
     prefix = slots[0].shape[-1]
@@ -250,9 +249,9 @@
         input_output_aliases={len(operands) - 1: 0} if before else {},
         compiler_params=pltpu.CompilerParams(vmem_limit_bytes=16 * 1024 * 1024),
         cost_estimate=pl.CostEstimate(
-            flops=COST * 2 * work * width * (depth + LAT),
-            bytes_accessed=COST * (count * depth * width * 2 + work * LAT * 2),
-            transcendentals=COST * work * width,
+            flops=cost * 2 * work * width * (depth + LAT),
+            bytes_accessed=cost * (count * depth * width * 2 + work * LAT * 2),
+            transcendentals=cost * work * width,
         ),
     )(*operands)
 
@@ -274,9 +273,8 @@
 
     mine = jnp.swapaxes(parent_cache[0], 0, 1)
     other = lax.ppermute(mine, "node", across)
-    plan, query, kept, other = prepare(
-        parent_place, jnp.swapaxes(child_parent, 0, 1), live_rows, child_query, mine, other
-    )
+    other, place = lax.optimization_barrier((other, parent_place))
+    plan, query, kept = prepare(place, jnp.swapaxes(child_parent, 0, 1), live_rows, child_query, mine)
     padded = -(-rows // 128) * 128
     pick = jnp.arange(rows)[:, None] == jnp.arange(padded)[None, :]
     own = lax.dot_general(
@@ -290,11 +288,13 @@
     def work(phase, last=False):
         nonlocal first, result
         before = 2 if first else 0
-        result = attend(plan, first, query, own, phases[phase], before, result[1], result[0], last)
+        result = attend(plan, first, query, own, phases[phase], before, result[1], result[0], last, COST if first else FIRST)
         first += 2
 
     for i in range(1, chips):
         a = forward = lax.ppermute(sent[i - 1], "node", along)
+        if i == 1:
+            forward, plan = lax.optimization_barrier((a, plan))
         if i >= 2:
             work(i - 2)
             forward, done = lax.optimization_barrier((a, result[1]))

time: 46.5 us -> 45.5 us (0.978)
  waiting for transfers between devices: 6.38 us -> 2.78 us
  Pallas kernels: 24.2 us -> 26.1 us
    ppermute x7, waiting for transfers between devices: 6.36 us -> 2.76 us  [shards(): a = forward = lax.ppermute(sent[i - 1], 'node', along)]
    pallas_call x8, Pallas kernels: 20.4 us -> 22.2 us  [attend(): pl.pallas_call(functools.partial(attend_kernel, first, before, last, coun...]
  transfers between devices with their start and end apart: 15 -> 15, of which waited for: 7 -> 2; matrix products, arithmetic and copies ran while one was open for 1% -> 1% of each run, Pallas kernels for 47% -> 52%
where the time goes in v3:
time: 45.5 us; the launch traced here: 44.6 us
  Pallas kernels  26.1 us (57%)
  starting transfers between devices  13.9 us (31%)
  waiting for transfers between devices  2.78 us (6%)
  between operations  1.01 us (2%)
  local copies, waits for them, and re-layouts  0.66 us (1%)
    pallas_call x8, Pallas kernels, attend(): pl.pallas_call(functools.partial(attend_kernel, first, before, last, coun...  22.2 us
    ppermute x7, starting transfers between devices, shards(): a = forward = lax.ppermute(sent[i - 1], 'node', along)  12.9 us
    pallas_call x1, Pallas kernels, prepare(): pl.pallas_call(prepare_kernel, out_shape=(jax.ShapeDtypeStruct((parents +...  3.81 us
    ppermute x7, waiting for transfers between devices, shards(): a = forward = lax.ppermute(sent[i - 1], 'node', along)  2.76 us
  transfers between devices with their start and end apart: 15, of which 2 were waited for; matrix products, arithmetic and copies ran while one was open for 1% of the time, Pallas kernels for 52%

profile of v3, /device:TPU:0, one launch (start us, length us, event | category | flops | bytes accessed | tf_op | source)
XLA Modules:
  0.0 44.6 jit_solution(18009445900325298788)
XLA Ops:
  0.0 0.0 copy-start
  0.0 0.5 %collective-permute-start.1 = (bf16[576,384]{1,0:T(8,128)(2,1)}, bf16[576,384]{1,0:T(8,128)(2,1)S(1)}, u32[]{:S(2)}, u32[]{:S(2)}) collective-permute-start(bf16[576,384]{1,0:T(8,128)(2,1)} %bitcast.7), channel_id=1, source_target_pairs={{0,1},{1,0},{2,3},{3,2},{4,5},{5,4},{6,7},{7,6},{8,9},{9,8},{10,11... | collective-permute-start | bytes 1327112 | tf_op jit(solution)/shard_map/ppermute | solution.py:275
  0.5 2.6 %collective-permute-start = (bf16[576,384]{1,0:T(8,128)(2,1)}, bf16[576,384]{1,0:T(8,128)(2,1)S(1)}, u32[]{:S(2)}, u32[]{:S(2)}) collective-permute-start(bf16[576,384]{1,0:T(8,128)(2,1)} %bitcast.8), channel_id=1, source_target_pairs={{0,4},{4,8},{8,12},{12,14},{14,10},{10,6},{6,2},{2,0},{5,1},{9,5},... | collective-permute-start | bytes 1327112 | tf_op jit(solution)/shard_map/ppermute | solution.py:295
  3.7 0.0 collective-permute-done.1.refs_1_
  3.7 1.6 %collective-permute-start.4 = (bf16[576,384]{1,0:T(8,128)(2,1)S(1)}, bf16[576,384]{1,0:T(8,128)(2,1)S(1)}, u32[]{:S(2)}, u32[]{:S(2)}) collective-permute-start(bf16[576,384]{1,0:T(8,128)(2,1)S(1)} %collective-permute-done.1.refs_1_), channel_id=1, source_target_pairs={{0,4},{4,8},{8,12},{12,14},{14,10},{10,6},{6,2},{2,0},{5,1},{9,5},... | collective-permute-start | bytes 1327112 | tf_op jit(solution)/shard_map/ppermute | solution.py:295
  5.4 3.8 %shard_map.64 = (s32[119]{0:T(128)}, bf16[96,64,576]{2,1,0:T(8,128)(2,1)S(1)}, bf16[576,384]{1,0:T(8,128)(2,1)S(1)}) custom-call(s32[16]{0:T(128)} %place_in, s32[1,96]{1,0:T(1,128)} %bitcast.10, s32[1]{0:T(128)S(6)} %copy.21.live_in, bf16[96,64,576]{2,1,0:T(8,128)(2,1)} %query_in.1, bf16[576,384]{1,0:T(8,128)(2,1)} %bitcast.9), custom_call_target="tpu_custom_call" | custom-call | bytes 14155776 | tf_op jit(solution)/shard_map/pallas_call | solution.py:109
  9.2 0.3 collective-permute-done.refs_0_
  9.5 0.0 collective-permute-start.3
  9.5 2.1 %collective-permute-start.2 = (bf16[576,384]{1,0:T(8,128)(2,1)S(1)}, bf16[576,384]{1,0:T(8,128)(2,1)S(1)}, u32[]{:S(2)}, u32[]{:S(2)}) collective-permute-start(bf16[576,384]{1,0:T(8,128)(2,1)S(1)} %collective-permute-done.refs_0_), channel_id=1, source_target_pairs={{0,4},{4,8},{8,12},{12,14},{14,10},{10,6},{6,2},{2,0},{5,1},{9,5},... | collective-permute-start | bytes 1327112 | tf_op jit(solution)/shard_map/ppermute | solution.py:295
  11.6 0.0 copy-done
  11.6 0.2 fusion.own
  11.8 0.0 copy-start.2
  11.9 0.6 %copy-done.2 = s32[119]{0:T(128)S(1)} copy-done((s32[119]{0:T(128)S(1)}, s32[119]{0:T(128)}, u32[]{:S(2)}) %copy-start.2) | copy-done | bytes 500
  12.5 3.0 %shard_map.65 = (bf16[96,64,512]{2,1,0:T(8,128)(2,1)}, bf16[102,64,512]{2,1,0:T(8,128)(2,1)S(1)}) custom-call(s32[119]{0:T(128)S(1)} %copy-done.2, bf16[96,64,576]{2,1,0:T(8,128)(2,1)S(1)} %get-tuple-element.41.query, bf16[576,128]{1,0:T(8,128)(2,1)S(1)} %fusion.own, bf16[576,384]{1,0:T(8,128)(2,1)S(1)} %get-tuple-element.44.refs_0_, ...), custom_call_target="tpu_custom_call" | custom-call | flops 855638016 | bytes 1966080 | tf_op jit(solution)/shard_map/pallas_call | solution.py:236
  15.5 0.0 collective-permute-done.4.refs_0_
  15.5 0.1 collective-permute-start.8
  15.6 1.8 %collective-permute-start.7 = (bf16[576,384]{1,0:T(8,128)(2,1)S(1)}, bf16[576,384]{1,0:T(8,128)(2,1)S(1)}, u32[]{:S(2)}, u32[]{:S(2)}) collective-permute-start(bf16[576,384]{1,0:T(8,128)(2,1)S(1)} %collective-permute-done.4.refs_0_), channel_id=1, source_target_pairs={{0,4},{4,8},{8,12},{12,14},{14,10},{10,6},{6,2},{2,0},{5,1},{9,5},... | collective-permute-start | bytes 1327112 | tf_op jit(solution)/shard_map/ppermute | solution.py:295
  17.3 0.0 collective-permute-done.3.refs_1_
  17.3 2.1 %shard_map.66 = (bf16[96,64,512]{2,1,0:T(8,128)(2,1)}, bf16[102,64,512]{2,1,0:T(8,128)(2,1)S(1)}) custom-call(s32[119]{0:T(128)S(1)} %copy-done.2, bf16[96,64,576]{2,1,0:T(8,128)(2,1)S(1)} %get-tuple-element.41.query, bf16[576,128]{1,0:T(8,128)(2,1)S(1)} %fusion.own, ...), custom_call_target="tpu_custom_call", output_to_operand_aliasing={{0}: (6, {})} | custom-call | flops 3422552064 | bytes 7864320 | tf_op jit(solution)/shard_map/pallas_call | solution.py:236
  19.4 0.0 collective-permute-done.2.refs_0_
  19.4 0.1 collective-permute-start.6
  19.5 2.8 %collective-permute-start.5 = (bf16[576,384]{1,0:T(8,128)(2,1)S(1)}, bf16[576,384]{1,0:T(8,128)(2,1)S(1)}, u32[]{:S(2)}, u32[]{:S(2)}) collective-permute-start(bf16[576,384]{1,0:T(8,128)(2,1)S(1)} %collective-permute-done.2.refs_0_), channel_id=1, source_target_pairs={{0,4},{4,8},{8,12},{12,14},{14,10},{10,6},{6,2},{2,0},{5,1},{9,5},... | collective-permute-start | bytes 1327112 | tf_op jit(solution)/shard_map/ppermute | solution.py:295
  22.3 0.0 collective-permute-done.8.refs_1_
  22.3 3.0 %shard_map.67 = (bf16[96,64,512]{2,1,0:T(8,128)(2,1)}, bf16[102,64,512]{2,1,0:T(8,128)(2,1)S(1)}) custom-call(s32[119]{0:T(128)S(1)} %copy-done.2, bf16[96,64,576]{2,1,0:T(8,128)(2,1)S(1)} %get-tuple-element.41.query, bf16[576,128]{1,0:T(8,128)(2,1)S(1)} %fusion.own, ...), custom_call_target="tpu_custom_call", output_to_operand_aliasing={{0}: (6, {})} | custom-call | flops 3422552064 | bytes 7864320 | tf_op jit(solution)/shard_map/pallas_call | solution.py:236
  25.3 0.0 collective-permute-done.7.refs_0_
  25.4 0.1 collective-permute-start.12
  25.4 0.4 collective-permute-start.11
  25.8 0.0 collective-permute-done.6.refs_1_
  25.8 3.1 %shard_map.68 = (bf16[96,64,512]{2,1,0:T(8,128)(2,1)}, bf16[102,64,512]{2,1,0:T(8,128)(2,1)S(1)}) custom-call(s32[119]{0:T(128)S(1)} %copy-done.2, bf16[96,64,576]{2,1,0:T(8,128)(2,1)S(1)} %get-tuple-element.41.query, bf16[576,128]{1,0:T(8,128)(2,1)S(1)} %fusion.own, ...), custom_call_target="tpu_custom_call", output_to_operand_aliasing={{0}: (6, {})} | custom-call | flops 3422552064 | bytes 7864320 | tf_op jit(solution)/shard_map/pallas_call | solution.py:236
  28.9 0.0 collective-permute-done.5.refs_0_
  28.9 0.2 collective-permute-start.10
  29.1 1.7 %collective-permute-start.9 = (bf16[576,384]{1,0:T(8,128)(2,1)S(1)}, bf16[576,384]{1,0:T(8,128)(2,1)S(1)}, u32[]{:S(2)}, u32[]{:S(2)}) collective-permute-start(bf16[576,384]{1,0:T(8,128)(2,1)S(1)} %collective-permute-done.5.refs_0_), channel_id=1, source_target_pairs={{0,4},{4,8},{8,12},{12,14},{14,10},{10,6},{6,2},{2,0},{5,1},{9,5},... | collective-permute-start | bytes 1327112 | tf_op jit(solution)/shard_map/ppermute | solution.py:295
  30.8 0.0 collective-permute-done.12.refs_1_
  30.8 3.1 %shard_map.69 = (bf16[96,64,512]{2,1,0:T(8,128)(2,1)}, bf16[102,64,512]{2,1,0:T(8,128)(2,1)S(1)}) custom-call(s32[119]{0:T(128)S(1)} %copy-done.2, bf16[96,64,576]{2,1,0:T(8,128)(2,1)S(1)} %get-tuple-element.41.query, bf16[576,128]{1,0:T(8,128)(2,1)S(1)} %fusion.own, ...), custom_call_target="tpu_custom_call", output_to_operand_aliasing={{0}: (6, {})} | custom-call | flops 3422552064 | bytes 7864320 | tf_op jit(solution)/shard_map/pallas_call | solution.py:236
  33.9 0.0 collective-permute-done.11.refs_0_
  33.9 0.1 collective-permute-start.14
  34.0 0.0 collective-permute-done.10.refs_1_
  34.0 2.1 %shard_map.70 = (bf16[96,64,512]{2,1,0:T(8,128)(2,1)}, bf16[102,64,512]{2,1,0:T(8,128)(2,1)S(1)}) custom-call(s32[119]{0:T(128)S(1)} %copy-done.2, bf16[96,64,576]{2,1,0:T(8,128)(2,1)S(1)} %get-tuple-element.41.query, bf16[576,128]{1,0:T(8,128)(2,1)S(1)} %fusion.own, ...), custom_call_target="tpu_custom_call", output_to_operand_aliasing={{0}: (6, {})} | custom-call | flops 3422552064 | bytes 7864320 | tf_op jit(solution)/shard_map/pallas_call | solution.py:236
  36.1 2.4 %collective-permute-done.9.refs_0_ = bf16[576,384]{1,0:T(8,128)(2,1)S(1)} collective-permute-done((bf16[576,384]{1,0:T(8,128)(2,1)S(1)}, bf16[576,384]{1,0:T(8,128)(2,1)S(1)}, u32[]{:S(2)}, u32[]{:S(2)}) %collective-permute-start.9) | collective-permute-done | bytes 442400 | tf_op jit(solution)/shard_map/ppermute | solution.py:295
  38.5 0.0 collective-permute-start.13
  38.5 0.0 collective-permute-done.14.refs_1_
  38.5 3.1 %shard_map.71 = (bf16[96,64,512]{2,1,0:T(8,128)(2,1)}, bf16[102,64,512]{2,1,0:T(8,128)(2,1)S(1)}) custom-call(s32[119]{0:T(128)S(1)} %copy-done.2, bf16[96,64,576]{2,1,0:T(8,128)(2,1)S(1)} %get-tuple-element.41.query, bf16[576,128]{1,0:T(8,128)(2,1)S(1)} %fusion.own, ...), custom_call_target="tpu_custom_call", output_to_operand_aliasing={{0}: (6, {})} | custom-call | flops 3422552064 | bytes 7864320 | tf_op jit(solution)/shard_map/pallas_call | solution.py:236
  41.7 0.0 collective-permute-done.13.refs_1_
  41.7 0.0 copy-start.1
  41.7 2.8 %shard_map.72 = bf16[96,64,512]{2,1,0:T(8,128)(2,1)} custom-call(s32[119]{0:T(128)S(1)} %copy-done.2, bf16[96,64,576]{2,1,0:T(8,128)(2,1)S(1)} %get-tuple-element.41.query, bf16[576,128]{1,0:T(8,128)(2,1)S(1)} %fusion.own, bf16[576,384]{1,0:T(8,128)(2,1)S(1)} %collective-permute-done.9.refs_0_, ...), custom_call_target="tpu_custom_call", output_to_operand_aliasing={{}: (6, {})} | custom-call | flops 3422552064 | bytes 7864320 | tf_op jit(solution)/shard_map/pallas_call | solution.py:236
  44.5 0.0 copy-done.1
Async XLA Ops:
  0.0 11.6 %copy-start = (bf16[96,576]{1,0:T(8,128)(2,1)S(1)}, bf16[96,576]{1,0:T(8,128)(2,1)}, u32[]{:S(2)}) copy-start(bf16[96,576]{1,0:T(8,128)(2,1)} %param.8) | copy-start | bytes 331780
  0.0 3.7 %collective-permute-start.1 = (bf16[576,384]{1,0:T(8,128)(2,1)}, bf16[576,384]{1,0:T(8,128)(2,1)S(1)}, u32[]{:S(2)}, u32[]{:S(2)}) collective-permute-start(bf16[576,384]{1,0:T(8,128)(2,1)} %bitcast.7), channel_id=1, source_target_pairs={{0,1},{1,0},{2,3},{3,2},{4,5},{5,4},{6,7},{7,6},{8,9},{9,8},{10,11... | collective-permute-start | bytes 1327112 | tf_op jit(solution)/shard_map/ppermute | solution.py:275
  0.5 9.1 %collective-permute-start = (bf16[576,384]{1,0:T(8,128)(2,1)}, bf16[576,384]{1,0:T(8,128)(2,1)S(1)}, u32[]{:S(2)}, u32[]{:S(2)}) collective-permute-start(bf16[576,384]{1,0:T(8,128)(2,1)} %bitcast.8), channel_id=1, source_target_pairs={{0,4},{4,8},{8,12},{12,14},{14,10},{10,6},{6,2},{2,0},{5,1},{9,5},... | collective-permute-start | bytes 1327112 | tf_op jit(solution)/shard_map/ppermute | solution.py:295
  3.7 11.8 %collective-permute-start.4 = (bf16[576,384]{1,0:T(8,128)(2,1)S(1)}, bf16[576,384]{1,0:T(8,128)(2,1)S(1)}, u32[]{:S(2)}, u32[]{:S(2)}) collective-permute-start(bf16[576,384]{1,0:T(8,128)(2,1)S(1)} %collective-permute-done.1.refs_1_), channel_id=1, source_target_pairs={{0,4},{4,8},{8,12},{12,14},{14,10},{10,6},{6,2},{2,0},{5,1},{9,5},... | collective-permute-start | bytes 1327112 | tf_op jit(solution)/shard_map/ppermute | solution.py:295
  9.5 7.8 %collective-permute-start.3 = (bf16[576,384]{1,0:T(8,128)(2,1)S(1)}, bf16[576,384]{1,0:T(8,128)(2,1)S(1)}, u32[]{:S(2)}, u32[]{:S(2)}) collective-permute-start(bf16[576,384]{1,0:T(8,128)(2,1)S(1)} %collective-permute-done.refs_0_), channel_id=1, source_target_pairs={{0,1},{1,0},{2,3},{3,2},{4,5},{5,4},{6,7},{7,6},{8,9},{9,8},{10,11... | collective-permute-start | bytes 1327112 | tf_op jit(solution)/shard_map/ppermute | solution.py:303
  9.5 9.9 %collective-permute-start.2 = (bf16[576,384]{1,0:T(8,128)(2,1)S(1)}, bf16[576,384]{1,0:T(8,128)(2,1)S(1)}, u32[]{:S(2)}, u32[]{:S(2)}) collective-permute-start(bf16[576,384]{1,0:T(8,128)(2,1)S(1)} %collective-permute-done.refs_0_), channel_id=1, source_target_pairs={{0,4},{4,8},{8,12},{12,14},{14,10},{10,6},{6,2},{2,0},{5,1},{9,5},... | collective-permute-start | bytes 1327112 | tf_op jit(solution)/shard_map/ppermute | solution.py:295
  11.8 0.7 %copy-start.2 = (s32[119]{0:T(128)S(1)}, s32[119]{0:T(128)}, u32[]{:S(2)}) copy-start(s32[119]{0:T(128)} %get-tuple-element.40.plan) | copy-start | bytes 1432
  15.5 6.8 %collective-permute-start.8 = (bf16[576,384]{1,0:T(8,128)(2,1)S(1)}, bf16[576,384]{1,0:T(8,128)(2,1)S(1)}, u32[]{:S(2)}, u32[]{:S(2)}) collective-permute-start(bf16[576,384]{1,0:T(8,128)(2,1)S(1)} %collective-permute-done.4.refs_0_), channel_id=1, source_target_pairs={{0,1},{1,0},{2,3},{3,2},{4,5},{5,4},{6,7},{7,6},{8,9},{9,8},{10,11... | collective-permute-start | bytes 1327112 | tf_op jit(solution)/shard_map/ppermute | solution.py:303
  15.6 9.8 %collective-permute-start.7 = (bf16[576,384]{1,0:T(8,128)(2,1)S(1)}, bf16[576,384]{1,0:T(8,128)(2,1)S(1)}, u32[]{:S(2)}, u32[]{:S(2)}) collective-permute-start(bf16[576,384]{1,0:T(8,128)(2,1)S(1)} %collective-permute-done.4.refs_0_), channel_id=1, source_target_pairs={{0,4},{4,8},{8,12},{12,14},{14,10},{10,6},{6,2},{2,0},{5,1},{9,5},... | collective-permute-start | bytes 1327112 | tf_op jit(solution)/shard_map/ppermute | solution.py:295
  19.4 6.4 %collective-permute-start.6 = (bf16[576,384]{1,0:T(8,128)(2,1)S(1)}, bf16[576,384]{1,0:T(8,128)(2,1)S(1)}, u32[]{:S(2)}, u32[]{:S(2)}) collective-permute-start(bf16[576,384]{1,0:T(8,128)(2,1)S(1)} %collective-permute-done.2.refs_0_), channel_id=1, source_target_pairs={{0,1},{1,0},{2,3},{3,2},{4,5},{5,4},{6,7},{7,6},{8,9},{9,8},{10,11... | collective-permute-start | bytes 1327112 | tf_op jit(solution)/shard_map/ppermute | solution.py:303
  19.5 9.4 %collective-permute-start.5 = (bf16[576,384]{1,0:T(8,128)(2,1)S(1)}, bf16[576,384]{1,0:T(8,128)(2,1)S(1)}, u32[]{:S(2)}, u32[]{:S(2)}) collective-permute-start(bf16[576,384]{1,0:T(8,128)(2,1)S(1)} %collective-permute-done.2.refs_0_), channel_id=1, source_target_pairs={{0,4},{4,8},{8,12},{12,14},{14,10},{10,6},{6,2},{2,0},{5,1},{9,5},... | collective-permute-start | bytes 1327112 | tf_op jit(solution)/shard_map/ppermute | solution.py:295
  25.4 5.4 %collective-permute-start.12 = (bf16[576,384]{1,0:T(8,128)(2,1)S(1)}, bf16[576,384]{1,0:T(8,128)(2,1)S(1)}, u32[]{:S(2)}, u32[]{:S(2)}) collective-permute-start(bf16[576,384]{1,0:T(8,128)(2,1)S(1)} %collective-permute-done.7.refs_0_), channel_id=1, source_target_pairs={{0,1},{1,0},{2,3},{3,2},{4,5},{5,4},{6,7},{7,6},{8,9},{9,8},{10,11... | collective-permute-start | bytes 1327112 | tf_op jit(solution)/shard_map/ppermute | solution.py:303
  25.4 8.5 %collective-permute-start.11 = (bf16[576,384]{1,0:T(8,128)(2,1)S(1)}, bf16[576,384]{1,0:T(8,128)(2,1)S(1)}, u32[]{:S(2)}, u32[]{:S(2)}) collective-permute-start(bf16[576,384]{1,0:T(8,128)(2,1)S(1)} %collective-permute-done.7.refs_0_), channel_id=1, source_target_pairs={{0,4},{4,8},{8,12},{12,14},{14,10},{10,6},{6,2},{2,0},{5,1},{9,5},... | collective-permute-start | bytes 1327112 | tf_op jit(solution)/shard_map/ppermute | solution.py:295
  28.9 5.1 %collective-permute-start.10 = (bf16[576,384]{1,0:T(8,128)(2,1)S(1)}, bf16[576,384]{1,0:T(8,128)(2,1)S(1)}, u32[]{:S(2)}, u32[]{:S(2)}) collective-permute-start(bf16[576,384]{1,0:T(8,128)(2,1)S(1)} %collective-permute-done.5.refs_0_), channel_id=1, source_target_pairs={{0,1},{1,0},{2,3},{3,2},{4,5},{5,4},{6,7},{7,6},{8,9},{9,8},{10,11... | collective-permute-start | bytes 1327112 | tf_op jit(solution)/shard_map/ppermute | solution.py:303
  29.1 9.4 %collective-permute-start.9 = (bf16[576,384]{1,0:T(8,128)(2,1)S(1)}, bf16[576,384]{1,0:T(8,128)(2,1)S(1)}, u32[]{:S(2)}, u32[]{:S(2)}) collective-permute-start(bf16[576,384]{1,0:T(8,128)(2,1)S(1)} %collective-permute-done.5.refs_0_), channel_id=1, source_target_pairs={{0,4},{4,8},{8,12},{12,14},{14,10},{10,6},{6,2},{2,0},{5,1},{9,5},... | collective-permute-start | bytes 1327112 | tf_op jit(solution)/shard_map/ppermute | solution.py:295
  33.9 4.6 %collective-permute-start.14 = (bf16[576,384]{1,0:T(8,128)(2,1)S(1)}, bf16[576,384]{1,0:T(8,128)(2,1)S(1)}, u32[]{:S(2)}, u32[]{:S(2)}) collective-permute-start(bf16[576,384]{1,0:T(8,128)(2,1)S(1)} %collective-permute-done.11.refs_0_), channel_id=1, source_target_pairs={{0,1},{1,0},{2,3},{3,2},{4,5},{5,4},{6,7},{7,6},{8,9},{9,8},{10,11... | collective-permute-start | bytes 1327112 | tf_op jit(solution)/shard_map/ppermute | solution.py:303
  38.5 3.2 %collective-permute-start.13 = (bf16[576,384]{1,0:T(8,128)(2,1)S(1)}, bf16[576,384]{1,0:T(8,128)(2,1)S(1)}, u32[]{:S(2)}, u32[]{:S(2)}) collective-permute-start(bf16[576,384]{1,0:T(8,128)(2,1)S(1)} %collective-permute-done.9.refs_0_), channel_id=1, source_target_pairs={{0,1},{1,0},{2,3},{3,2},{4,5},{5,4},{6,7},{7,6},{8,9},{9,8},{10,11... | collective-permute-start | bytes 1327112 | tf_op jit(solution)/shard_map/ppermute | solution.py:303
  41.7 2.8 %copy-start.1 = (bf16[96,576]{1,0:T(8,128)(2,1)S(1)}, bf16[96,576]{1,0:T(8,128)(2,1)}, u32[]{:S(2)}) copy-start(bf16[96,576]{1,0:T(8,128)(2,1)} %param.8) | copy-start | bytes 331780

commit v4 on v3

--- a/solution.py
+++ b/solution.py
@@ -287,20 +287,23 @@
 
     def work(phase, last=False):
         nonlocal first, result
-        before = 2 if first else 0
+        before = len(phases[phase - 1]) if first else 0
         result = attend(plan, first, query, own, phases[phase], before, result[1], result[0], last, COST if first else FIRST)
-        first += 2
+        first += len(phases[phase])
 
     for i in range(1, chips):
         a = forward = lax.ppermute(sent[i - 1], "node", along)
         if i == 1:
             forward, plan = lax.optimization_barrier((a, plan))
         if i >= 2:
+            if i == chips - 1:
+                phases[i - 2].append(phases[i - 1].pop(0))
             work(i - 2)
             forward, done = lax.optimization_barrier((a, result[1]))
             result = result[0], done
         sent.append(forward)
         phases.append([a, lax.ppermute(forward, "node", across)])
+    phases[-2].append(phases[-1].pop(0))
     work(chips - 2)
     work(chips - 1, True)
     return result

time: 45.5 us -> 44.7 us (0.982); the launches traced: 44.6 us -> 44.6 us
  waiting for transfers between devices: 2.78 us -> 3.86 us
  Pallas kernels: 26.1 us -> 25.1 us
    ppermute x7, waiting for transfers between devices: 2.76 us -> 3.84 us  [shards(): a = forward = lax.ppermute(sent[i - 1], 'node', along)]
    pallas_call x8, Pallas kernels: 22.2 us -> 21.3 us  [attend(): pl.pallas_call(functools.partial(attend_kernel, first, before, last, coun...]
  transfers between devices with their start and end apart: 15 -> 15, of which waited for: 2 -> 5; matrix products, arithmetic and copies ran while one was open for 1% -> 1% of each run, Pallas kernels for 52% -> 51%
where the time goes in v4:
time: 44.7 us; the launch traced here: 44.6 us
  Pallas kernels  25.1 us (56%)
  starting transfers between devices  13.7 us (31%)
  waiting for transfers between devices  3.86 us (9%)
  between operations  0.97 us (2%)
  local copies, waits for them, and re-layouts  0.66 us (1%)
    pallas_call x8, Pallas kernels, attend(): pl.pallas_call(functools.partial(attend_kernel, first, before, last, coun...  21.3 us
    ppermute x7, starting transfers between devices, shards(): a = forward = lax.ppermute(sent[i - 1], 'node', along)  12.8 us
    ppermute x7, waiting for transfers between devices, shards(): a = forward = lax.ppermute(sent[i - 1], 'node', along)  3.84 us
    pallas_call x1, Pallas kernels, prepare(): pl.pallas_call(prepare_kernel, out_shape=(jax.ShapeDtypeStruct((parents +...  3.81 us
  transfers between devices with their start and end apart: 15, of which 5 were waited for; matrix products, arithmetic and copies ran while one was open for 1% of the time, Pallas kernels for 51%

profile of v4, /device:TPU:0, one launch (start us, length us, event | category | flops | bytes accessed | tf_op | source)
XLA Modules:
  0.0 44.6 jit_solution(5296449757696136053)
XLA Ops:
  0.0 0.0 copy-start
  0.0 0.5 %collective-permute-start.1 = (bf16[576,384]{1,0:T(8,128)(2,1)}, bf16[576,384]{1,0:T(8,128)(2,1)S(1)}, u32[]{:S(2)}, u32[]{:S(2)}) collective-permute-start(bf16[576,384]{1,0:T(8,128)(2,1)} %bitcast.7), channel_id=1, source_target_pairs={{0,1},{1,0},{2,3},{3,2},{4,5},{5,4},{6,7},{7,6},{8,9},{9,8},{10,11... | collective-permute-start | bytes 1327112 | tf_op jit(solution)/shard_map/ppermute | solution.py:275
  0.5 2.6 %collective-permute-start = (bf16[576,384]{1,0:T(8,128)(2,1)}, bf16[576,384]{1,0:T(8,128)(2,1)S(1)}, u32[]{:S(2)}, u32[]{:S(2)}) collective-permute-start(bf16[576,384]{1,0:T(8,128)(2,1)} %bitcast.8), channel_id=1, source_target_pairs={{0,4},{4,8},{8,12},{12,14},{14,10},{10,6},{6,2},{2,0},{5,1},{9,5},... | collective-permute-start | bytes 1327112 | tf_op jit(solution)/shard_map/ppermute | solution.py:295
  3.7 0.0 collective-permute-done.1.refs_1_
  3.7 1.6 %collective-permute-start.4 = (bf16[576,384]{1,0:T(8,128)(2,1)S(1)}, bf16[576,384]{1,0:T(8,128)(2,1)S(1)}, u32[]{:S(2)}, u32[]{:S(2)}) collective-permute-start(bf16[576,384]{1,0:T(8,128)(2,1)S(1)} %collective-permute-done.1.refs_1_), channel_id=1, source_target_pairs={{0,4},{4,8},{8,12},{12,14},{14,10},{10,6},{6,2},{2,0},{5,1},{9,5},... | collective-permute-start | bytes 1327112 | tf_op jit(solution)/shard_map/ppermute | solution.py:295
  5.4 3.8 %shard_map.64 = (s32[119]{0:T(128)}, bf16[96,64,576]{2,1,0:T(8,128)(2,1)S(1)}, bf16[576,384]{1,0:T(8,128)(2,1)S(1)}) custom-call(s32[16]{0:T(128)} %place_in, s32[1,96]{1,0:T(1,128)} %bitcast.10, s32[1]{0:T(128)S(6)} %copy.21.live_in, bf16[96,64,576]{2,1,0:T(8,128)(2,1)} %query_in.1, bf16[576,384]{1,0:T(8,128)(2,1)} %bitcast.9), custom_call_target="tpu_custom_call" | custom-call | bytes 14155776 | tf_op jit(solution)/shard_map/pallas_call | solution.py:109
  9.2 0.3 collective-permute-done.refs_0_
  9.5 0.0 collective-permute-start.3
  9.5 2.1 %collective-permute-start.2 = (bf16[576,384]{1,0:T(8,128)(2,1)S(1)}, bf16[576,384]{1,0:T(8,128)(2,1)S(1)}, u32[]{:S(2)}, u32[]{:S(2)}) collective-permute-start(bf16[576,384]{1,0:T(8,128)(2,1)S(1)} %collective-permute-done.refs_0_), channel_id=1, source_target_pairs={{0,4},{4,8},{8,12},{12,14},{14,10},{10,6},{6,2},{2,0},{5,1},{9,5},... | collective-permute-start | bytes 1327112 | tf_op jit(solution)/shard_map/ppermute | solution.py:295
  11.6 0.0 copy-done
  11.6 0.2 fusion.own
  11.8 0.0 copy-start.2
  11.9 0.6 %copy-done.2 = s32[119]{0:T(128)S(1)} copy-done((s32[119]{0:T(128)S(1)}, s32[119]{0:T(128)}, u32[]{:S(2)}) %copy-start.2) | copy-done | bytes 500
  12.5 3.1 %shard_map.65 = (bf16[96,64,512]{2,1,0:T(8,128)(2,1)}, bf16[102,64,512]{2,1,0:T(8,128)(2,1)S(1)}) custom-call(s32[119]{0:T(128)S(1)} %copy-done.2, bf16[96,64,576]{2,1,0:T(8,128)(2,1)S(1)} %get-tuple-element.41.query, bf16[576,128]{1,0:T(8,128)(2,1)S(1)} %fusion.own, bf16[576,384]{1,0:T(8,128)(2,1)S(1)} %get-tuple-element.44.refs_0_, ...), custom_call_target="tpu_custom_call" | custom-call | flops 855638016 | bytes 1966080 | tf_op jit(solution)/shard_map/pallas_call | solution.py:236
  15.6 0.0 collective-permute-done.4.refs_0_
  15.6 0.1 collective-permute-start.8
  15.7 0.7 %collective-permute-start.7 = (bf16[576,384]{1,0:T(8,128)(2,1)S(1)}, bf16[576,384]{1,0:T(8,128)(2,1)S(1)}, u32[]{:S(2)}, u32[]{:S(2)}) collective-permute-start(bf16[576,384]{1,0:T(8,128)(2,1)S(1)} %collective-permute-done.4.refs_0_), channel_id=1, source_target_pairs={{0,4},{4,8},{8,12},{12,14},{14,10},{10,6},{6,2},{2,0},{5,1},{9,5},... | collective-permute-start | bytes 1327112 | tf_op jit(solution)/shard_map/ppermute | solution.py:295
  16.3 0.0 collective-permute-done.3.refs_1_
  16.3 2.1 %shard_map.66 = (bf16[96,64,512]{2,1,0:T(8,128)(2,1)}, bf16[102,64,512]{2,1,0:T(8,128)(2,1)S(1)}) custom-call(s32[119]{0:T(128)S(1)} %copy-done.2, bf16[96,64,576]{2,1,0:T(8,128)(2,1)S(1)} %get-tuple-element.41.query, bf16[576,128]{1,0:T(8,128)(2,1)S(1)} %fusion.own, ...), custom_call_target="tpu_custom_call", output_to_operand_aliasing={{0}: (6, {})} | custom-call | flops 3422552064 | bytes 7864320 | tf_op jit(solution)/shard_map/pallas_call | solution.py:236
  18.4 0.6 %collective-permute-done.2.refs_0_ = bf16[576,384]{1,0:T(8,128)(2,1)S(1)} collective-permute-done((bf16[576,384]{1,0:T(8,128)(2,1)S(1)}, bf16[576,384]{1,0:T(8,128)(2,1)S(1)}, u32[]{:S(2)}, u32[]{:S(2)}) %collective-permute-start.2) | collective-permute-done | bytes 442400 | tf_op jit(solution)/shard_map/ppermute | solution.py:295
  19.0 0.0 collective-permute-start.6
  19.0 2.1 %collective-permute-start.5 = (bf16[576,384]{1,0:T(8,128)(2,1)S(1)}, bf16[576,384]{1,0:T(8,128)(2,1)S(1)}, u32[]{:S(2)}, u32[]{:S(2)}) collective-permute-start(bf16[576,384]{1,0:T(8,128)(2,1)S(1)} %collective-permute-done.2.refs_0_), channel_id=1, source_target_pairs={{0,4},{4,8},{8,12},{12,14},{14,10},{10,6},{6,2},{2,0},{5,1},{9,5},... | collective-permute-start | bytes 1327112 | tf_op jit(solution)/shard_map/ppermute | solution.py:295
  21.1 0.0 collective-permute-done.8.refs_1_
  21.1 2.0 %shard_map.67 = (bf16[96,64,512]{2,1,0:T(8,128)(2,1)}, bf16[102,64,512]{2,1,0:T(8,128)(2,1)S(1)}) custom-call(s32[119]{0:T(128)S(1)} %copy-done.2, bf16[96,64,576]{2,1,0:T(8,128)(2,1)S(1)} %get-tuple-element.41.query, bf16[576,128]{1,0:T(8,128)(2,1)S(1)} %fusion.own, ...), custom_call_target="tpu_custom_call", output_to_operand_aliasing={{0}: (6, {})} | custom-call | flops 3422552064 | bytes 7864320 | tf_op jit(solution)/shard_map/pallas_call | solution.py:236
  23.1 0.9 %collective-permute-done.7.refs_0_ = bf16[576,384]{1,0:T(8,128)(2,1)S(1)} collective-permute-done((bf16[576,384]{1,0:T(8,128)(2,1)S(1)}, bf16[576,384]{1,0:T(8,128)(2,1)S(1)}, u32[]{:S(2)}, u32[]{:S(2)}) %collective-permute-start.7) | collective-permute-done | bytes 442400 | tf_op jit(solution)/shard_map/ppermute | solution.py:295
  24.0 0.0 collective-permute-start.12
  24.0 2.9 %collective-permute-start.11 = (bf16[576,384]{1,0:T(8,128)(2,1)S(1)}, bf16[576,384]{1,0:T(8,128)(2,1)S(1)}, u32[]{:S(2)}, u32[]{:S(2)}) collective-permute-start(bf16[576,384]{1,0:T(8,128)(2,1)S(1)} %collective-permute-done.7.refs_0_), channel_id=1, source_target_pairs={{0,4},{4,8},{8,12},{12,14},{14,10},{10,6},{6,2},{2,0},{5,1},{9,5},... | collective-permute-start | bytes 1327112 | tf_op jit(solution)/shard_map/ppermute | solution.py:295
  26.9 0.0 collective-permute-done.6.refs_1_
  27.0 3.0 %shard_map.68 = (bf16[96,64,512]{2,1,0:T(8,128)(2,1)}, bf16[102,64,512]{2,1,0:T(8,128)(2,1)S(1)}) custom-call(s32[119]{0:T(128)S(1)} %copy-done.2, bf16[96,64,576]{2,1,0:T(8,128)(2,1)S(1)} %get-tuple-element.41.query, bf16[576,128]{1,0:T(8,128)(2,1)S(1)} %fusion.own, ...), custom_call_target="tpu_custom_call", output_to_operand_aliasing={{0}: (6, {})} | custom-call | flops 3422552064 | bytes 7864320 | tf_op jit(solution)/shard_map/pallas_call | solution.py:236
  30.0 0.0 collective-permute-done.5.refs_0_
  30.0 0.1 collective-permute-start.10
  30.1 0.8 %collective-permute-start.9 = (bf16[576,384]{1,0:T(8,128)(2,1)S(1)}, bf16[576,384]{1,0:T(8,128)(2,1)S(1)}, u32[]{:S(2)}, u32[]{:S(2)}) collective-permute-start(bf16[576,384]{1,0:T(8,128)(2,1)S(1)} %collective-permute-done.5.refs_0_), channel_id=1, source_target_pairs={{0,4},{4,8},{8,12},{12,14},{14,10},{10,6},{6,2},{2,0},{5,1},{9,5},... | collective-permute-start | bytes 1327112 | tf_op jit(solution)/shard_map/ppermute | solution.py:295
  30.8 0.0 collective-permute-done.12.refs_1_
  30.8 2.1 %shard_map.69 = (bf16[96,64,512]{2,1,0:T(8,128)(2,1)}, bf16[102,64,512]{2,1,0:T(8,128)(2,1)S(1)}) custom-call(s32[119]{0:T(128)S(1)} %copy-done.2, bf16[96,64,576]{2,1,0:T(8,128)(2,1)S(1)} %get-tuple-element.41.query, bf16[576,128]{1,0:T(8,128)(2,1)S(1)} %fusion.own, ...), custom_call_target="tpu_custom_call", output_to_operand_aliasing={{0}: (6, {})} | custom-call | flops 3422552064 | bytes 7864320 | tf_op jit(solution)/shard_map/pallas_call | solution.py:236
  32.9 0.6 %collective-permute-done.11.refs_2_ = bf16[576,384]{1,0:T(8,128)(2,1)S(1)} collective-permute-done((bf16[576,384]{1,0:T(8,128)(2,1)S(1)}, bf16[576,384]{1,0:T(8,128)(2,1)S(1)}, u32[]{:S(2)}, u32[]{:S(2)}) %collective-permute-start.11) | collective-permute-done | bytes 442400 | tf_op jit(solution)/shard_map/ppermute | solution.py:295
  33.5 0.0 collective-permute-start.14
  33.5 0.0 collective-permute-done.10.refs_1_
  33.5 3.4 %shard_map.70 = (bf16[96,64,512]{2,1,0:T(8,128)(2,1)}, bf16[102,64,512]{2,1,0:T(8,128)(2,1)S(1)}) custom-call(s32[119]{0:T(128)S(1)} %copy-done.2, bf16[96,64,576]{2,1,0:T(8,128)(2,1)S(1)} %get-tuple-element.41.query, bf16[576,128]{1,0:T(8,128)(2,1)S(1)} %fusion.own, ...), custom_call_target="tpu_custom_call", output_to_operand_aliasing={{0}: (7, {})} | custom-call | flops 5133828096 | bytes 11796480 | tf_op jit(solution)/shard_map/pallas_call | solution.py:236
  36.9 1.5 %collective-permute-done.9.refs_1_ = bf16[576,384]{1,0:T(8,128)(2,1)S(1)} collective-permute-done((bf16[576,384]{1,0:T(8,128)(2,1)S(1)}, bf16[576,384]{1,0:T(8,128)(2,1)S(1)}, u32[]{:S(2)}, u32[]{:S(2)}) %collective-permute-start.9) | collective-permute-done | bytes 442400 | tf_op jit(solution)/shard_map/ppermute | solution.py:295
  38.4 0.3 collective-permute-start.13
  38.7 0.0 collective-permute-done.14.refs_0_
  38.7 3.3 %shard_map.71 = (bf16[96,64,512]{2,1,0:T(8,128)(2,1)}, bf16[102,64,512]{2,1,0:T(8,128)(2,1)S(1)}) custom-call(s32[119]{0:T(128)S(1)} %copy-done.2, bf16[96,64,576]{2,1,0:T(8,128)(2,1)S(1)} %get-tuple-element.41.query, bf16[576,128]{1,0:T(8,128)(2,1)S(1)} %fusion.own, ...), custom_call_target="tpu_custom_call", output_to_operand_aliasing={{0}: (6, {})} | custom-call | flops 3422552064 | bytes 7864320 | tf_op jit(solution)/shard_map/pallas_call | solution.py:236
  42.1 0.0 collective-permute-done.13.refs_0_
  42.1 0.0 copy-start.1
  42.1 2.3 %shard_map.72 = bf16[96,64,512]{2,1,0:T(8,128)(2,1)} custom-call(s32[119]{0:T(128)S(1)} %copy-done.2, bf16[96,64,576]{2,1,0:T(8,128)(2,1)S(1)} %get-tuple-element.41.query, bf16[576,128]{1,0:T(8,128)(2,1)S(1)} %fusion.own, bf16[576,384]{1,0:T(8,128)(2,1)S(1)} %collective-permute-done.13.refs_0_, ...), custom_call_target="tpu_custom_call", output_to_operand_aliasing={{}: (5, {})} | custom-call | flops 1711276032 | bytes 3932160 | tf_op jit(solution)/shard_map/pallas_call | solution.py:236
  44.4 0.0 copy-done.1
Async XLA Ops:
  0.0 11.6 %copy-start = (bf16[96,576]{1,0:T(8,128)(2,1)S(1)}, bf16[96,576]{1,0:T(8,128)(2,1)}, u32[]{:S(2)}) copy-start(bf16[96,576]{1,0:T(8,128)(2,1)} %param.8) | copy-start | bytes 331780
  0.0 3.7 %collective-permute-start.1 = (bf16[576,384]{1,0:T(8,128)(2,1)}, bf16[576,384]{1,0:T(8,128)(2,1)S(1)}, u32[]{:S(2)}, u32[]{:S(2)}) collective-permute-start(bf16[576,384]{1,0:T(8,128)(2,1)} %bitcast.7), channel_id=1, source_target_pairs={{0,1},{1,0},{2,3},{3,2},{4,5},{5,4},{6,7},{7,6},{8,9},{9,8},{10,11... | collective-permute-start | bytes 1327112 | tf_op jit(solution)/shard_map/ppermute | solution.py:275
  0.5 9.1 %collective-permute-start = (bf16[576,384]{1,0:T(8,128)(2,1)}, bf16[576,384]{1,0:T(8,128)(2,1)S(1)}, u32[]{:S(2)}, u32[]{:S(2)}) collective-permute-start(bf16[576,384]{1,0:T(8,128)(2,1)} %bitcast.8), channel_id=1, source_target_pairs={{0,4},{4,8},{8,12},{12,14},{14,10},{10,6},{6,2},{2,0},{5,1},{9,5},... | collective-permute-start | bytes 1327112 | tf_op jit(solution)/shard_map/ppermute | solution.py:295
  3.7 11.8 %collective-permute-start.4 = (bf16[576,384]{1,0:T(8,128)(2,1)S(1)}, bf16[576,384]{1,0:T(8,128)(2,1)S(1)}, u32[]{:S(2)}, u32[]{:S(2)}) collective-permute-start(bf16[576,384]{1,0:T(8,128)(2,1)S(1)} %collective-permute-done.1.refs_1_), channel_id=1, source_target_pairs={{0,4},{4,8},{8,12},{12,14},{14,10},{10,6},{6,2},{2,0},{5,1},{9,5},... | collective-permute-start | bytes 1327112 | tf_op jit(solution)/shard_map/ppermute | solution.py:295
  9.5 6.8 %collective-permute-start.3 = (bf16[576,384]{1,0:T(8,128)(2,1)S(1)}, bf16[576,384]{1,0:T(8,128)(2,1)S(1)}, u32[]{:S(2)}, u32[]{:S(2)}) collective-permute-start(bf16[576,384]{1,0:T(8,128)(2,1)S(1)} %collective-permute-done.refs_0_), channel_id=1, source_target_pairs={{0,1},{1,0},{2,3},{3,2},{4,5},{5,4},{6,7},{7,6},{8,9},{9,8},{10,11... | collective-permute-start | bytes 1327112 | tf_op jit(solution)/shard_map/ppermute | solution.py:305
  9.5 9.5 %collective-permute-start.2 = (bf16[576,384]{1,0:T(8,128)(2,1)S(1)}, bf16[576,384]{1,0:T(8,128)(2,1)S(1)}, u32[]{:S(2)}, u32[]{:S(2)}) collective-permute-start(bf16[576,384]{1,0:T(8,128)(2,1)S(1)} %collective-permute-done.refs_0_), channel_id=1, source_target_pairs={{0,4},{4,8},{8,12},{12,14},{14,10},{10,6},{6,2},{2,0},{5,1},{9,5},... | collective-permute-start | bytes 1327112 | tf_op jit(solution)/shard_map/ppermute | solution.py:295
  11.8 0.7 %copy-start.2 = (s32[119]{0:T(128)S(1)}, s32[119]{0:T(128)}, u32[]{:S(2)}) copy-start(s32[119]{0:T(128)} %get-tuple-element.40.plan) | copy-start | bytes 1432
  15.6 5.5 %collective-permute-start.8 = (bf16[576,384]{1,0:T(8,128)(2,1)S(1)}, bf16[576,384]{1,0:T(8,128)(2,1)S(1)}, u32[]{:S(2)}, u32[]{:S(2)}) collective-permute-start(bf16[576,384]{1,0:T(8,128)(2,1)S(1)} %collective-permute-done.4.refs_0_), channel_id=1, source_target_pairs={{0,1},{1,0},{2,3},{3,2},{4,5},{5,4},{6,7},{7,6},{8,9},{9,8},{10,11... | collective-permute-start | bytes 1327112 | tf_op jit(solution)/shard_map/ppermute | solution.py:305
  15.7 8.4 %collective-permute-start.7 = (bf16[576,384]{1,0:T(8,128)(2,1)S(1)}, bf16[576,384]{1,0:T(8,128)(2,1)S(1)}, u32[]{:S(2)}, u32[]{:S(2)}) collective-permute-start(bf16[576,384]{1,0:T(8,128)(2,1)S(1)} %collective-permute-done.4.refs_0_), channel_id=1, source_target_pairs={{0,4},{4,8},{8,12},{12,14},{14,10},{10,6},{6,2},{2,0},{5,1},{9,5},... | collective-permute-start | bytes 1327112 | tf_op jit(solution)/shard_map/ppermute | solution.py:295
  19.0 7.9 %collective-permute-start.6 = (bf16[576,384]{1,0:T(8,128)(2,1)S(1)}, bf16[576,384]{1,0:T(8,128)(2,1)S(1)}, u32[]{:S(2)}, u32[]{:S(2)}) collective-permute-start(bf16[576,384]{1,0:T(8,128)(2,1)S(1)} %collective-permute-done.2.refs_0_), channel_id=1, source_target_pairs={{0,1},{1,0},{2,3},{3,2},{4,5},{5,4},{6,7},{7,6},{8,9},{9,8},{10,11... | collective-permute-start | bytes 1327112 | tf_op jit(solution)/shard_map/ppermute | solution.py:305
  19.0 11.0 %collective-permute-start.5 = (bf16[576,384]{1,0:T(8,128)(2,1)S(1)}, bf16[576,384]{1,0:T(8,128)(2,1)S(1)}, u32[]{:S(2)}, u32[]{:S(2)}) collective-permute-start(bf16[576,384]{1,0:T(8,128)(2,1)S(1)} %collective-permute-done.2.refs_0_), channel_id=1, source_target_pairs={{0,4},{4,8},{8,12},{12,14},{14,10},{10,6},{6,2},{2,0},{5,1},{9,5},... | collective-permute-start | bytes 1327112 | tf_op jit(solution)/shard_map/ppermute | solution.py:295
  24.0 6.8 %collective-permute-start.12 = (bf16[576,384]{1,0:T(8,128)(2,1)S(1)}, bf16[576,384]{1,0:T(8,128)(2,1)S(1)}, u32[]{:S(2)}, u32[]{:S(2)}) collective-permute-start(bf16[576,384]{1,0:T(8,128)(2,1)S(1)} %collective-permute-done.7.refs_0_), channel_id=1, source_target_pairs={{0,1},{1,0},{2,3},{3,2},{4,5},{5,4},{6,7},{7,6},{8,9},{9,8},{10,11... | collective-permute-start | bytes 1327112 | tf_op jit(solution)/shard_map/ppermute | solution.py:305
  24.0 9.5 %collective-permute-start.11 = (bf16[576,384]{1,0:T(8,128)(2,1)S(1)}, bf16[576,384]{1,0:T(8,128)(2,1)S(1)}, u32[]{:S(2)}, u32[]{:S(2)}) collective-permute-start(bf16[576,384]{1,0:T(8,128)(2,1)S(1)} %collective-permute-done.7.refs_0_), channel_id=1, source_target_pairs={{0,4},{4,8},{8,12},{12,14},{14,10},{10,6},{6,2},{2,0},{5,1},{9,5},... | collective-permute-start | bytes 1327112 | tf_op jit(solution)/shard_map/ppermute | solution.py:295
  30.0 3.5 %collective-permute-start.10 = (bf16[576,384]{1,0:T(8,128)(2,1)S(1)}, bf16[576,384]{1,0:T(8,128)(2,1)S(1)}, u32[]{:S(2)}, u32[]{:S(2)}) collective-permute-start(bf16[576,384]{1,0:T(8,128)(2,1)S(1)} %collective-permute-done.5.refs_0_), channel_id=1, source_target_pairs={{0,1},{1,0},{2,3},{3,2},{4,5},{5,4},{6,7},{7,6},{8,9},{9,8},{10,11... | collective-permute-start | bytes 1327112 | tf_op jit(solution)/shard_map/ppermute | solution.py:305
  30.1 8.4 %collective-permute-start.9 = (bf16[576,384]{1,0:T(8,128)(2,1)S(1)}, bf16[576,384]{1,0:T(8,128)(2,1)S(1)}, u32[]{:S(2)}, u32[]{:S(2)}) collective-permute-start(bf16[576,384]{1,0:T(8,128)(2,1)S(1)} %collective-permute-done.5.refs_0_), channel_id=1, source_target_pairs={{0,4},{4,8},{8,12},{12,14},{14,10},{10,6},{6,2},{2,0},{5,1},{9,5},... | collective-permute-start | bytes 1327112 | tf_op jit(solution)/shard_map/ppermute | solution.py:295
  33.5 5.2 %collective-permute-start.14 = (bf16[576,384]{1,0:T(8,128)(2,1)S(1)}, bf16[576,384]{1,0:T(8,128)(2,1)S(1)}, u32[]{:S(2)}, u32[]{:S(2)}) collective-permute-start(bf16[576,384]{1,0:T(8,128)(2,1)S(1)} %collective-permute-done.11.refs_2_), channel_id=1, source_target_pairs={{0,1},{1,0},{2,3},{3,2},{4,5},{5,4},{6,7},{7,6},{8,9},{9,8},{10,11... | collective-permute-start | bytes 1327112 | tf_op jit(solution)/shard_map/ppermute | solution.py:305
  38.4 3.7 %collective-permute-start.13 = (bf16[576,384]{1,0:T(8,128)(2,1)S(1)}, bf16[576,384]{1,0:T(8,128)(2,1)S(1)}, u32[]{:S(2)}, u32[]{:S(2)}) collective-permute-start(bf16[576,384]{1,0:T(8,128)(2,1)S(1)} %collective-permute-done.9.refs_1_), channel_id=1, source_target_pairs={{0,1},{1,0},{2,3},{3,2},{4,5},{5,4},{6,7},{7,6},{8,9},{9,8},{10,11... | collective-permute-start | bytes 1327112 | tf_op jit(solution)/shard_map/ppermute | solution.py:305
  42.1 2.3 %copy-start.1 = (bf16[96,576]{1,0:T(8,128)(2,1)S(1)}, bf16[96,576]{1,0:T(8,128)(2,1)}, u32[]{:S(2)}) copy-start(bf16[96,576]{1,0:T(8,128)(2,1)} %param.8) | copy-start | bytes 331780

commit v5 on v4

--- a/solution.py
+++ b/solution.py
@@ -10,7 +10,7 @@
 
 LAT = 512
 SCALE = 0.07216878364870322
-BLOCK = 6
+BLOCK = 5
 COST = 4
 FIRST = 1
 ANY = pl.BlockSpec(memory_space=pl.ANY)

time: 44.7 us -> 45.6 us (1.020)
  waiting for transfers between devices: 3.86 us -> 0.36 us
  starting transfers between devices: 13.7 us -> 17.1 us
  Pallas kernels: 25.1 us -> 26.5 us
    ppermute x7, waiting for transfers between devices: 3.84 us -> 0.34 us  [shards(): a = forward = lax.ppermute(sent[i - 1], 'node', along)]
    ppermute x7, starting transfers between devices: 0.49 us -> 2.67 us  [shards(): phases.append([a, lax.ppermute(forward, 'node', across)])]
    pallas_call x8, Pallas kernels: 21.3 us -> 22.7 us  [attend(): pl.pallas_call(functools.partial(attend_kernel, first, before, last, coun...]
    ppermute x7, starting transfers between devices: 12.8 us -> 14 us  [shards(): a = forward = lax.ppermute(sent[i - 1], 'node', along)]
  transfers between devices with their start and end apart: 15 -> 15, of which waited for: 5 -> 1; matrix products, arithmetic and copies ran while one was open for 1% -> 1% of each run, Pallas kernels for 51% -> 53%
where the time goes in v5:
time: 45.6 us; the launch traced here: 45.7 us
  Pallas kernels  26.5 us (58%)
  starting transfers between devices  17.1 us (38%)
  between operations  0.85 us (2%)
  local copies, waits for them, and re-layouts  0.66 us (1%)
    pallas_call x8, Pallas kernels, attend(): pl.pallas_call(functools.partial(attend_kernel, first, before, last, coun...  22.7 us
    ppermute x7, starting transfers between devices, shards(): a = forward = lax.ppermute(sent[i - 1], 'node', along)  14 us
    pallas_call x1, Pallas kernels, prepare(): pl.pallas_call(prepare_kernel, out_shape=(jax.ShapeDtypeStruct((parents +...  3.81 us
    ppermute x7, starting transfers between devices, shards(): phases.append([a, lax.ppermute(forward, 'node', across)])  2.67 us
  transfers between devices with their start and end apart: 15, of which 1 were waited for; matrix products, arithmetic and copies ran while one was open for 1% of the time, Pallas kernels for 53%

profile of v5, /device:TPU:0, one launch (start us, length us, event | category | flops | bytes accessed | tf_op | source)
XLA Modules:
  0.0 45.7 jit_solution(9376615054789937288)
XLA Ops:
  0.0 0.0 copy-start
  0.0 0.5 collective-permute-start.1
  0.5 2.6 %collective-permute-start = (bf16[576,384]{1,0:T(8,128)(2,1)}, bf16[576,384]{1,0:T(8,128)(2,1)S(1)}, u32[]{:S(2)}, u32[]{:S(2)}) collective-permute-start(bf16[576,384]{1,0:T(8,128)(2,1)} %bitcast.8), channel_id=1, source_target_pairs={{0,4},{4,8},{8,12},{12,14},{14,10},{10,6},{6,2},{2,0},{5,1},{9,5},... | collective-permute-start | bytes 1327112 | tf_op jit(solution)/shard_map/ppermute | solution.py:295
  3.7 0.0 collective-permute-done.1.refs_1_
  3.7 1.6 %collective-permute-start.4 = (bf16[576,384]{1,0:T(8,128)(2,1)S(1)}, bf16[576,384]{1,0:T(8,128)(2,1)S(1)}, u32[]{:S(2)}, u32[]{:S(2)}) collective-permute-start(bf16[576,384]{1,0:T(8,128)(2,1)S(1)} %collective-permute-done.1.refs_1_), channel_id=1, source_target_pairs={{0,4},{4,8},{8,12},{12,14},{14,10},{10,6},{6,2},{2,0},{5,1},{9,5},... | collective-permute-start | bytes 1327112 | tf_op jit(solution)/shard_map/ppermute | solution.py:295
  5.4 3.8 %shard_map.64 = (s32[118]{0:T(128)}, bf16[96,64,576]{2,1,0:T(8,128)(2,1)S(1)}, bf16[576,384]{1,0:T(8,128)(2,1)S(1)}) custom-call(s32[16]{0:T(128)} %place_in, s32[1,96]{1,0:T(1,128)} %bitcast.10, s32[1]{0:T(128)S(6)} %copy.21.live_in, bf16[96,64,576]{2,1,0:T(8,128)(2,1)} %query_in.1, bf16[576,384]{1,0:T(8,128)(2,1)} %bitcast.9), custom_call_target="tpu_custom_call" | custom-call | bytes 14155776 | tf_op jit(solution)/shard_map/pallas_call | solution.py:109
  9.2 0.3 collective-permute-done.refs_0_
  9.5 0.0 collective-permute-start.3
  9.5 2.1 %collective-permute-start.2 = (bf16[576,384]{1,0:T(8,128)(2,1)S(1)}, bf16[576,384]{1,0:T(8,128)(2,1)S(1)}, u32[]{:S(2)}, u32[]{:S(2)}) collective-permute-start(bf16[576,384]{1,0:T(8,128)(2,1)S(1)} %collective-permute-done.refs_0_), channel_id=1, source_target_pairs={{0,4},{4,8},{8,12},{12,14},{14,10},{10,6},{6,2},{2,0},{5,1},{9,5},... | collective-permute-start | bytes 1327112 | tf_op jit(solution)/shard_map/ppermute | solution.py:295
  11.6 0.0 copy-done
  11.6 0.2 fusion.own
  11.8 0.0 copy-start.2
  11.9 0.6 %copy-done.2 = s32[118]{0:T(128)S(1)} copy-done((s32[118]{0:T(128)S(1)}, s32[118]{0:T(128)}, u32[]{:S(2)}) %copy-start.2) | copy-done | bytes 496
  12.5 2.8 %shard_map.65 = (bf16[96,64,512]{2,1,0:T(8,128)(2,1)}, bf16[101,64,512]{2,1,0:T(8,128)(2,1)S(1)}) custom-call(s32[118]{0:T(128)S(1)} %copy-done.2, bf16[96,64,576]{2,1,0:T(8,128)(2,1)S(1)} %get-tuple-element.41.query, bf16[576,128]{1,0:T(8,128)(2,1)S(1)} %fusion.own, bf16[576,384]{1,0:T(8,128)(2,1)S(1)} %get-tuple-element.44.refs_0_, ...), custom_call_target="tpu_custom_call" | custom-call | flops 855638016 | bytes 1966080 | tf_op jit(solution)/shard_map/pallas_call | solution.py:236
  15.3 0.0 collective-permute-done.4.refs_0_
  15.3 0.1 collective-permute-start.8
  15.4 0.9 %collective-permute-start.7 = (bf16[576,384]{1,0:T(8,128)(2,1)S(1)}, bf16[576,384]{1,0:T(8,128)(2,1)S(1)}, u32[]{:S(2)}, u32[]{:S(2)}) collective-permute-start(bf16[576,384]{1,0:T(8,128)(2,1)S(1)} %collective-permute-done.4.refs_0_), channel_id=1, source_target_pairs={{0,4},{4,8},{8,12},{12,14},{14,10},{10,6},{6,2},{2,0},{5,1},{9,5},... | collective-permute-start | bytes 1327112 | tf_op jit(solution)/shard_map/ppermute | solution.py:295
  16.3 0.0 collective-permute-done.3.refs_1_
  16.3 2.9 %shard_map.66 = (bf16[96,64,512]{2,1,0:T(8,128)(2,1)}, bf16[101,64,512]{2,1,0:T(8,128)(2,1)S(1)}) custom-call(s32[118]{0:T(128)S(1)} %copy-done.2, bf16[96,64,576]{2,1,0:T(8,128)(2,1)S(1)} %get-tuple-element.41.query, bf16[576,128]{1,0:T(8,128)(2,1)S(1)} %fusion.own, ...), custom_call_target="tpu_custom_call", output_to_operand_aliasing={{0}: (6, {})} | custom-call | flops 3422552064 | bytes 7864320 | tf_op jit(solution)/shard_map/pallas_call | solution.py:236
  19.2 0.0 collective-permute-done.2.refs_0_
  19.2 0.2 collective-permute-start.6
  19.4 1.7 %collective-permute-start.5 = (bf16[576,384]{1,0:T(8,128)(2,1)S(1)}, bf16[576,384]{1,0:T(8,128)(2,1)S(1)}, u32[]{:S(2)}, u32[]{:S(2)}) collective-permute-start(bf16[576,384]{1,0:T(8,128)(2,1)S(1)} %collective-permute-done.2.refs_0_), channel_id=1, source_target_pairs={{0,4},{4,8},{8,12},{12,14},{14,10},{10,6},{6,2},{2,0},{5,1},{9,5},... | collective-permute-start | bytes 1327112 | tf_op jit(solution)/shard_map/ppermute | solution.py:295
  21.1 0.0 collective-permute-done.8.refs_1_
  21.1 2.8 %shard_map.67 = (bf16[96,64,512]{2,1,0:T(8,128)(2,1)}, bf16[101,64,512]{2,1,0:T(8,128)(2,1)S(1)}) custom-call(s32[118]{0:T(128)S(1)} %copy-done.2, bf16[96,64,576]{2,1,0:T(8,128)(2,1)S(1)} %get-tuple-element.41.query, bf16[576,128]{1,0:T(8,128)(2,1)S(1)} %fusion.own, ...), custom_call_target="tpu_custom_call", output_to_operand_aliasing={{0}: (6, {})} | custom-call | flops 3422552064 | bytes 7864320 | tf_op jit(solution)/shard_map/pallas_call | solution.py:236
  23.9 0.0 collective-permute-done.7.refs_0_
  23.9 0.2 collective-permute-start.12
  24.2 2.7 %collective-permute-start.11 = (bf16[576,384]{1,0:T(8,128)(2,1)S(1)}, bf16[576,384]{1,0:T(8,128)(2,1)S(1)}, u32[]{:S(2)}, u32[]{:S(2)}) collective-permute-start(bf16[576,384]{1,0:T(8,128)(2,1)S(1)} %collective-permute-done.7.refs_0_), channel_id=1, source_target_pairs={{0,4},{4,8},{8,12},{12,14},{14,10},{10,6},{6,2},{2,0},{5,1},{9,5},... | collective-permute-start | bytes 1327112 | tf_op jit(solution)/shard_map/ppermute | solution.py:295
  26.8 0.0 collective-permute-done.6.refs_1_
  26.8 2.0 %shard_map.68 = (bf16[96,64,512]{2,1,0:T(8,128)(2,1)}, bf16[101,64,512]{2,1,0:T(8,128)(2,1)S(1)}) custom-call(s32[118]{0:T(128)S(1)} %copy-done.2, bf16[96,64,576]{2,1,0:T(8,128)(2,1)S(1)} %get-tuple-element.41.query, bf16[576,128]{1,0:T(8,128)(2,1)S(1)} %fusion.own, ...), custom_call_target="tpu_custom_call", output_to_operand_aliasing={{0}: (6, {})} | custom-call | flops 3422552064 | bytes 7864320 | tf_op jit(solution)/shard_map/pallas_call | solution.py:236
  28.9 0.0 collective-permute-done.5.refs_0_
  28.9 0.1 collective-permute-start.10
  28.9 2.4 %collective-permute-start.9 = (bf16[576,384]{1,0:T(8,128)(2,1)S(1)}, bf16[576,384]{1,0:T(8,128)(2,1)S(1)}, u32[]{:S(2)}, u32[]{:S(2)}) collective-permute-start(bf16[576,384]{1,0:T(8,128)(2,1)S(1)} %collective-permute-done.5.refs_0_), channel_id=1, source_target_pairs={{0,4},{4,8},{8,12},{12,14},{14,10},{10,6},{6,2},{2,0},{5,1},{9,5},... | collective-permute-start | bytes 1327112 | tf_op jit(solution)/shard_map/ppermute | solution.py:295
  31.4 0.0 collective-permute-done.12.refs_1_
  31.4 2.8 %shard_map.69 = (bf16[96,64,512]{2,1,0:T(8,128)(2,1)}, bf16[101,64,512]{2,1,0:T(8,128)(2,1)S(1)}) custom-call(s32[118]{0:T(128)S(1)} %copy-done.2, bf16[96,64,576]{2,1,0:T(8,128)(2,1)S(1)} %get-tuple-element.41.query, bf16[576,128]{1,0:T(8,128)(2,1)S(1)} %fusion.own, ...), custom_call_target="tpu_custom_call", output_to_operand_aliasing={{0}: (6, {})} | custom-call | flops 3422552064 | bytes 7864320 | tf_op jit(solution)/shard_map/pallas_call | solution.py:236
  34.2 0.0 collective-permute-done.11.refs_2_
  34.2 0.1 collective-permute-start.14
  34.3 0.0 collective-permute-done.10.refs_1_
  34.3 4.1 %shard_map.70 = (bf16[96,64,512]{2,1,0:T(8,128)(2,1)}, bf16[101,64,512]{2,1,0:T(8,128)(2,1)S(1)}) custom-call(s32[118]{0:T(128)S(1)} %copy-done.2, bf16[96,64,576]{2,1,0:T(8,128)(2,1)S(1)} %get-tuple-element.41.query, bf16[576,128]{1,0:T(8,128)(2,1)S(1)} %fusion.own, ...), custom_call_target="tpu_custom_call", output_to_operand_aliasing={{0}: (7, {})} | custom-call | flops 5133828096 | bytes 11796480 | tf_op jit(solution)/shard_map/pallas_call | solution.py:236
  38.4 0.0 collective-permute-done.9.refs_1_
  38.4 2.0 %collective-permute-start.13 = (bf16[576,384]{1,0:T(8,128)(2,1)S(1)}, bf16[576,384]{1,0:T(8,128)(2,1)S(1)}, u32[]{:S(2)}, u32[]{:S(2)}) collective-permute-start(bf16[576,384]{1,0:T(8,128)(2,1)S(1)} %collective-permute-done.9.refs_1_), channel_id=1, source_target_pairs={{0,1},{1,0},{2,3},{3,2},{4,5},{5,4},{6,7},{7,6},{8,9},{9,8},{10,11... | collective-permute-start | bytes 1327112 | tf_op jit(solution)/shard_map/ppermute | solution.py:305
  40.4 0.0 collective-permute-done.14.refs_0_
  40.4 3.0 %shard_map.71 = (bf16[96,64,512]{2,1,0:T(8,128)(2,1)}, bf16[101,64,512]{2,1,0:T(8,128)(2,1)S(1)}) custom-call(s32[118]{0:T(128)S(1)} %copy-done.2, bf16[96,64,576]{2,1,0:T(8,128)(2,1)S(1)} %get-tuple-element.41.query, bf16[576,128]{1,0:T(8,128)(2,1)S(1)} %fusion.own, ...), custom_call_target="tpu_custom_call", output_to_operand_aliasing={{0}: (6, {})} | custom-call | flops 3422552064 | bytes 7864320 | tf_op jit(solution)/shard_map/pallas_call | solution.py:236
  43.4 0.0 collective-permute-done.13.refs_0_
  43.4 0.0 copy-start.1
  43.4 2.3 %shard_map.72 = bf16[96,64,512]{2,1,0:T(8,128)(2,1)} custom-call(s32[118]{0:T(128)S(1)} %copy-done.2, bf16[96,64,576]{2,1,0:T(8,128)(2,1)S(1)} %get-tuple-element.41.query, bf16[576,128]{1,0:T(8,128)(2,1)S(1)} %fusion.own, bf16[576,384]{1,0:T(8,128)(2,1)S(1)} %collective-permute-done.13.refs_0_, ...), custom_call_target="tpu_custom_call", output_to_operand_aliasing={{}: (5, {})} | custom-call | flops 1711276032 | bytes 3932160 | tf_op jit(solution)/shard_map/pallas_call | solution.py:236
  45.7 0.0 copy-done.1
Async XLA Ops:
  0.0 11.6 %copy-start = (bf16[96,576]{1,0:T(8,128)(2,1)S(1)}, bf16[96,576]{1,0:T(8,128)(2,1)}, u32[]{:S(2)}) copy-start(bf16[96,576]{1,0:T(8,128)(2,1)} %param.8) | copy-start | bytes 331780
  0.0 3.7 %collective-permute-start.1 = (bf16[576,384]{1,0:T(8,128)(2,1)}, bf16[576,384]{1,0:T(8,128)(2,1)S(1)}, u32[]{:S(2)}, u32[]{:S(2)}) collective-permute-start(bf16[576,384]{1,0:T(8,128)(2,1)} %bitcast.7), channel_id=1, source_target_pairs={{0,1},{1,0},{2,3},{3,2},{4,5},{5,4},{6,7},{7,6},{8,9},{9,8},{10,11... | collective-permute-start | bytes 1327112 | tf_op jit(solution)/shard_map/ppermute | solution.py:275
  0.5 9.1 %collective-permute-start = (bf16[576,384]{1,0:T(8,128)(2,1)}, bf16[576,384]{1,0:T(8,128)(2,1)S(1)}, u32[]{:S(2)}, u32[]{:S(2)}) collective-permute-start(bf16[576,384]{1,0:T(8,128)(2,1)} %bitcast.8), channel_id=1, source_target_pairs={{0,4},{4,8},{8,12},{12,14},{14,10},{10,6},{6,2},{2,0},{5,1},{9,5},... | collective-permute-start | bytes 1327112 | tf_op jit(solution)/shard_map/ppermute | solution.py:295
  3.7 11.6 %collective-permute-start.4 = (bf16[576,384]{1,0:T(8,128)(2,1)S(1)}, bf16[576,384]{1,0:T(8,128)(2,1)S(1)}, u32[]{:S(2)}, u32[]{:S(2)}) collective-permute-start(bf16[576,384]{1,0:T(8,128)(2,1)S(1)} %collective-permute-done.1.refs_1_), channel_id=1, source_target_pairs={{0,4},{4,8},{8,12},{12,14},{14,10},{10,6},{6,2},{2,0},{5,1},{9,5},... | collective-permute-start | bytes 1327112 | tf_op jit(solution)/shard_map/ppermute | solution.py:295
  9.5 6.8 %collective-permute-start.3 = (bf16[576,384]{1,0:T(8,128)(2,1)S(1)}, bf16[576,384]{1,0:T(8,128)(2,1)S(1)}, u32[]{:S(2)}, u32[]{:S(2)}) collective-permute-start(bf16[576,384]{1,0:T(8,128)(2,1)S(1)} %collective-permute-done.refs_0_), channel_id=1, source_target_pairs={{0,1},{1,0},{2,3},{3,2},{4,5},{5,4},{6,7},{7,6},{8,9},{9,8},{10,11... | collective-permute-start | bytes 1327112 | tf_op jit(solution)/shard_map/ppermute | solution.py:305
  9.5 9.7 %collective-permute-start.2 = (bf16[576,384]{1,0:T(8,128)(2,1)S(1)}, bf16[576,384]{1,0:T(8,128)(2,1)S(1)}, u32[]{:S(2)}, u32[]{:S(2)}) collective-permute-start(bf16[576,384]{1,0:T(8,128)(2,1)S(1)} %collective-permute-done.refs_0_), channel_id=1, source_target_pairs={{0,4},{4,8},{8,12},{12,14},{14,10},{10,6},{6,2},{2,0},{5,1},{9,5},... | collective-permute-start | bytes 1327112 | tf_op jit(solution)/shard_map/ppermute | solution.py:295
  11.8 0.7 %copy-start.2 = (s32[118]{0:T(128)S(1)}, s32[118]{0:T(128)}, u32[]{:S(2)}) copy-start(s32[118]{0:T(128)} %get-tuple-element.40.plan) | copy-start | bytes 1420
  15.3 5.7 %collective-permute-start.8 = (bf16[576,384]{1,0:T(8,128)(2,1)S(1)}, bf16[576,384]{1,0:T(8,128)(2,1)S(1)}, u32[]{:S(2)}, u32[]{:S(2)}) collective-permute-start(bf16[576,384]{1,0:T(8,128)(2,1)S(1)} %collective-permute-done.4.refs_0_), channel_id=1, source_target_pairs={{0,1},{1,0},{2,3},{3,2},{4,5},{5,4},{6,7},{7,6},{8,9},{9,8},{10,11... | collective-permute-start | bytes 1327112 | tf_op jit(solution)/shard_map/ppermute | solution.py:305
  15.4 8.5 %collective-permute-start.7 = (bf16[576,384]{1,0:T(8,128)(2,1)S(1)}, bf16[576,384]{1,0:T(8,128)(2,1)S(1)}, u32[]{:S(2)}, u32[]{:S(2)}) collective-permute-start(bf16[576,384]{1,0:T(8,128)(2,1)S(1)} %collective-permute-done.4.refs_0_), channel_id=1, source_target_pairs={{0,4},{4,8},{8,12},{12,14},{14,10},{10,6},{6,2},{2,0},{5,1},{9,5},... | collective-permute-start | bytes 1327112 | tf_op jit(solution)/shard_map/ppermute | solution.py:295
  19.2 7.6 %collective-permute-start.6 = (bf16[576,384]{1,0:T(8,128)(2,1)S(1)}, bf16[576,384]{1,0:T(8,128)(2,1)S(1)}, u32[]{:S(2)}, u32[]{:S(2)}) collective-permute-start(bf16[576,384]{1,0:T(8,128)(2,1)S(1)} %collective-permute-done.2.refs_0_), channel_id=1, source_target_pairs={{0,1},{1,0},{2,3},{3,2},{4,5},{5,4},{6,7},{7,6},{8,9},{9,8},{10,11... | collective-permute-start | bytes 1327112 | tf_op jit(solution)/shard_map/ppermute | solution.py:305
  19.4 9.4 %collective-permute-start.5 = (bf16[576,384]{1,0:T(8,128)(2,1)S(1)}, bf16[576,384]{1,0:T(8,128)(2,1)S(1)}, u32[]{:S(2)}, u32[]{:S(2)}) collective-permute-start(bf16[576,384]{1,0:T(8,128)(2,1)S(1)} %collective-permute-done.2.refs_0_), channel_id=1, source_target_pairs={{0,4},{4,8},{8,12},{12,14},{14,10},{10,6},{6,2},{2,0},{5,1},{9,5},... | collective-permute-start | bytes 1327112 | tf_op jit(solution)/shard_map/ppermute | solution.py:295
  23.9 7.4 %collective-permute-start.12 = (bf16[576,384]{1,0:T(8,128)(2,1)S(1)}, bf16[576,384]{1,0:T(8,128)(2,1)S(1)}, u32[]{:S(2)}, u32[]{:S(2)}) collective-permute-start(bf16[576,384]{1,0:T(8,128)(2,1)S(1)} %collective-permute-done.7.refs_0_), channel_id=1, source_target_pairs={{0,1},{1,0},{2,3},{3,2},{4,5},{5,4},{6,7},{7,6},{8,9},{9,8},{10,11... | collective-permute-start | bytes 1327112 | tf_op jit(solution)/shard_map/ppermute | solution.py:305
  24.2 10.0 %collective-permute-start.11 = (bf16[576,384]{1,0:T(8,128)(2,1)S(1)}, bf16[576,384]{1,0:T(8,128)(2,1)S(1)}, u32[]{:S(2)}, u32[]{:S(2)}) collective-permute-start(bf16[576,384]{1,0:T(8,128)(2,1)S(1)} %collective-permute-done.7.refs_0_), channel_id=1, source_target_pairs={{0,4},{4,8},{8,12},{12,14},{14,10},{10,6},{6,2},{2,0},{5,1},{9,5},... | collective-permute-start | bytes 1327112 | tf_op jit(solution)/shard_map/ppermute | solution.py:295
  28.9 5.4 %collective-permute-start.10 = (bf16[576,384]{1,0:T(8,128)(2,1)S(1)}, bf16[576,384]{1,0:T(8,128)(2,1)S(1)}, u32[]{:S(2)}, u32[]{:S(2)}) collective-permute-start(bf16[576,384]{1,0:T(8,128)(2,1)S(1)} %collective-permute-done.5.refs_0_), channel_id=1, source_target_pairs={{0,1},{1,0},{2,3},{3,2},{4,5},{5,4},{6,7},{7,6},{8,9},{9,8},{10,11... | collective-permute-start | bytes 1327112 | tf_op jit(solution)/shard_map/ppermute | solution.py:305
  28.9 9.4 %collective-permute-start.9 = (bf16[576,384]{1,0:T(8,128)(2,1)S(1)}, bf16[576,384]{1,0:T(8,128)(2,1)S(1)}, u32[]{:S(2)}, u32[]{:S(2)}) collective-permute-start(bf16[576,384]{1,0:T(8,128)(2,1)S(1)} %collective-permute-done.5.refs_0_), channel_id=1, source_target_pairs={{0,4},{4,8},{8,12},{12,14},{14,10},{10,6},{6,2},{2,0},{5,1},{9,5},... | collective-permute-start | bytes 1327112 | tf_op jit(solution)/shard_map/ppermute | solution.py:295
  34.2 6.2 %collective-permute-start.14 = (bf16[576,384]{1,0:T(8,128)(2,1)S(1)}, bf16[576,384]{1,0:T(8,128)(2,1)S(1)}, u32[]{:S(2)}, u32[]{:S(2)}) collective-permute-start(bf16[576,384]{1,0:T(8,128)(2,1)S(1)} %collective-permute-done.11.refs_2_), channel_id=1, source_target_pairs={{0,1},{1,0},{2,3},{3,2},{4,5},{5,4},{6,7},{7,6},{8,9},{9,8},{10,11... | collective-permute-start | bytes 1327112 | tf_op jit(solution)/shard_map/ppermute | solution.py:305
  38.4 5.0 %collective-permute-start.13 = (bf16[576,384]{1,0:T(8,128)(2,1)S(1)}, bf16[576,384]{1,0:T(8,128)(2,1)S(1)}, u32[]{:S(2)}, u32[]{:S(2)}) collective-permute-start(bf16[576,384]{1,0:T(8,128)(2,1)S(1)} %collective-permute-done.9.refs_1_), channel_id=1, source_target_pairs={{0,1},{1,0},{2,3},{3,2},{4,5},{5,4},{6,7},{7,6},{8,9},{9,8},{10,11... | collective-permute-start | bytes 1327112 | tf_op jit(solution)/shard_map/ppermute | solution.py:305
  43.4 2.3 %copy-start.1 = (bf16[96,576]{1,0:T(8,128)(2,1)S(1)}, bf16[96,576]{1,0:T(8,128)(2,1)}, u32[]{:S(2)}) copy-start(bf16[96,576]{1,0:T(8,128)(2,1)} %param.8) | copy-start | bytes 331780

commit v6 on v4

--- a/solution.py
+++ b/solution.py
@@ -135,6 +135,7 @@
     done = refs[arrays] if before else None
     rows, heads, depth = query.shape
     prefix = slots[0].shape[-1]
+    block = even.shape[0] // heads
     width = kv.shape[2]
     dead = plan.shape[0] - BLOCK - rows - 1
     order = plan.at[pl.ds(dead + 1, rows + BLOCK)]
@@ -157,12 +158,12 @@
         kv[s, :, 0:prefix] = slots[s][...]
         kv[s, :, prefix:width] = own[...]
         lo, hi = starts[first + s], starts[first + s + 1]
-        more = (hi - lo + BLOCK - 1) // BLOCK
+        more = (hi - lo + block - 1) // block
 
         def note(b, _):
             blocks[0, number + b] = s
-            blocks[1, number + b] = lo + b * BLOCK
-            blocks[2, number + b] = jnp.minimum(lo + (b + 1) * BLOCK, hi)
+            blocks[1, number + b] = lo + b * block
+            blocks[2, number + b] = jnp.minimum(lo + (b + 1) * block, hi)
             return 0
 
         lax.fori_loop(0, more, note, 0)
@@ -171,14 +172,14 @@
 
     def score(b, to):
         begin = blocks[1, b]
-        q = jnp.concatenate([query[order[begin + r]] for r in range(BLOCK)])
+        q = jnp.concatenate([query[order[begin + r]] for r in range(block)])
         to[...] = jnp.dot(q, kv[blocks[0, b]], preferred_element_type=jnp.float32)
 
     def finish(b, scores):
         begin = blocks[1, b]
         mine = [
             jnp.where(column == order[begin + r], scores[r * heads:(r + 1) * heads, prefix:width], -jnp.inf)
-            for r in range(BLOCK)
+            for r in range(block)
         ]
         s = jnp.concatenate([scores[:, 0:prefix], jnp.concatenate(mine)], axis=1)
         top = jnp.max(s, axis=1, keepdims=True)
@@ -188,7 +189,7 @@
         mixed = lax.dot_general(
             weights, kv[blocks[0, b], 0:LAT, :], (((1,), (1,)), ((), ())), preferred_element_type=jnp.float32
         )
-        ov[pl.ds(begin, BLOCK)] = mixed.astype(jnp.bfloat16).reshape(BLOCK, heads, LAT)
+        ov[pl.ds(begin, block)] = mixed.astype(jnp.bfloat16).reshape(block, heads, LAT)
 
     def send(b):
         @pl.loop(blocks[1, b], blocks[2, b])
@@ -227,6 +228,7 @@
 def attend(plan, first, query, own, slots, before=0, done=None, out=None, last=False, cost=COST):
     rows, heads, depth = query.shape
     count = len(slots)
+    block = BLOCK // 2 if last else BLOCK
     prefix = slots[0].shape[-1]
     width = prefix + own.shape[1]
     operands = [plan, query, own, *slots] + ([done, out] if before else [])
@@ -240,10 +242,10 @@
         out_specs=ANY if last else (ANY, VMEM),
         scratch_shapes=[made] * last + [
             pltpu.VMEM((count, depth, width), jnp.bfloat16),
-            pltpu.VMEM((BLOCK * heads, width), jnp.float32),
-            pltpu.VMEM((BLOCK * heads, width), jnp.float32),
+            pltpu.VMEM((block * heads, width), jnp.float32),
+            pltpu.VMEM((block * heads, width), jnp.float32),
             pltpu.VMEM((heads, LAT), jnp.bfloat16),
-            pltpu.SMEM((3, rows // BLOCK + count + 4), jnp.int32),
+            pltpu.SMEM((3, rows // block + count + 4), jnp.int32),
             pltpu.SemaphoreType.DMA,
         ],
         input_output_aliases={len(operands) - 1: 0} if before else {},

time: 44.7 us -> 44.8 us (level); the launches traced: 44.6 us -> 44.1 us
  Pallas kernels: 25.1 us -> 27.1 us
  waiting for transfers between devices: 3.86 us -> 2.33 us
  starting transfers between devices: 13.7 us -> 12.8 us
    pallas_call x8, Pallas kernels: 21.3 us -> 23.3 us  [attend(): pl.pallas_call(functools.partial(attend_kernel, first, before, last, coun...]
    ppermute x7, waiting for transfers between devices: 3.84 us -> 2.31 us  [shards(): a = forward = lax.ppermute(sent[i - 1], 'node', along)]
    ppermute x7, starting transfers between devices: 12.8 us -> 11.9 us  [shards(): a = forward = lax.ppermute(sent[i - 1], 'node', along)]
  transfers between devices with their start and end apart: 15 -> 15, of which waited for: 5 -> 5; matrix products, arithmetic and copies ran while one was open for 1% -> 1% of each run, Pallas kernels for 51% -> 57%
where the time goes in v6:
time: 44.8 us; the launch traced here: 44.1 us
  Pallas kernels  27.1 us (60%)
  starting transfers between devices  12.8 us (29%)
  waiting for transfers between devices  2.33 us (5%)
  between operations  0.98 us (2%)
  local copies, waits for them, and re-layouts  0.66 us (1%)
    pallas_call x8, Pallas kernels, attend(): pl.pallas_call(functools.partial(attend_kernel, first, before, last, coun...  23.3 us
    ppermute x7, starting transfers between devices, shards(): a = forward = lax.ppermute(sent[i - 1], 'node', along)  11.9 us
    pallas_call x1, Pallas kernels, prepare(): pl.pallas_call(prepare_kernel, out_shape=(jax.ShapeDtypeStruct((parents +...  3.81 us
    ppermute x7, waiting for transfers between devices, shards(): a = forward = lax.ppermute(sent[i - 1], 'node', along)  2.31 us
  transfers between devices with their start and end apart: 15, of which 5 were waited for; matrix products, arithmetic and copies ran while one was open for 1% of the time, Pallas kernels for 57%

profile of v6, /device:TPU:0, one launch (start us, length us, event | category | flops | bytes accessed | tf_op | source)
XLA Modules:
  0.0 44.1 jit_solution(5162065618378960226)
XLA Ops:
  0.0 0.0 copy-start
  0.0 0.5 %collective-permute-start.1 = (bf16[576,384]{1,0:T(8,128)(2,1)}, bf16[576,384]{1,0:T(8,128)(2,1)S(1)}, u32[]{:S(2)}, u32[]{:S(2)}) collective-permute-start(bf16[576,384]{1,0:T(8,128)(2,1)} %bitcast.7), channel_id=1, source_target_pairs={{0,1},{1,0},{2,3},{3,2},{4,5},{5,4},{6,7},{7,6},{8,9},{9,8},{10,11... | collective-permute-start | bytes 1327112 | tf_op jit(solution)/shard_map/ppermute | solution.py:277
  0.5 2.6 %collective-permute-start = (bf16[576,384]{1,0:T(8,128)(2,1)}, bf16[576,384]{1,0:T(8,128)(2,1)S(1)}, u32[]{:S(2)}, u32[]{:S(2)}) collective-permute-start(bf16[576,384]{1,0:T(8,128)(2,1)} %bitcast.8), channel_id=1, source_target_pairs={{0,4},{4,8},{8,12},{12,14},{14,10},{10,6},{6,2},{2,0},{5,1},{9,5},... | collective-permute-start | bytes 1327112 | tf_op jit(solution)/shard_map/ppermute | solution.py:297
  3.7 0.0 collective-permute-done.1.refs_1_
  3.7 1.6 %collective-permute-start.4 = (bf16[576,384]{1,0:T(8,128)(2,1)S(1)}, bf16[576,384]{1,0:T(8,128)(2,1)S(1)}, u32[]{:S(2)}, u32[]{:S(2)}) collective-permute-start(bf16[576,384]{1,0:T(8,128)(2,1)S(1)} %collective-permute-done.1.refs_1_), channel_id=1, source_target_pairs={{0,4},{4,8},{8,12},{12,14},{14,10},{10,6},{6,2},{2,0},{5,1},{9,5},... | collective-permute-start | bytes 1327112 | tf_op jit(solution)/shard_map/ppermute | solution.py:297
  5.4 3.8 %shard_map.64 = (s32[119]{0:T(128)}, bf16[96,64,576]{2,1,0:T(8,128)(2,1)S(1)}, bf16[576,384]{1,0:T(8,128)(2,1)S(1)}) custom-call(s32[16]{0:T(128)} %place_in, s32[1,96]{1,0:T(1,128)} %bitcast.10, s32[1]{0:T(128)S(6)} %copy.21.live_in, bf16[96,64,576]{2,1,0:T(8,128)(2,1)} %query_in.1, bf16[576,384]{1,0:T(8,128)(2,1)} %bitcast.9), custom_call_target="tpu_custom_call" | custom-call | bytes 14155776 | tf_op jit(solution)/shard_map/pallas_call | solution.py:109
  9.2 0.3 collective-permute-done.refs_0_
  9.5 0.0 collective-permute-start.3
  9.5 2.1 %collective-permute-start.2 = (bf16[576,384]{1,0:T(8,128)(2,1)S(1)}, bf16[576,384]{1,0:T(8,128)(2,1)S(1)}, u32[]{:S(2)}, u32[]{:S(2)}) collective-permute-start(bf16[576,384]{1,0:T(8,128)(2,1)S(1)} %collective-permute-done.refs_0_), channel_id=1, source_target_pairs={{0,4},{4,8},{8,12},{12,14},{14,10},{10,6},{6,2},{2,0},{5,1},{9,5},... | collective-permute-start | bytes 1327112 | tf_op jit(solution)/shard_map/ppermute | solution.py:297
  11.6 0.0 copy-done
  11.6 0.2 fusion.own
  11.8 0.0 copy-start.2
  11.9 0.6 %copy-done.2 = s32[119]{0:T(128)S(1)} copy-done((s32[119]{0:T(128)S(1)}, s32[119]{0:T(128)}, u32[]{:S(2)}) %copy-start.2) | copy-done | bytes 500
  12.5 3.4 %shard_map.65 = (bf16[96,64,512]{2,1,0:T(8,128)(2,1)}, bf16[102,64,512]{2,1,0:T(8,128)(2,1)S(1)}) custom-call(s32[119]{0:T(128)S(1)} %copy-done.2, bf16[96,64,576]{2,1,0:T(8,128)(2,1)S(1)} %get-tuple-element.41.query, bf16[576,128]{1,0:T(8,128)(2,1)S(1)} %fusion.own, bf16[576,384]{1,0:T(8,128)(2,1)S(1)} %get-tuple-element.44.refs_0_, ...), custom_call_target="tpu_custom_call" | custom-call | flops 855638016 | bytes 1966080 | tf_op jit(solution)/shard_map/pallas_call | solution.py:238
  15.9 0.0 collective-permute-done.4.refs_0_
  15.9 0.1 collective-permute-start.8
  16.0 0.4 collective-permute-start.7
  16.3 0.0 collective-permute-done.3.refs_1_
  16.3 2.1 %shard_map.66 = (bf16[96,64,512]{2,1,0:T(8,128)(2,1)}, bf16[102,64,512]{2,1,0:T(8,128)(2,1)S(1)}) custom-call(s32[119]{0:T(128)S(1)} %copy-done.2, bf16[96,64,576]{2,1,0:T(8,128)(2,1)S(1)} %get-tuple-element.41.query, bf16[576,128]{1,0:T(8,128)(2,1)S(1)} %fusion.own, ...), custom_call_target="tpu_custom_call", output_to_operand_aliasing={{0}: (6, {})} | custom-call | flops 3422552064 | bytes 7864320 | tf_op jit(solution)/shard_map/pallas_call | solution.py:238
  18.5 0.5 %collective-permute-done.2.refs_0_ = bf16[576,384]{1,0:T(8,128)(2,1)S(1)} collective-permute-done((bf16[576,384]{1,0:T(8,128)(2,1)S(1)}, bf16[576,384]{1,0:T(8,128)(2,1)S(1)}, u32[]{:S(2)}, u32[]{:S(2)}) %collective-permute-start.2) | collective-permute-done | bytes 442400 | tf_op jit(solution)/shard_map/ppermute | solution.py:297
  19.0 0.2 collective-permute-start.6
  19.2 3.1 %collective-permute-start.5 = (bf16[576,384]{1,0:T(8,128)(2,1)S(1)}, bf16[576,384]{1,0:T(8,128)(2,1)S(1)}, u32[]{:S(2)}, u32[]{:S(2)}) collective-permute-start(bf16[576,384]{1,0:T(8,128)(2,1)S(1)} %collective-permute-done.2.refs_0_), channel_id=1, source_target_pairs={{0,4},{4,8},{8,12},{12,14},{14,10},{10,6},{6,2},{2,0},{5,1},{9,5},... | collective-permute-start | bytes 1327112 | tf_op jit(solution)/shard_map/ppermute | solution.py:297
  22.3 0.0 collective-permute-done.8.refs_1_
  22.3 3.0 %shard_map.67 = (bf16[96,64,512]{2,1,0:T(8,128)(2,1)}, bf16[102,64,512]{2,1,0:T(8,128)(2,1)S(1)}) custom-call(s32[119]{0:T(128)S(1)} %copy-done.2, bf16[96,64,576]{2,1,0:T(8,128)(2,1)S(1)} %get-tuple-element.41.query, bf16[576,128]{1,0:T(8,128)(2,1)S(1)} %fusion.own, ...), custom_call_target="tpu_custom_call", output_to_operand_aliasing={{0}: (6, {})} | custom-call | flops 3422552064 | bytes 7864320 | tf_op jit(solution)/shard_map/pallas_call | solution.py:238
  25.3 0.0 collective-permute-done.7.refs_0_
  25.3 0.1 collective-permute-start.12
  25.4 0.6 %collective-permute-start.11 = (bf16[576,384]{1,0:T(8,128)(2,1)S(1)}, bf16[576,384]{1,0:T(8,128)(2,1)S(1)}, u32[]{:S(2)}, u32[]{:S(2)}) collective-permute-start(bf16[576,384]{1,0:T(8,128)(2,1)S(1)} %collective-permute-done.7.refs_0_), channel_id=1, source_target_pairs={{0,4},{4,8},{8,12},{12,14},{14,10},{10,6},{6,2},{2,0},{5,1},{9,5},... | collective-permute-start | bytes 1327112 | tf_op jit(solution)/shard_map/ppermute | solution.py:297
  25.9 0.0 collective-permute-done.6.refs_1_
  25.9 3.0 %shard_map.68 = (bf16[96,64,512]{2,1,0:T(8,128)(2,1)}, bf16[102,64,512]{2,1,0:T(8,128)(2,1)S(1)}) custom-call(s32[119]{0:T(128)S(1)} %copy-done.2, bf16[96,64,576]{2,1,0:T(8,128)(2,1)S(1)} %get-tuple-element.41.query, bf16[576,128]{1,0:T(8,128)(2,1)S(1)} %fusion.own, ...), custom_call_target="tpu_custom_call", output_to_operand_aliasing={{0}: (6, {})} | custom-call | flops 3422552064 | bytes 7864320 | tf_op jit(solution)/shard_map/pallas_call | solution.py:238
  29.0 0.1 collective-permute-done.5.refs_0_
  29.1 0.0 collective-permute-start.10
  29.1 1.5 %collective-permute-start.9 = (bf16[576,384]{1,0:T(8,128)(2,1)S(1)}, bf16[576,384]{1,0:T(8,128)(2,1)S(1)}, u32[]{:S(2)}, u32[]{:S(2)}) collective-permute-start(bf16[576,384]{1,0:T(8,128)(2,1)S(1)} %collective-permute-done.5.refs_0_), channel_id=1, source_target_pairs={{0,4},{4,8},{8,12},{12,14},{14,10},{10,6},{6,2},{2,0},{5,1},{9,5},... | collective-permute-start | bytes 1327112 | tf_op jit(solution)/shard_map/ppermute | solution.py:297
  30.6 0.0 collective-permute-done.12.refs_1_
  30.6 3.1 %shard_map.69 = (bf16[96,64,512]{2,1,0:T(8,128)(2,1)}, bf16[102,64,512]{2,1,0:T(8,128)(2,1)S(1)}) custom-call(s32[119]{0:T(128)S(1)} %copy-done.2, bf16[96,64,576]{2,1,0:T(8,128)(2,1)S(1)} %get-tuple-element.41.query, bf16[576,128]{1,0:T(8,128)(2,1)S(1)} %fusion.own, ...), custom_call_target="tpu_custom_call", output_to_operand_aliasing={{0}: (6, {})} | custom-call | flops 3422552064 | bytes 7864320 | tf_op jit(solution)/shard_map/pallas_call | solution.py:238
  33.7 0.1 collective-permute-done.11.refs_2_
  33.8 0.0 collective-permute-start.14
  33.8 0.0 collective-permute-done.10.refs_1_
  33.8 3.4 %shard_map.70 = (bf16[96,64,512]{2,1,0:T(8,128)(2,1)}, bf16[102,64,512]{2,1,0:T(8,128)(2,1)S(1)}) custom-call(s32[119]{0:T(128)S(1)} %copy-done.2, bf16[96,64,576]{2,1,0:T(8,128)(2,1)S(1)} %get-tuple-element.41.query, bf16[576,128]{1,0:T(8,128)(2,1)S(1)} %fusion.own, ...), custom_call_target="tpu_custom_call", output_to_operand_aliasing={{0}: (7, {})} | custom-call | flops 5133828096 | bytes 11796480 | tf_op jit(solution)/shard_map/pallas_call | solution.py:238
  37.2 1.3 %collective-permute-done.9.refs_1_ = bf16[576,384]{1,0:T(8,128)(2,1)S(1)} collective-permute-done((bf16[576,384]{1,0:T(8,128)(2,1)S(1)}, bf16[576,384]{1,0:T(8,128)(2,1)S(1)}, u32[]{:S(2)}, u32[]{:S(2)}) %collective-permute-start.9) | collective-permute-done | bytes 442400 | tf_op jit(solution)/shard_map/ppermute | solution.py:297
  38.5 0.0 collective-permute-start.13
  38.5 0.0 collective-permute-done.14.refs_0_
  38.5 3.3 %shard_map.71 = (bf16[96,64,512]{2,1,0:T(8,128)(2,1)}, bf16[102,64,512]{2,1,0:T(8,128)(2,1)S(1)}) custom-call(s32[119]{0:T(128)S(1)} %copy-done.2, bf16[96,64,576]{2,1,0:T(8,128)(2,1)S(1)} %get-tuple-element.41.query, bf16[576,128]{1,0:T(8,128)(2,1)S(1)} %fusion.own, ...), custom_call_target="tpu_custom_call", output_to_operand_aliasing={{0}: (6, {})} | custom-call | flops 3422552064 | bytes 7864320 | tf_op jit(solution)/shard_map/pallas_call | solution.py:238
  41.8 0.0 collective-permute-done.13.refs_0_
  41.8 0.0 copy-start.1
  41.8 2.1 %shard_map.72 = bf16[96,64,512]{2,1,0:T(8,128)(2,1)} custom-call(s32[119]{0:T(128)S(1)} %copy-done.2, bf16[96,64,576]{2,1,0:T(8,128)(2,1)S(1)} %get-tuple-element.41.query, bf16[576,128]{1,0:T(8,128)(2,1)S(1)} %fusion.own, bf16[576,384]{1,0:T(8,128)(2,1)S(1)} %collective-permute-done.13.refs_0_, ...), custom_call_target="tpu_custom_call", output_to_operand_aliasing={{}: (5, {})} | custom-call | flops 1711276032 | bytes 3932160 | tf_op jit(solution)/shard_map/pallas_call | solution.py:238
  43.9 0.0 copy-done.1
Async XLA Ops:
  0.0 11.6 %copy-start = (bf16[96,576]{1,0:T(8,128)(2,1)S(1)}, bf16[96,576]{1,0:T(8,128)(2,1)}, u32[]{:S(2)}) copy-start(bf16[96,576]{1,0:T(8,128)(2,1)} %param.8) | copy-start | bytes 331780
  0.0 3.7 %collective-permute-start.1 = (bf16[576,384]{1,0:T(8,128)(2,1)}, bf16[576,384]{1,0:T(8,128)(2,1)S(1)}, u32[]{:S(2)}, u32[]{:S(2)}) collective-permute-start(bf16[576,384]{1,0:T(8,128)(2,1)} %bitcast.7), channel_id=1, source_target_pairs={{0,1},{1,0},{2,3},{3,2},{4,5},{5,4},{6,7},{7,6},{8,9},{9,8},{10,11... | collective-permute-start | bytes 1327112 | tf_op jit(solution)/shard_map/ppermute | solution.py:277
  0.5 9.1 %collective-permute-start = (bf16[576,384]{1,0:T(8,128)(2,1)}, bf16[576,384]{1,0:T(8,128)(2,1)S(1)}, u32[]{:S(2)}, u32[]{:S(2)}) collective-permute-start(bf16[576,384]{1,0:T(8,128)(2,1)} %bitcast.8), channel_id=1, source_target_pairs={{0,4},{4,8},{8,12},{12,14},{14,10},{10,6},{6,2},{2,0},{5,1},{9,5},... | collective-permute-start | bytes 1327112 | tf_op jit(solution)/shard_map/ppermute | solution.py:297
  3.7 12.1 %collective-permute-start.4 = (bf16[576,384]{1,0:T(8,128)(2,1)S(1)}, bf16[576,384]{1,0:T(8,128)(2,1)S(1)}, u32[]{:S(2)}, u32[]{:S(2)}) collective-permute-start(bf16[576,384]{1,0:T(8,128)(2,1)S(1)} %collective-permute-done.1.refs_1_), channel_id=1, source_target_pairs={{0,4},{4,8},{8,12},{12,14},{14,10},{10,6},{6,2},{2,0},{5,1},{9,5},... | collective-permute-start | bytes 1327112 | tf_op jit(solution)/shard_map/ppermute | solution.py:297
  9.5 6.8 %collective-permute-start.3 = (bf16[576,384]{1,0:T(8,128)(2,1)S(1)}, bf16[576,384]{1,0:T(8,128)(2,1)S(1)}, u32[]{:S(2)}, u32[]{:S(2)}) collective-permute-start(bf16[576,384]{1,0:T(8,128)(2,1)S(1)} %collective-permute-done.refs_0_), channel_id=1, source_target_pairs={{0,1},{1,0},{2,3},{3,2},{4,5},{5,4},{6,7},{7,6},{8,9},{9,8},{10,11... | collective-permute-start | bytes 1327112 | tf_op jit(solution)/shard_map/ppermute | solution.py:307
  9.5 9.5 %collective-permute-start.2 = (bf16[576,384]{1,0:T(8,128)(2,1)S(1)}, bf16[576,384]{1,0:T(8,128)(2,1)S(1)}, u32[]{:S(2)}, u32[]{:S(2)}) collective-permute-start(bf16[576,384]{1,0:T(8,128)(2,1)S(1)} %collective-permute-done.refs_0_), channel_id=1, source_target_pairs={{0,4},{4,8},{8,12},{12,14},{14,10},{10,6},{6,2},{2,0},{5,1},{9,5},... | collective-permute-start | bytes 1327112 | tf_op jit(solution)/shard_map/ppermute | solution.py:297
  11.8 0.7 %copy-start.2 = (s32[119]{0:T(128)S(1)}, s32[119]{0:T(128)}, u32[]{:S(2)}) copy-start(s32[119]{0:T(128)} %get-tuple-element.40.plan) | copy-start | bytes 1432
  15.9 6.4 %collective-permute-start.8 = (bf16[576,384]{1,0:T(8,128)(2,1)S(1)}, bf16[576,384]{1,0:T(8,128)(2,1)S(1)}, u32[]{:S(2)}, u32[]{:S(2)}) collective-permute-start(bf16[576,384]{1,0:T(8,128)(2,1)S(1)} %collective-permute-done.4.refs_0_), channel_id=1, source_target_pairs={{0,1},{1,0},{2,3},{3,2},{4,5},{5,4},{6,7},{7,6},{8,9},{9,8},{10,11... | collective-permute-start | bytes 1327112 | tf_op jit(solution)/shard_map/ppermute | solution.py:307
  16.0 9.3 %collective-permute-start.7 = (bf16[576,384]{1,0:T(8,128)(2,1)S(1)}, bf16[576,384]{1,0:T(8,128)(2,1)S(1)}, u32[]{:S(2)}, u32[]{:S(2)}) collective-permute-start(bf16[576,384]{1,0:T(8,128)(2,1)S(1)} %collective-permute-done.4.refs_0_), channel_id=1, source_target_pairs={{0,4},{4,8},{8,12},{12,14},{14,10},{10,6},{6,2},{2,0},{5,1},{9,5},... | collective-permute-start | bytes 1327112 | tf_op jit(solution)/shard_map/ppermute | solution.py:297
  19.0 6.9 %collective-permute-start.6 = (bf16[576,384]{1,0:T(8,128)(2,1)S(1)}, bf16[576,384]{1,0:T(8,128)(2,1)S(1)}, u32[]{:S(2)}, u32[]{:S(2)}) collective-permute-start(bf16[576,384]{1,0:T(8,128)(2,1)S(1)} %collective-permute-done.2.refs_0_), channel_id=1, source_target_pairs={{0,1},{1,0},{2,3},{3,2},{4,5},{5,4},{6,7},{7,6},{8,9},{9,8},{10,11... | collective-permute-start | bytes 1327112 | tf_op jit(solution)/shard_map/ppermute | solution.py:307
  19.2 9.8 %collective-permute-start.5 = (bf16[576,384]{1,0:T(8,128)(2,1)S(1)}, bf16[576,384]{1,0:T(8,128)(2,1)S(1)}, u32[]{:S(2)}, u32[]{:S(2)}) collective-permute-start(bf16[576,384]{1,0:T(8,128)(2,1)S(1)} %collective-permute-done.2.refs_0_), channel_id=1, source_target_pairs={{0,4},{4,8},{8,12},{12,14},{14,10},{10,6},{6,2},{2,0},{5,1},{9,5},... | collective-permute-start | bytes 1327112 | tf_op jit(solution)/shard_map/ppermute | solution.py:297
  25.3 5.3 %collective-permute-start.12 = (bf16[576,384]{1,0:T(8,128)(2,1)S(1)}, bf16[576,384]{1,0:T(8,128)(2,1)S(1)}, u32[]{:S(2)}, u32[]{:S(2)}) collective-permute-start(bf16[576,384]{1,0:T(8,128)(2,1)S(1)} %collective-permute-done.7.refs_0_), channel_id=1, source_target_pairs={{0,1},{1,0},{2,3},{3,2},{4,5},{5,4},{6,7},{7,6},{8,9},{9,8},{10,11... | collective-permute-start | bytes 1327112 | tf_op jit(solution)/shard_map/ppermute | solution.py:307
  25.4 8.4 %collective-permute-start.11 = (bf16[576,384]{1,0:T(8,128)(2,1)S(1)}, bf16[576,384]{1,0:T(8,128)(2,1)S(1)}, u32[]{:S(2)}, u32[]{:S(2)}) collective-permute-start(bf16[576,384]{1,0:T(8,128)(2,1)S(1)} %collective-permute-done.7.refs_0_), channel_id=1, source_target_pairs={{0,4},{4,8},{8,12},{12,14},{14,10},{10,6},{6,2},{2,0},{5,1},{9,5},... | collective-permute-start | bytes 1327112 | tf_op jit(solution)/shard_map/ppermute | solution.py:297
  29.1 4.7 %collective-permute-start.10 = (bf16[576,384]{1,0:T(8,128)(2,1)S(1)}, bf16[576,384]{1,0:T(8,128)(2,1)S(1)}, u32[]{:S(2)}, u32[]{:S(2)}) collective-permute-start(bf16[576,384]{1,0:T(8,128)(2,1)S(1)} %collective-permute-done.5.refs_0_), channel_id=1, source_target_pairs={{0,1},{1,0},{2,3},{3,2},{4,5},{5,4},{6,7},{7,6},{8,9},{9,8},{10,11... | collective-permute-start | bytes 1327112 | tf_op jit(solution)/shard_map/ppermute | solution.py:307
  29.1 9.4 %collective-permute-start.9 = (bf16[576,384]{1,0:T(8,128)(2,1)S(1)}, bf16[576,384]{1,0:T(8,128)(2,1)S(1)}, u32[]{:S(2)}, u32[]{:S(2)}) collective-permute-start(bf16[576,384]{1,0:T(8,128)(2,1)S(1)} %collective-permute-done.5.refs_0_), channel_id=1, source_target_pairs={{0,4},{4,8},{8,12},{12,14},{14,10},{10,6},{6,2},{2,0},{5,1},{9,5},... | collective-permute-start | bytes 1327112 | tf_op jit(solution)/shard_map/ppermute | solution.py:297
  33.8 4.7 %collective-permute-start.14 = (bf16[576,384]{1,0:T(8,128)(2,1)S(1)}, bf16[576,384]{1,0:T(8,128)(2,1)S(1)}, u32[]{:S(2)}, u32[]{:S(2)}) collective-permute-start(bf16[576,384]{1,0:T(8,128)(2,1)S(1)} %collective-permute-done.11.refs_2_), channel_id=1, source_target_pairs={{0,1},{1,0},{2,3},{3,2},{4,5},{5,4},{6,7},{7,6},{8,9},{9,8},{10,11... | collective-permute-start | bytes 1327112 | tf_op jit(solution)/shard_map/ppermute | solution.py:307
  38.5 3.3 %collective-permute-start.13 = (bf16[576,384]{1,0:T(8,128)(2,1)S(1)}, bf16[576,384]{1,0:T(8,128)(2,1)S(1)}, u32[]{:S(2)}, u32[]{:S(2)}) collective-permute-start(bf16[576,384]{1,0:T(8,128)(2,1)S(1)} %collective-permute-done.9.refs_1_), channel_id=1, source_target_pairs={{0,1},{1,0},{2,3},{3,2},{4,5},{5,4},{6,7},{7,6},{8,9},{9,8},{10,11... | collective-permute-start | bytes 1327112 | tf_op jit(solution)/shard_map/ppermute | solution.py:307
  41.8 2.1 %copy-start.1 = (bf16[96,576]{1,0:T(8,128)(2,1)S(1)}, bf16[96,576]{1,0:T(8,128)(2,1)}, u32[]{:S(2)}) copy-start(bf16[96,576]{1,0:T(8,128)(2,1)} %param.8) | copy-start | bytes 331780

commit v7 on v4

--- a/solution.py
+++ b/solution.py
@@ -201,9 +201,10 @@
         score(b, even)
         score(b + 1, odd)
         finish(b, even)
+        if last:
+            send(b)
         finish(b + 1, odd)
         if last:
-            send(b)
             send(b + 1)
 
     @pl.when(number % 2 == 1)

time: 44.7 us -> 44.4 us (level)
  Pallas kernels: 25.1 us -> 26.7 us
  starting transfers between devices: 13.7 us -> 12.6 us
  waiting for transfers between devices: 3.86 us -> 3.15 us
    pallas_call x8, Pallas kernels: 21.3 us -> 22.9 us  [attend(): pl.pallas_call(functools.partial(attend_kernel, first, before, last, coun...]
    ppermute x7, starting transfers between devices: 12.8 us -> 11.7 us  [shards(): a = forward = lax.ppermute(sent[i - 1], 'node', along)]
    ppermute x7, waiting for transfers between devices: 3.84 us -> 3.13 us  [shards(): a = forward = lax.ppermute(sent[i - 1], 'node', along)]
  transfers between devices with their start and end apart: 15 -> 15, of which waited for: 5 -> 4; matrix products, arithmetic and copies ran while one was open for 1% -> 1% of each run, Pallas kernels for 51% -> 55%
where the time goes in v7:
time: 44.4 us; the launch traced here: 44.3 us
  Pallas kernels  26.7 us (60%)
  starting transfers between devices  12.6 us (28%)
  waiting for transfers between devices  3.15 us (7%)
  between operations  0.97 us (2%)
  local copies, waits for them, and re-layouts  0.66 us (1%)
    pallas_call x8, Pallas kernels, attend(): pl.pallas_call(functools.partial(attend_kernel, first, before, last, coun...  22.9 us
    ppermute x7, starting transfers between devices, shards(): a = forward = lax.ppermute(sent[i - 1], 'node', along)  11.7 us
    pallas_call x1, Pallas kernels, prepare(): pl.pallas_call(prepare_kernel, out_shape=(jax.ShapeDtypeStruct((parents +...  3.81 us
    ppermute x7, waiting for transfers between devices, shards(): a = forward = lax.ppermute(sent[i - 1], 'node', along)  3.13 us
  transfers between devices with their start and end apart: 15, of which 4 were waited for; matrix products, arithmetic and copies ran while one was open for 1% of the time, Pallas kernels for 55%

profile of v7, /device:TPU:0, one launch (start us, length us, event | category | flops | bytes accessed | tf_op | source)
XLA Modules:
  0.0 44.3 jit_solution(5728204259894587956)
XLA Ops:
  0.0 0.0 copy-start
  0.0 0.5 %collective-permute-start.1 = (bf16[576,384]{1,0:T(8,128)(2,1)}, bf16[576,384]{1,0:T(8,128)(2,1)S(1)}, u32[]{:S(2)}, u32[]{:S(2)}) collective-permute-start(bf16[576,384]{1,0:T(8,128)(2,1)} %bitcast.7), channel_id=1, source_target_pairs={{0,1},{1,0},{2,3},{3,2},{4,5},{5,4},{6,7},{7,6},{8,9},{9,8},{10,11... | collective-permute-start | bytes 1327112 | tf_op jit(solution)/shard_map/ppermute | solution.py:276
  0.5 2.6 %collective-permute-start = (bf16[576,384]{1,0:T(8,128)(2,1)}, bf16[576,384]{1,0:T(8,128)(2,1)S(1)}, u32[]{:S(2)}, u32[]{:S(2)}) collective-permute-start(bf16[576,384]{1,0:T(8,128)(2,1)} %bitcast.8), channel_id=1, source_target_pairs={{0,4},{4,8},{8,12},{12,14},{14,10},{10,6},{6,2},{2,0},{5,1},{9,5},... | collective-permute-start | bytes 1327112 | tf_op jit(solution)/shard_map/ppermute | solution.py:296
  3.7 0.0 collective-permute-done.1.refs_1_
  3.7 1.6 %collective-permute-start.4 = (bf16[576,384]{1,0:T(8,128)(2,1)S(1)}, bf16[576,384]{1,0:T(8,128)(2,1)S(1)}, u32[]{:S(2)}, u32[]{:S(2)}) collective-permute-start(bf16[576,384]{1,0:T(8,128)(2,1)S(1)} %collective-permute-done.1.refs_1_), channel_id=1, source_target_pairs={{0,4},{4,8},{8,12},{12,14},{14,10},{10,6},{6,2},{2,0},{5,1},{9,5},... | collective-permute-start | bytes 1327112 | tf_op jit(solution)/shard_map/ppermute | solution.py:296
  5.4 3.8 %shard_map.64 = (s32[119]{0:T(128)}, bf16[96,64,576]{2,1,0:T(8,128)(2,1)S(1)}, bf16[576,384]{1,0:T(8,128)(2,1)S(1)}) custom-call(s32[16]{0:T(128)} %place_in, s32[1,96]{1,0:T(1,128)} %bitcast.10, s32[1]{0:T(128)S(6)} %copy.21.live_in, bf16[96,64,576]{2,1,0:T(8,128)(2,1)} %query_in.1, bf16[576,384]{1,0:T(8,128)(2,1)} %bitcast.9), custom_call_target="tpu_custom_call" | custom-call | bytes 14155776 | tf_op jit(solution)/shard_map/pallas_call | solution.py:109
  9.2 0.3 collective-permute-done.refs_0_
  9.5 0.0 collective-permute-start.3
  9.5 2.1 %collective-permute-start.2 = (bf16[576,384]{1,0:T(8,128)(2,1)S(1)}, bf16[576,384]{1,0:T(8,128)(2,1)S(1)}, u32[]{:S(2)}, u32[]{:S(2)}) collective-permute-start(bf16[576,384]{1,0:T(8,128)(2,1)S(1)} %collective-permute-done.refs_0_), channel_id=1, source_target_pairs={{0,4},{4,8},{8,12},{12,14},{14,10},{10,6},{6,2},{2,0},{5,1},{9,5},... | collective-permute-start | bytes 1327112 | tf_op jit(solution)/shard_map/ppermute | solution.py:296
  11.6 0.0 copy-done
  11.6 0.2 fusion.own
  11.8 0.0 copy-start.2
  11.9 0.6 %copy-done.2 = s32[119]{0:T(128)S(1)} copy-done((s32[119]{0:T(128)S(1)}, s32[119]{0:T(128)}, u32[]{:S(2)}) %copy-start.2) | copy-done | bytes 500
  12.5 3.0 %shard_map.65 = (bf16[96,64,512]{2,1,0:T(8,128)(2,1)}, bf16[102,64,512]{2,1,0:T(8,128)(2,1)S(1)}) custom-call(s32[119]{0:T(128)S(1)} %copy-done.2, bf16[96,64,576]{2,1,0:T(8,128)(2,1)S(1)} %get-tuple-element.41.query, bf16[576,128]{1,0:T(8,128)(2,1)S(1)} %fusion.own, bf16[576,384]{1,0:T(8,128)(2,1)S(1)} %get-tuple-element.44.refs_0_, ...), custom_call_target="tpu_custom_call" | custom-call | flops 855638016 | bytes 1966080 | tf_op jit(solution)/shard_map/pallas_call | solution.py:237
  15.5 0.0 collective-permute-done.4.refs_0_
  15.5 0.2 collective-permute-start.8
  15.7 1.9 %collective-permute-start.7 = (bf16[576,384]{1,0:T(8,128)(2,1)S(1)}, bf16[576,384]{1,0:T(8,128)(2,1)S(1)}, u32[]{:S(2)}, u32[]{:S(2)}) collective-permute-start(bf16[576,384]{1,0:T(8,128)(2,1)S(1)} %collective-permute-done.4.refs_0_), channel_id=1, source_target_pairs={{0,4},{4,8},{8,12},{12,14},{14,10},{10,6},{6,2},{2,0},{5,1},{9,5},... | collective-permute-start | bytes 1327112 | tf_op jit(solution)/shard_map/ppermute | solution.py:296
  17.5 0.0 collective-permute-done.3.refs_1_
  17.5 3.1 %shard_map.66 = (bf16[96,64,512]{2,1,0:T(8,128)(2,1)}, bf16[102,64,512]{2,1,0:T(8,128)(2,1)S(1)}) custom-call(s32[119]{0:T(128)S(1)} %copy-done.2, bf16[96,64,576]{2,1,0:T(8,128)(2,1)S(1)} %get-tuple-element.41.query, bf16[576,128]{1,0:T(8,128)(2,1)S(1)} %fusion.own, ...), custom_call_target="tpu_custom_call", output_to_operand_aliasing={{0}: (6, {})} | custom-call | flops 3422552064 | bytes 7864320 | tf_op jit(solution)/shard_map/pallas_call | solution.py:237
  20.6 0.0 collective-permute-done.2.refs_0_
  20.6 0.1 collective-permute-start.6
  20.7 0.5 %collective-permute-start.5 = (bf16[576,384]{1,0:T(8,128)(2,1)S(1)}, bf16[576,384]{1,0:T(8,128)(2,1)S(1)}, u32[]{:S(2)}, u32[]{:S(2)}) collective-permute-start(bf16[576,384]{1,0:T(8,128)(2,1)S(1)} %collective-permute-done.2.refs_0_), channel_id=1, source_target_pairs={{0,4},{4,8},{8,12},{12,14},{14,10},{10,6},{6,2},{2,0},{5,1},{9,5},... | collective-permute-start | bytes 1327112 | tf_op jit(solution)/shard_map/ppermute | solution.py:296
  21.2 0.0 collective-permute-done.8.refs_1_
  21.2 3.0 %shard_map.67 = (bf16[96,64,512]{2,1,0:T(8,128)(2,1)}, bf16[102,64,512]{2,1,0:T(8,128)(2,1)S(1)}) custom-call(s32[119]{0:T(128)S(1)} %copy-done.2, bf16[96,64,576]{2,1,0:T(8,128)(2,1)S(1)} %get-tuple-element.41.query, bf16[576,128]{1,0:T(8,128)(2,1)S(1)} %fusion.own, ...), custom_call_target="tpu_custom_call", output_to_operand_aliasing={{0}: (6, {})} | custom-call | flops 3422552064 | bytes 7864320 | tf_op jit(solution)/shard_map/pallas_call | solution.py:237
  24.2 0.0 collective-permute-done.7.refs_0_
  24.2 0.1 collective-permute-start.12
  24.4 1.5 %collective-permute-start.11 = (bf16[576,384]{1,0:T(8,128)(2,1)S(1)}, bf16[576,384]{1,0:T(8,128)(2,1)S(1)}, u32[]{:S(2)}, u32[]{:S(2)}) collective-permute-start(bf16[576,384]{1,0:T(8,128)(2,1)S(1)} %collective-permute-done.7.refs_0_), channel_id=1, source_target_pairs={{0,4},{4,8},{8,12},{12,14},{14,10},{10,6},{6,2},{2,0},{5,1},{9,5},... | collective-permute-start | bytes 1327112 | tf_op jit(solution)/shard_map/ppermute | solution.py:296
  25.8 0.0 collective-permute-done.6.refs_1_
  25.8 2.2 %shard_map.68 = (bf16[96,64,512]{2,1,0:T(8,128)(2,1)}, bf16[102,64,512]{2,1,0:T(8,128)(2,1)S(1)}) custom-call(s32[119]{0:T(128)S(1)} %copy-done.2, bf16[96,64,576]{2,1,0:T(8,128)(2,1)S(1)} %get-tuple-element.41.query, bf16[576,128]{1,0:T(8,128)(2,1)S(1)} %fusion.own, ...), custom_call_target="tpu_custom_call", output_to_operand_aliasing={{0}: (6, {})} | custom-call | flops 3422552064 | bytes 7864320 | tf_op jit(solution)/shard_map/pallas_call | solution.py:237
  28.0 1.0 %collective-permute-done.5.refs_0_ = bf16[576,384]{1,0:T(8,128)(2,1)S(1)} collective-permute-done((bf16[576,384]{1,0:T(8,128)(2,1)S(1)}, bf16[576,384]{1,0:T(8,128)(2,1)S(1)}, u32[]{:S(2)}, u32[]{:S(2)}) %collective-permute-start.5) | collective-permute-done | bytes 442400 | tf_op jit(solution)/shard_map/ppermute | solution.py:296
  29.1 0.0 collective-permute-start.10
  29.1 1.5 %collective-permute-start.9 = (bf16[576,384]{1,0:T(8,128)(2,1)S(1)}, bf16[576,384]{1,0:T(8,128)(2,1)S(1)}, u32[]{:S(2)}, u32[]{:S(2)}) collective-permute-start(bf16[576,384]{1,0:T(8,128)(2,1)S(1)} %collective-permute-done.5.refs_0_), channel_id=1, source_target_pairs={{0,4},{4,8},{8,12},{12,14},{14,10},{10,6},{6,2},{2,0},{5,1},{9,5},... | collective-permute-start | bytes 1327112 | tf_op jit(solution)/shard_map/ppermute | solution.py:296
  30.6 0.0 collective-permute-done.12.refs_1_
  30.6 3.0 %shard_map.69 = (bf16[96,64,512]{2,1,0:T(8,128)(2,1)}, bf16[102,64,512]{2,1,0:T(8,128)(2,1)S(1)}) custom-call(s32[119]{0:T(128)S(1)} %copy-done.2, bf16[96,64,576]{2,1,0:T(8,128)(2,1)S(1)} %get-tuple-element.41.query, bf16[576,128]{1,0:T(8,128)(2,1)S(1)} %fusion.own, ...), custom_call_target="tpu_custom_call", output_to_operand_aliasing={{0}: (6, {})} | custom-call | flops 3422552064 | bytes 7864320 | tf_op jit(solution)/shard_map/pallas_call | solution.py:237
  33.6 0.2 collective-permute-done.11.refs_2_
  33.8 0.1 collective-permute-start.14
  33.8 0.0 collective-permute-done.10.refs_1_
  33.8 3.1 %shard_map.70 = (bf16[96,64,512]{2,1,0:T(8,128)(2,1)}, bf16[102,64,512]{2,1,0:T(8,128)(2,1)S(1)}) custom-call(s32[119]{0:T(128)S(1)} %copy-done.2, bf16[96,64,576]{2,1,0:T(8,128)(2,1)S(1)} %get-tuple-element.41.query, bf16[576,128]{1,0:T(8,128)(2,1)S(1)} %fusion.own, ...), custom_call_target="tpu_custom_call", output_to_operand_aliasing={{0}: (7, {})} | custom-call | flops 5133828096 | bytes 11796480 | tf_op jit(solution)/shard_map/pallas_call | solution.py:237
  37.0 1.5 %collective-permute-done.9.refs_1_ = bf16[576,384]{1,0:T(8,128)(2,1)S(1)} collective-permute-done((bf16[576,384]{1,0:T(8,128)(2,1)S(1)}, bf16[576,384]{1,0:T(8,128)(2,1)S(1)}, u32[]{:S(2)}, u32[]{:S(2)}) %collective-permute-start.9) | collective-permute-done | bytes 442400 | tf_op jit(solution)/shard_map/ppermute | solution.py:296
  38.5 0.0 collective-permute-start.13
  38.5 0.0 collective-permute-done.14.refs_0_
  38.5 3.2 %shard_map.71 = (bf16[96,64,512]{2,1,0:T(8,128)(2,1)}, bf16[102,64,512]{2,1,0:T(8,128)(2,1)S(1)}) custom-call(s32[119]{0:T(128)S(1)} %copy-done.2, bf16[96,64,576]{2,1,0:T(8,128)(2,1)S(1)} %get-tuple-element.41.query, bf16[576,128]{1,0:T(8,128)(2,1)S(1)} %fusion.own, ...), custom_call_target="tpu_custom_call", output_to_operand_aliasing={{0}: (6, {})} | custom-call | flops 3422552064 | bytes 7864320 | tf_op jit(solution)/shard_map/pallas_call | solution.py:237
  41.8 0.0 collective-permute-done.13.refs_0_
  41.8 0.0 copy-start.1
  41.8 2.3 %shard_map.72 = bf16[96,64,512]{2,1,0:T(8,128)(2,1)} custom-call(s32[119]{0:T(128)S(1)} %copy-done.2, bf16[96,64,576]{2,1,0:T(8,128)(2,1)S(1)} %get-tuple-element.41.query, bf16[576,128]{1,0:T(8,128)(2,1)S(1)} %fusion.own, bf16[576,384]{1,0:T(8,128)(2,1)S(1)} %collective-permute-done.13.refs_0_, ...), custom_call_target="tpu_custom_call", output_to_operand_aliasing={{}: (5, {})} | custom-call | flops 1711276032 | bytes 3932160 | tf_op jit(solution)/shard_map/pallas_call | solution.py:237
  44.1 0.0 copy-done.1
Async XLA Ops:
  0.0 11.6 %copy-start = (bf16[96,576]{1,0:T(8,128)(2,1)S(1)}, bf16[96,576]{1,0:T(8,128)(2,1)}, u32[]{:S(2)}) copy-start(bf16[96,576]{1,0:T(8,128)(2,1)} %param.8) | copy-start | bytes 331780
  0.0 3.7 %collective-permute-start.1 = (bf16[576,384]{1,0:T(8,128)(2,1)}, bf16[576,384]{1,0:T(8,128)(2,1)S(1)}, u32[]{:S(2)}, u32[]{:S(2)}) collective-permute-start(bf16[576,384]{1,0:T(8,128)(2,1)} %bitcast.7), channel_id=1, source_target_pairs={{0,1},{1,0},{2,3},{3,2},{4,5},{5,4},{6,7},{7,6},{8,9},{9,8},{10,11... | collective-permute-start | bytes 1327112 | tf_op jit(solution)/shard_map/ppermute | solution.py:276
  0.5 9.1 %collective-permute-start = (bf16[576,384]{1,0:T(8,128)(2,1)}, bf16[576,384]{1,0:T(8,128)(2,1)S(1)}, u32[]{:S(2)}, u32[]{:S(2)}) collective-permute-start(bf16[576,384]{1,0:T(8,128)(2,1)} %bitcast.8), channel_id=1, source_target_pairs={{0,4},{4,8},{8,12},{12,14},{14,10},{10,6},{6,2},{2,0},{5,1},{9,5},... | collective-permute-start | bytes 1327112 | tf_op jit(solution)/shard_map/ppermute | solution.py:296
  3.7 11.7 %collective-permute-start.4 = (bf16[576,384]{1,0:T(8,128)(2,1)S(1)}, bf16[576,384]{1,0:T(8,128)(2,1)S(1)}, u32[]{:S(2)}, u32[]{:S(2)}) collective-permute-start(bf16[576,384]{1,0:T(8,128)(2,1)S(1)} %collective-permute-done.1.refs_1_), channel_id=1, source_target_pairs={{0,4},{4,8},{8,12},{12,14},{14,10},{10,6},{6,2},{2,0},{5,1},{9,5},... | collective-permute-start | bytes 1327112 | tf_op jit(solution)/shard_map/ppermute | solution.py:296
  9.5 8.0 %collective-permute-start.3 = (bf16[576,384]{1,0:T(8,128)(2,1)S(1)}, bf16[576,384]{1,0:T(8,128)(2,1)S(1)}, u32[]{:S(2)}, u32[]{:S(2)}) collective-permute-start(bf16[576,384]{1,0:T(8,128)(2,1)S(1)} %collective-permute-done.refs_0_), channel_id=1, source_target_pairs={{0,1},{1,0},{2,3},{3,2},{4,5},{5,4},{6,7},{7,6},{8,9},{9,8},{10,11... | collective-permute-start | bytes 1327112 | tf_op jit(solution)/shard_map/ppermute | solution.py:306
  9.5 11.1 %collective-permute-start.2 = (bf16[576,384]{1,0:T(8,128)(2,1)S(1)}, bf16[576,384]{1,0:T(8,128)(2,1)S(1)}, u32[]{:S(2)}, u32[]{:S(2)}) collective-permute-start(bf16[576,384]{1,0:T(8,128)(2,1)S(1)} %collective-permute-done.refs_0_), channel_id=1, source_target_pairs={{0,4},{4,8},{8,12},{12,14},{14,10},{10,6},{6,2},{2,0},{5,1},{9,5},... | collective-permute-start | bytes 1327112 | tf_op jit(solution)/shard_map/ppermute | solution.py:296
  11.8 0.7 %copy-start.2 = (s32[119]{0:T(128)S(1)}, s32[119]{0:T(128)}, u32[]{:S(2)}) copy-start(s32[119]{0:T(128)} %get-tuple-element.40.plan) | copy-start | bytes 1432
  15.5 5.7 %collective-permute-start.8 = (bf16[576,384]{1,0:T(8,128)(2,1)S(1)}, bf16[576,384]{1,0:T(8,128)(2,1)S(1)}, u32[]{:S(2)}, u32[]{:S(2)}) collective-permute-start(bf16[576,384]{1,0:T(8,128)(2,1)S(1)} %collective-permute-done.4.refs_0_), channel_id=1, source_target_pairs={{0,1},{1,0},{2,3},{3,2},{4,5},{5,4},{6,7},{7,6},{8,9},{9,8},{10,11... | collective-permute-start | bytes 1327112 | tf_op jit(solution)/shard_map/ppermute | solution.py:306
  15.7 8.6 %collective-permute-start.7 = (bf16[576,384]{1,0:T(8,128)(2,1)S(1)}, bf16[576,384]{1,0:T(8,128)(2,1)S(1)}, u32[]{:S(2)}, u32[]{:S(2)}) collective-permute-start(bf16[576,384]{1,0:T(8,128)(2,1)S(1)} %collective-permute-done.4.refs_0_), channel_id=1, source_target_pairs={{0,4},{4,8},{8,12},{12,14},{14,10},{10,6},{6,2},{2,0},{5,1},{9,5},... | collective-permute-start | bytes 1327112 | tf_op jit(solution)/shard_map/ppermute | solution.py:296
  20.6 5.2 %collective-permute-start.6 = (bf16[576,384]{1,0:T(8,128)(2,1)S(1)}, bf16[576,384]{1,0:T(8,128)(2,1)S(1)}, u32[]{:S(2)}, u32[]{:S(2)}) collective-permute-start(bf16[576,384]{1,0:T(8,128)(2,1)S(1)} %collective-permute-done.2.refs_0_), channel_id=1, source_target_pairs={{0,1},{1,0},{2,3},{3,2},{4,5},{5,4},{6,7},{7,6},{8,9},{9,8},{10,11... | collective-permute-start | bytes 1327112 | tf_op jit(solution)/shard_map/ppermute | solution.py:306
  20.7 8.4 %collective-permute-start.5 = (bf16[576,384]{1,0:T(8,128)(2,1)S(1)}, bf16[576,384]{1,0:T(8,128)(2,1)S(1)}, u32[]{:S(2)}, u32[]{:S(2)}) collective-permute-start(bf16[576,384]{1,0:T(8,128)(2,1)S(1)} %collective-permute-done.2.refs_0_), channel_id=1, source_target_pairs={{0,4},{4,8},{8,12},{12,14},{14,10},{10,6},{6,2},{2,0},{5,1},{9,5},... | collective-permute-start | bytes 1327112 | tf_op jit(solution)/shard_map/ppermute | solution.py:296
  24.2 6.3 %collective-permute-start.12 = (bf16[576,384]{1,0:T(8,128)(2,1)S(1)}, bf16[576,384]{1,0:T(8,128)(2,1)S(1)}, u32[]{:S(2)}, u32[]{:S(2)}) collective-permute-start(bf16[576,384]{1,0:T(8,128)(2,1)S(1)} %collective-permute-done.7.refs_0_), channel_id=1, source_target_pairs={{0,1},{1,0},{2,3},{3,2},{4,5},{5,4},{6,7},{7,6},{8,9},{9,8},{10,11... | collective-permute-start | bytes 1327112 | tf_op jit(solution)/shard_map/ppermute | solution.py:306
  24.4 9.4 %collective-permute-start.11 = (bf16[576,384]{1,0:T(8,128)(2,1)S(1)}, bf16[576,384]{1,0:T(8,128)(2,1)S(1)}, u32[]{:S(2)}, u32[]{:S(2)}) collective-permute-start(bf16[576,384]{1,0:T(8,128)(2,1)S(1)} %collective-permute-done.7.refs_0_), channel_id=1, source_target_pairs={{0,4},{4,8},{8,12},{12,14},{14,10},{10,6},{6,2},{2,0},{5,1},{9,5},... | collective-permute-start | bytes 1327112 | tf_op jit(solution)/shard_map/ppermute | solution.py:296
  29.1 4.8 %collective-permute-start.10 = (bf16[576,384]{1,0:T(8,128)(2,1)S(1)}, bf16[576,384]{1,0:T(8,128)(2,1)S(1)}, u32[]{:S(2)}, u32[]{:S(2)}) collective-permute-start(bf16[576,384]{1,0:T(8,128)(2,1)S(1)} %collective-permute-done.5.refs_0_), channel_id=1, source_target_pairs={{0,1},{1,0},{2,3},{3,2},{4,5},{5,4},{6,7},{7,6},{8,9},{9,8},{10,11... | collective-permute-start | bytes 1327112 | tf_op jit(solution)/shard_map/ppermute | solution.py:306
  29.1 9.5 %collective-permute-start.9 = (bf16[576,384]{1,0:T(8,128)(2,1)S(1)}, bf16[576,384]{1,0:T(8,128)(2,1)S(1)}, u32[]{:S(2)}, u32[]{:S(2)}) collective-permute-start(bf16[576,384]{1,0:T(8,128)(2,1)S(1)} %collective-permute-done.5.refs_0_), channel_id=1, source_target_pairs={{0,4},{4,8},{8,12},{12,14},{14,10},{10,6},{6,2},{2,0},{5,1},{9,5},... | collective-permute-start | bytes 1327112 | tf_op jit(solution)/shard_map/ppermute | solution.py:296
  33.8 4.7 %collective-permute-start.14 = (bf16[576,384]{1,0:T(8,128)(2,1)S(1)}, bf16[576,384]{1,0:T(8,128)(2,1)S(1)}, u32[]{:S(2)}, u32[]{:S(2)}) collective-permute-start(bf16[576,384]{1,0:T(8,128)(2,1)S(1)} %collective-permute-done.11.refs_2_), channel_id=1, source_target_pairs={{0,1},{1,0},{2,3},{3,2},{4,5},{5,4},{6,7},{7,6},{8,9},{9,8},{10,11... | collective-permute-start | bytes 1327112 | tf_op jit(solution)/shard_map/ppermute | solution.py:306
  38.5 3.2 %collective-permute-start.13 = (bf16[576,384]{1,0:T(8,128)(2,1)S(1)}, bf16[576,384]{1,0:T(8,128)(2,1)S(1)}, u32[]{:S(2)}, u32[]{:S(2)}) collective-permute-start(bf16[576,384]{1,0:T(8,128)(2,1)S(1)} %collective-permute-done.9.refs_1_), channel_id=1, source_target_pairs={{0,1},{1,0},{2,3},{3,2},{4,5},{5,4},{6,7},{7,6},{8,9},{9,8},{10,11... | collective-permute-start | bytes 1327112 | tf_op jit(solution)/shard_map/ppermute | solution.py:306
  41.8 2.4 %copy-start.1 = (bf16[96,576]{1,0:T(8,128)(2,1)S(1)}, bf16[96,576]{1,0:T(8,128)(2,1)}, u32[]{:S(2)}) copy-start(bf16[96,576]{1,0:T(8,128)(2,1)} %param.8) | copy-start | bytes 331780
